TPU v7x, 32 devices: a whole 2x2x4 slice. The times are simulated.
32 devices in a mesh: gx: 4 (over y, core), gy: 8 (over z, x).
Axes of the slice: x: 2, y: 2, z: 4, core: 2. Of those that a mesh axis runs over, the one named last changes fastest.
Arguments:
- source_mass: float32 [4, 1024, 1024], P(None, 'gx', 'gy'), may hold values from 0.1 to 2
- target_density: float32 [4, 1024, 1024], P(None, 'gx', 'gy'), may hold values from 0.25 to 4
- potential: float32 [4, 1024, 1024], P(None, 'gx', 'gy'), may hold values from -6 to 6
- dest_device: int32 [4, 8, 128, 4], P('gx', 'gy'), may hold values from 0 to 31, all different within a row; in each aligned block of 128 rows (0 to 127, 128 to 255, ..., all dimensions but the last counted through in order) at most 24 rows name the same one
- dest_tile: int32 [4, 8, 128, 4], P('gx', 'gy'), may hold values from 0 to 127
- mass_counts: int32 [4, 8, 128, 4], P('gx', 'gy'), may hold values from 1 to 8
- reach: float32 [4], replicated, may hold values from 2 to 8192
Outputs:
- pushed: float32 [4, 1024, 1024], P(None, 'gx', 'gy')
- potential_next: float32 [4, 1024, 1024], P(None, 'gx', 'gy')
Inputs may be any that keep to these rules, and one draw needn't show every extreme that they name: `dest_device`: within one block's 128 x 4 entries no destination block is named more than 24 times, and in some blocks one is named exactly 24 times; the 4 entries of one source tile name different blocks.
All inputs are finite; a program needn't handle non-finite values.
Results may differ from a plain program's by a relative error of at most 0.0001.
Values sent between devices are 32-bit elements; how exact they have to be, the bound alone decides.
No kernel may reach another device: no remote copies, remote signals or barrier semaphores. Data moves between devices by JAX's collectives and lax.ppermute only.
A program may use at most 64 MiB of HBM per device.

v0:
```python
import jax
import jax.numpy as jnp
from jax import lax
from jax.sharding import PartitionSpec as P

TS = 16


def entering_2(array, axis, combine, identity, reverse):
    devices, position = (lax.axis_size(axis), lax.axis_index(axis))
    everything = jax.tree.map(lambda part: lax.all_gather(part, axis), array)
    start = jax.tree.map(
        lambda part, zero: jnp.broadcast_to(jnp.asarray(zero, part.dtype), part.shape),
        array,
        identity,
    )

    def step(k, before):
        at = devices - 1 - k if reverse else k
        reached = at > position if reverse else at < position
        new = combine(before, jax.tree.map(lambda part: part[at], everything))
        return jax.tree.map(lambda a, b: jnp.where(reached, a, b), new, before)

    return lax.fori_loop(0, devices, step, start)


def line_tables(reach, length):
    decay = 1.0 - 1.0 / reach
    logs = jnp.log(decay)[:, None, None]
    rows = lax.broadcasted_iota(jnp.float32, (1, length, length), 1)
    cols = lax.broadcasted_iota(jnp.float32, (1, length, length), 2)
    spacing = rows - cols
    lower = jnp.where(spacing >= 0.0, jnp.exp(jnp.maximum(spacing, 0.0) * logs), 0.0)
    place = lax.broadcasted_iota(jnp.float32, (1, length), 1)
    rise = jnp.exp((place + 1.0) * logs[:, :, 0])
    fall = jnp.exp((length - place) * logs[:, :, 0])
    across = jnp.exp(length * logs[:, :, 0])
    scale = ((1.0 - decay) ** 2)[:, None, None]
    return (lower, rise, fall, across, scale)


def compose(former, latter):
    return (former[0] * latter[0], latter[0] * former[1] + latter[1])


def ahead_x(lower, field):
    return jnp.einsum("zij,zjy->ziy", lower, field, precision=lax.Precision.HIGHEST)


def finish_x(local, tables):
    lower, rise, fall, across, scale = tables
    start = (jnp.ones_like(across), jnp.zeros_like(local[:, -1, :]))
    entering = entering_2((across, local[:, -1, :]), "gx", compose, start, False)[1]
    running = local + rise[:, :, None] * entering[:, None, :]
    base = scale * jnp.einsum("zji,zjy->ziy", lower, running, precision=lax.Precision.HIGHEST)
    leaving = entering_2((across, base[:, 0, :]), "gx", compose, start, True)[1]
    return base + fall[:, :, None] * leaving[:, None, :]


def sweep_y(field, tables):
    lower, rise, fall, across, scale = tables
    local = jnp.einsum("zij,zxj->zxi", lower, field, precision=lax.Precision.HIGHEST)
    start = (jnp.ones_like(across), jnp.zeros_like(local[:, :, -1]))
    entering = entering_2((across, local[:, :, -1]), "gy", compose, start, False)[1]
    running = local + rise[:, None, :] * entering[:, :, None]
    base = scale * jnp.einsum("zji,zxj->zxi", lower, running, precision=lax.Precision.HIGHEST)
    leaving = entering_2((across, base[:, :, 0]), "gy", compose, start, True)[1]
    return base + fall[:, None, :] * leaving[:, :, None]


def per_device(source_mass, target_density, potential, dest_device, dest_tile, mass_counts, reach):
    planes, cells_x, cells_y = source_mass.shape
    tile_count = dest_device.shape[2]
    fanout = dest_device.shape[3]
    tiles_x = cells_x // TS
    tiles_y = cells_y // TS
    tile_cells = planes * TS * TS
    grid_x = lax.axis_size("gx")
    grid_y = lax.axis_size("gy")
    device_count = grid_x * grid_y
    capacity = max(2, 3 * fanout * tile_count // (2 * device_count))
    entries = tile_count * fanout
    tables_x = line_tables(reach, cells_x)
    tables_y = line_tables(reach, cells_y)
    target_ahead = ahead_x(tables_x[0], target_density)
    tiles = (
        source_mass.reshape(planes, tiles_x, TS, tiles_y, TS)
        .transpose(1, 3, 0, 2, 4)
        .reshape(tile_count, tile_cells)
    )
    counts = mass_counts.reshape(tile_count, fanout).astype(jnp.float32)
    shares = (counts / jnp.sum(counts, axis=1, keepdims=True)).reshape(entries)
    targets = dest_device.reshape(entries)
    target_tiles = dest_tile.reshape(entries)
    matches = (targets[:, None] == jnp.arange(device_count, dtype=jnp.int32)[None, :]).astype(
        jnp.int32
    )
    earlier_count = jnp.cumsum(matches, axis=0) - matches
    ranking = jnp.sum(earlier_count * matches, axis=1)
    slot_of = targets * capacity + ranking
    owner = (
        jnp.full((device_count * capacity,), entries, jnp.int32)
        .at[slot_of]
        .set(jnp.arange(entries, dtype=jnp.int32))
    )
    filled = owner < entries
    owner_safe = jnp.minimum(owner, entries - 1)
    weights = jnp.where(filled, shares[owner_safe], 0.0)
    outgoing = tiles[owner_safe // fanout] * weights[:, None]
    labels = jnp.where(filled, target_tiles[owner_safe], tile_count)
    arrived, arrived_labels = (
        lax.all_to_all(
            outgoing.reshape(device_count, capacity, tile_cells),
            ("gx", "gy"),
            split_axis=0,
            concat_axis=0,
            tiled=True,
        ),
        lax.all_to_all(
            labels.reshape(device_count, capacity),
            ("gx", "gy"),
            split_axis=0,
            concat_axis=0,
            tiled=True,
        ),
    )
    arrived = arrived.reshape(device_count * capacity, tile_cells)
    arrived_labels = arrived_labels.reshape(device_count * capacity)
    collect = (jnp.arange(tile_count, dtype=jnp.int32)[:, None] == arrived_labels[None, :]).astype(
        jnp.float32
    )
    pushed_tiles = jnp.dot(collect, arrived, precision=lax.Precision.HIGHEST)
    pushed = (
        pushed_tiles.reshape(tiles_x, tiles_y, planes, TS, TS)
        .transpose(2, 0, 3, 1, 4)
        .reshape(planes, cells_x, cells_y)
    )
    local = target_ahead - ahead_x(tables_x[0], pushed)
    smoothed_x = finish_x(local, tables_x)
    correction = sweep_y(smoothed_x, tables_y)
    return (pushed, potential + correction)


def solution(mesh):
    in_specs = (
        P(None, "gx", "gy"),
        P(None, "gx", "gy"),
        P(None, "gx", "gy"),
        P("gx", "gy", None, None),
        P("gx", "gy", None, None),
        P("gx", "gy", None, None),
        P(),
    )
    out_specs = (P(None, "gx", "gy"), P(None, "gx", "gy"))
    return jax.shard_map(
        per_device, mesh=mesh, in_specs=in_specs, out_specs=out_specs, check_vma=False
    )
```

profile of v0, /device:TPU:0, one launch (start us, length us, event | category | flops | bytes accessed | tf_op | source)
XLA Modules:
  0.0 231.8 jit_solution(6503121196957103940)
XLA Ops:
  0.7 0.8 broadcast_multiply_fusion.1
  1.4 0.8 copy.39
  2.4 0.8 copy.42
  3.6 1.2 reduce-window.6
  5.1 2.4 %scatter_custom_fusion = s32[768]{0:T(1024)S(1)} fusion(s32[512]{0:T(512)S(1)} %bitcast.113, s32[512]{0:T(512)S(1)} %iota.78, s32[]{:T(128)} %constant.172.clone.1), kind=kCustom, calls=%fused_computation.98 | custom fusion | bytes 3076 | tf_op jit(solution)/shard_map/scatter | solution.py:104
  7.6 5.0 %gather_fusion = s32[768]{0:T(1024)S(1)} fusion(s32[512]{0:T(512)S(1)} %reshape.271, s32[1024]{0:T(1024)S(1)} %pad_clamp_fusion.1), kind=kCustom, calls=%fused_computation | custom fusion | bytes 9216 | tf_op jit(solution)/shard_map/gather | solution.py:110
  13.3 7.3 %all-to-all-start = ((s32[32,1,24]{2,1,0:T(1,128)}), s32[32,1,24]{2,1,0:T(1,128)S(1)}, u32[]{:S(2)}, u32[]{:S(2)}) async-start(s32[32,1,24]{2,1,0:T(1,128)} %bitcast.3), calls=%async_computation | async-start | bytes 32768 | tf_op jit(solution)/shard_map/all_to_all | solution.py:119
  20.7 2.5 %reshape.272 = f32[4,16,16,8,16]{4,3,2,1,0:T(8,128)} reshape(f32[4,256,128]{2,1,0:T(8,128)S(1)} %copy-done.2) | data formatting | bytes 1048576 | tf_op jit(solution)/shard_map/reshape | solution.py:87
  23.2 4.9 %copy.69 = f32[4,16,16,8,16]{4,2,0,3,1:T(8,128)} copy(f32[4,16,16,8,16]{4,3,2,1,0:T(8,128)} %reshape.272) | data formatting | bytes 1048576 | tf_op jit(solution)/shard_map/reshape | solution.py:87
  28.1 4.7 %reshape.273 = f32[128,1024]{1,0:T(8,128)S(1)} reshape(f32[16,8,4,16,16]{4,3,2,1,0:T(8,128)} %bitcast.105) | data formatting | bytes 1048576 | tf_op jit(solution)/shard_map/reshape | solution.py:89
  33.3 5.0 %gather_fusion.2 = f32[768]{0:T(1024)S(1)} fusion(f32[512]{0:T(512)S(1)} %div.33, s32[1024]{0:T(1024)S(1)} %pad_clamp_fusion.1), kind=kCustom, calls=%fused_computation.2 | custom fusion | bytes 9216 | tf_op jit(solution)/shard_map/gather | solution.py:108
  38.4 3.6 %gather_fusion.1 = f32[768,1024]{1,0:T(8,128)} fusion(f32[128,1024]{1,0:T(8,128)S(1)} %reshape.273, s32[1024]{0:T(1024)S(1)} %pad_clamp_fusion), kind=kCustom, calls=%fused_computation.1 | custom fusion | bytes 6294528 | tf_op jit(solution)/shard_map/gather | solution.py:109
  42.0 3.9 %broadcast_multiply_fusion = f32[32,24,1024]{2,1,0:T(8,128)} fusion(f32[32,24,1024]{2,1,0:T(8,128)} %bitcast.106, f32[32,24]{1,0:T(8,128)S(1)} %mul.312), kind=kLoop, calls=%fused_computation.18 | loop fusion | flops 786432 | bytes 6294528 | tf_op jit(solution)/shard_map/mul | solution.py:109
  45.9 6.0 %all-to-all-start.1 = ((f32[32,24,1024]{2,1,0:T(8,128)}), f32[32,24,1024]{2,1,0:T(8,128)}, u32[]{:S(2)}, u32[]{:S(2)}) async-start(f32[32,24,1024]{2,1,0:T(8,128)} %broadcast_multiply_fusion), calls=%async_computation.1 | async-start | bytes 6291456 | tf_op jit(solution)/shard_map/all_to_all | solution.py:112
  54.6 17.5 %all-reduce = f32[16]{0:T(128)S(1)} all-reduce(f32[16]{0:T(128)S(1)} %get-tuple-element.640), channel_id=2, replica_groups=mesh['gx'=4,'gy'=8] {'gx'}, use_global_device_ids=true, to_apply=%add | all-reduce | flops 16 | bytes 128
  72.2 47.6 %all-reduce.1 = f32[32]{0:T(128)S(1)} all-reduce(f32[32]{0:T(128)S(1)} %get-tuple-element.630), channel_id=5, replica_groups=mesh['gx'=4,'gy'=8] {'gy'}, use_global_device_ids=true, to_apply=%add.1 | all-reduce | flops 32 | bytes 256
  120.3 2.0 fusion.4
  123.6 1.2 all-to-all-done.1
  124.9 3.6 %copy.46 = f32[1024,768]{1,0:T(8,128)} copy(f32[1024,768]{0,1:T(8,128)} %bitcast.9) | data formatting | bytes 6291456 | tf_op jit(solution)/shard_map/dot_general | solution.py:132
  128.4 7.6 %convolution_bitcast_fusion = f32[4,16,16,8,16]{4,3,2,0,1:T(8,128)S(1)} fusion(f32[4,16,16,768,1]{3,2,1,0,4:T(8,128)} %bitcast.108, s32[768]{0:T(1024)S(1)} %eq.63, s32[16,8]{1,0:T(8,128)S(1)} %multiply_add_fusion), kind=kOutput, calls=%fused_computation.17 | convolution fusion | flops 1208057856 | bytes 3673600 | tf_op jit(solution)/shard_map/dot_general | solution.py:132
  136.1 2.2 copy.47
  138.3 3.2 %reshape.275 = f32[4,256,128]{2,1,0:T(8,128)S(1)} reshape(f32[4,16,16,8,16]{4,3,2,1,0:T(8,128)} %copy.47) | data formatting | bytes 1048576 | tf_op jit(solution)/shard_map/reshape | solution.py:136
  141.5 2.0 convolution_subtract_fusion
  143.6 5.5 %all-gather.1 = f32[16,1,128]{2,1,0:T(1,128)S(1)} all-gather(f32[4,1,128]{2,1,0:T(1,128)S(1)} %slice.31), channel_id=3, replica_groups=mesh['gx'=4,'gy'=8] {'gx'}, dimensions={0}, use_global_device_ids=true | all-gather | bytes 10240 | tf_op jit(solution)/shard_map/all_gather | solution.py:11
  149.4 1.3 convolution_multiply_fusion
  150.8 5.2 %all-gather.2 = f32[16,1,128]{2,1,0:T(1,128)S(1)} all-gather(f32[4,1,128]{2,1,0:T(1,128)S(1)} %slice.32), channel_id=4, replica_groups=mesh['gx'=4,'gy'=8] {'gx'}, dimensions={0}, use_global_device_ids=true | all-gather | bytes 10240 | tf_op jit(solution)/shard_map/all_gather | solution.py:11
  156.3 0.8 fusion.7
  157.1 40.3 %all-gather.4 = f32[32,256,1]{1,2,0:T(1,128)S(1)} all-gather(f32[4,256,1]{1,2,0:T(1,128)S(1)} %slice.33), channel_id=6, replica_groups=mesh['gx'=4,'gy'=8] {'gy'}, dimensions={0}, use_global_device_ids=true | all-gather | bytes 36864 | tf_op jit(solution)/shard_map/all_gather | solution.py:11
  198.2 1.1 convolution_multiply_fusion.1
  199.6 30.4 %all-gather.5 = f32[32,256,1]{1,2,0:T(1,128)S(1)} all-gather(f32[4,256,1]{1,2,0:T(1,128)S(1)} %copy.56), channel_id=7, replica_groups=mesh['gx'=4,'gy'=8] {'gy'}, dimensions={0}, use_global_device_ids=true | all-gather | bytes 36864 | tf_op jit(solution)/shard_map/all_gather | solution.py:11
  230.1 0.7 while.63
  230.8 1.0 add_add_fusion
  (126 shorter events, 9.2 us)
Async XLA Ops:
  0.6 119.7 %copy-start = (f32[4,256,128]{2,1,0:T(8,128)S(1)}, f32[4,256,128]{2,1,0:T(8,128)}, u32[]{:S(2)}) copy-start(f32[4,256,128]{2,1,0:T(8,128)} %param.16) | copy-start | bytes 1572868
  0.6 20.0 %copy-start.4 = (s32[1,1,128,4]{2,3,1,0:T(4,128)S(1)}, s32[1,1,128,4]{2,3,1,0:T(4,128)}, u32[]{:S(2)}) copy-start(s32[1,1,128,4]{2,3,1,0:T(4,128)} %param.20) | copy-start | bytes 6148
  0.7 20.0 %copy-start.2 = (f32[4,256,128]{2,1,0:T(8,128)S(1)}, f32[4,256,128]{2,1,0:T(8,128)}, u32[]{:S(2)}) copy-start(f32[4,256,128]{2,1,0:T(8,128)} %param.15) | copy-start | bytes 1572868
  13.3 32.6 %all-to-all-start = ((s32[32,1,24]{2,1,0:T(1,128)}), s32[32,1,24]{2,1,0:T(1,128)S(1)}, u32[]{:S(2)}, u32[]{:S(2)}) async-start(s32[32,1,24]{2,1,0:T(1,128)} %bitcast.3), calls=%async_computation | async-start | bytes 32768 | tf_op jit(solution)/shard_map/all_to_all | solution.py:119
  45.9 6.0 %copy-start.7 = (u32[32]{0:T(128)S(1)}, u32[32]{0:T(128)}, u32[]{:S(2)}) copy-start(u32[32]{0:T(128)} %constant.198) | copy-start | bytes 388
  45.9 6.6 %copy-start.6 = (u32[32]{0:T(128)S(1)}, u32[32]{0:T(128)}, u32[]{:S(2)}) copy-start(u32[32]{0:T(128)} %constant.193) | copy-start | bytes 388
  45.9 8.5 %copy-start.5 = (f32[4]{0:T(128)S(1)}, f32[4]{0:T(128)}, u32[]{:S(2)}) copy-start(f32[4]{0:T(128)} %param.21) | copy-start | bytes 52
  45.9 79.0 %all-to-all-start.1 = ((f32[32,24,1024]{2,1,0:T(8,128)}), f32[32,24,1024]{2,1,0:T(8,128)}, u32[]{:S(2)}, u32[]{:S(2)}) async-start(f32[32,24,1024]{2,1,0:T(8,128)} %broadcast_multiply_fusion), calls=%async_computation.1 | async-start | bytes 6291456 | tf_op jit(solution)/shard_map/all_to_all | solution.py:112
  141.5 57.9 %copy-start.1 = (f32[4,256,128]{2,1,0:T(8,128)}, f32[4,256,128]{2,1,0:T(8,128)S(1)}, u32[]{:S(2)}) copy-start(f32[4,256,128]{2,1,0:T(8,128)S(1)} %reshape.275) | copy-start | bytes 1572868
  143.5 87.3 %copy-start.3 = (f32[4,256,128]{2,1,0:T(8,128)S(1)}, f32[4,256,128]{2,1,0:T(8,128)}, u32[]{:S(2)}) copy-start(f32[4,256,128]{2,1,0:T(8,128)} %param.17) | copy-start | bytes 1572868
where the time goes:
time: 232 us
  blocking collectives  147 us (63%)
  local copies, waits for them, and re-layouts  43 us (19%)
  matrix products  14.9 us (6%)
  starting transfers between devices  13.2 us (6%)
  other arithmetic  10.4 us (4%)
  between operations  2.37 us (1%)
    all_gather x4, blocking collectives, entering_2(): everything = jax.tree.map(lambda part: lax.all_gather(part, axis), array)  81.4 us
    unnamed x2, blocking collectives  65.1 us
    dot_general x1, matrix products, per_device(): pushed_tiles = jnp.dot(collect, arrived, precision=lax.Precision.HIGHEST)  7.64 us
    reshape x2, local copies, waits for them, and re-layouts, per_device(): source_mass.reshape(planes, tiles_x, TS, tiles_y, TS)  7.43 us
    all_to_all x1, starting transfers between devices, per_device(): lax.all_to_all(labels.reshape(device_count, capacity), ('gx', 'gy'), spli...  7.3 us
    all_to_all x1, starting transfers between devices, per_device(): lax.all_to_all(outgoing.reshape(device_count, capacity, tile_cells), ('gx...  5.95 us
    gather x1, local copies, waits for them, and re-layouts, per_device(): weights = jnp.where(filled, shares[owner_safe], 0.0)  5.01 us
    gather x1, local copies, waits for them, and re-layouts, per_device(): labels = jnp.where(filled, target_tiles[owner_safe], tile_count)  5.01 us
  transfers between devices with their start and end apart: 2, of which 1 were waited for; matrix products, arithmetic and copies ran while one was open for 13% of the time, Pallas kernels for 0%

commit v1 on v0

v1 whole, which is shorter than its diff:
```python
import functools

import jax
import jax.numpy as jnp
from jax import lax
from jax.experimental import pallas as pl
from jax.experimental.pallas import tpu as pltpu
from jax.sharding import Mesh
from jax.sharding import PartitionSpec as P

TS = 16
SUB = 8
LANES = 128
F32 = jnp.float32
BF16 = jnp.bfloat16
VMEM_LIMIT = 48 * 1024 * 1024


def split(x):
    high = x.astype(BF16)
    return high, (x - high.astype(F32)).astype(BF16)


def mm(a, b):
    return jnp.dot(a, b, preferred_element_type=F32)


def mm_t(a, b):
    return lax.dot_general(a, b, (((0,), (0,)), ((), ())), preferred_element_type=F32)


def dot3(a, b):
    a_high, a_low = split(a)
    b_high, b_low = split(b)
    return mm(a_high, b_high) + mm(a_high, b_low) + mm(a_low, b_high)


def swap_blocks(x):
    rows = x.shape[0]
    x = x.reshape(rows // SUB, SUB, LANES)
    sub = lax.broadcasted_iota(jnp.int32, x.shape, 1)
    block = lax.broadcasted_iota(jnp.int32, x.shape, 2) // TS
    for k in (4, 2, 1):
        up = pltpu.roll(pltpu.roll(x, SUB - k, 1), TS * k, 2)
        down = up if 2 * k == SUB else pltpu.roll(pltpu.roll(x, k, 1), LANES - TS * k, 2)
        moved = jnp.where((sub & k) == 0, up, down)
        x = jnp.where((sub & k) == (block & k), x, moved)
    return x.reshape(rows, LANES)


def tile_columns(tiled, planes, tiles_x):
    grouped = tiled.reshape(planes, tiles_x, 2, SUB, LANES)
    columns = [grouped[z, :, h].reshape(tiles_x * SUB, LANES) for z in range(planes) for h in range(2)]
    return jnp.concatenate(columns, axis=1)


def tile_rows(columns, planes, tiles_x):
    parts = [
        columns[:, i * LANES:(i + 1) * LANES].reshape(1, tiles_x, 1, SUB, LANES) for i in range(2 * planes)
    ]
    planes_of = [jnp.concatenate(parts[2 * z:2 * z + 2], axis=2) for z in range(planes)]
    return jnp.concatenate(planes_of, axis=0).reshape(planes * tiles_x * TS, LANES)


def route_rows(names, tiles, shares, wanted):
    fanout, count = names.shape
    member = jnp.zeros(wanted.shape, F32)
    weight = jnp.zeros(wanted.shape, F32)
    label = jnp.zeros(wanted.shape, F32)
    for k in range(fanout):
        hit = names[k:k + 1, :] == wanted
        member = member + jnp.where(hit, 1.0, 0.0)
        weight = weight + jnp.where(hit, shares[k:k + 1, :], 0.0)
        label = label + jnp.where(hit, tiles[k:k + 1, :], 0.0)
    before = lax.broadcasted_iota(jnp.int32, (count, count), 0) < lax.broadcasted_iota(
        jnp.int32, (count, count), 1
    )
    rank = mm(member.astype(BF16), jnp.where(before, 1.0, 0.0).astype(BF16))
    return jnp.where(member > 0.0, rank, 2.0 * count), weight, label


def slots_of(rank, weight, label, capacity):
    slot = lax.broadcasted_iota(jnp.int32, (capacity, rank.shape[1]), 0).astype(F32)
    chosen = rank == slot
    picked = jnp.where(chosen, weight, 0.0)
    labels = jnp.sum(jnp.where(chosen, label, 0.0), axis=1, keepdims=True)
    return picked, labels


def place_labels(board, labels, first):
    lane = lax.broadcasted_iota(jnp.int32, board.shape, 1)
    for g in range(labels.shape[0] // SUB):
        board = jnp.where(lane == first + g, labels[g * SUB:(g + 1) * SUB], board)
    return board


def read_labels(board, first, capacity):
    lane = lax.broadcasted_iota(jnp.int32, (SUB, LANES), 1).astype(F32)
    rows = [
        jnp.where(board[:, first + g:first + g + 1] == lane, 1.0, 0.0) for g in range(capacity // SUB)
    ]
    return jnp.concatenate(rows, axis=0)


def start_kernel(capacity, columns, depth, planes_a, source, names_in, tiles_in, counts_in, wanted, ring_out,
                 pack_out, picked):
    planes, cells_x, _ = source.shape
    tiles_x = cells_x // TS
    tile_count, fanout = names_in.shape
    names = names_in[...].astype(F32).T
    tiles = tiles_in[...].astype(F32).T
    counts = counts_in[...].astype(F32).T
    shares = counts / jnp.sum(counts, axis=0, keepdims=True)
    half = planes_a * cells_x
    ring_out[:half, :] = swap_blocks(source[:planes_a].reshape(half, LANES))
    ring_out[half:, :] = jnp.zeros((ring_out.shape[0] - half, LANES), F32)
    ring_out[half:half + fanout, :] = names
    ring_out[half + SUB:half + SUB + fanout, :] = tiles
    ring_out[half + 2 * SUB:half + 2 * SUB + fanout, :] = shares
    rank, weight, label = route_rows(names, tiles, shares, wanted[...])
    for j in range(columns):
        board = jnp.zeros((SUB, LANES), F32)
        for r in range(depth):
            n = j * depth + r
            rows, labels = slots_of(rank[n:n + 1], weight[n:n + 1], label[n:n + 1], capacity)
            picked[n * capacity:(n + 1) * capacity, :] = rows
            board = place_labels(board, labels, r * (capacity // SUB))
        pack_out[j, depth * capacity:, :] = jnp.zeros((SUB, pack_out.shape[2]), F32)
        pack_out[j, depth * capacity:, :LANES] = board
    rest = planes - planes_a
    cells = swap_blocks(source[planes_a:].reshape(rest * cells_x, LANES))
    packed = dot3(picked[...], tile_columns(cells, rest, tiles_x))
    pack_out[:, :depth * capacity, :] = packed.reshape(columns, depth * capacity, packed.shape[1])


def forward_kernel(capacity, columns, depth, planes_a, fanout, wanted, *refs):
    rings, pack_out, picked = refs[:depth], refs[depth], refs[depth + 1]
    half = rings[0].shape[0] - 3 * SUB
    tiles_x = half // planes_a // TS
    boards = [jnp.zeros((SUB, LANES), F32) for _ in range(columns)]
    for s in range(depth):
        ring = rings[s]
        names = ring[half:half + fanout, :]
        tiles = ring[half + SUB:half + SUB + fanout, :]
        shares = ring[half + 2 * SUB:half + 2 * SUB + fanout, :]
        rank, weight, label = route_rows(names, tiles, shares, wanted[...])
        for j in range(columns):
            rows, labels = slots_of(rank[j:j + 1], weight[j:j + 1], label[j:j + 1], capacity)
            picked[j * capacity:(j + 1) * capacity, :] = rows
            boards[j] = place_labels(boards[j], labels, s * (capacity // SUB))
        packed = dot3(picked[...], tile_columns(ring[:half, :], planes_a, tiles_x))
        pack_out[:, s * capacity:(s + 1) * capacity, :] = packed.reshape(columns, capacity, packed.shape[1])
    for j in range(columns):
        pack_out[j, depth * capacity:, :] = jnp.zeros((SUB, pack_out.shape[2]), F32)
        pack_out[j, depth * capacity:, :LANES] = boards[j]


def gather_sum(arrived, capacity, groups):
    columns, rows, _ = arrived.shape
    total = rows - SUB
    heads, cells = [], []
    for j in range(columns):
        board = arrived[j, total:, :LANES]
        for g in groups:
            heads.append(read_labels(board, g * (capacity // SUB), capacity))
            cells.append(arrived[j, g * capacity:(g + 1) * capacity, :])
    head = jnp.concatenate(heads, axis=0).astype(BF16)
    high, low = split(jnp.concatenate(cells, axis=0))
    return mm_t(head, high) + mm_t(head, low)


def partial_kernel(capacity, depth, arrived, *outs):
    for r in range(depth):
        outs[r][...] = gather_sum(arrived, capacity, [r])


def pushed_kernel(capacity, depth, planes_a, arrived, ring_sum, own_sum, pushed_out):
    planes, cells_x, _ = pushed_out.shape
    tiles_x = cells_x // TS
    first = gather_sum(arrived, capacity, list(range(depth)))
    rows = swap_blocks(tile_rows(first, planes_a, tiles_x))
    pushed_out[:planes_a] = rows.reshape(planes_a, cells_x, LANES)
    rest = planes - planes_a
    rows = swap_blocks(tile_rows(ring_sum[...] + own_sum[...], rest, tiles_x))
    pushed_out[planes_a:] = rows.reshape(rest, cells_x, LANES)


def call(body, out_shape, scratch=()):
    return pl.pallas_call(
        body,
        out_shape=out_shape,
        scratch_shapes=list(scratch),
        compiler_params=pltpu.CompilerParams(vmem_limit_bytes=VMEM_LIMIT),
    )


def line_tables(reach, length):
    decay = 1.0 - 1.0 / reach
    logs = jnp.log(decay)[:, None, None]
    rows = lax.broadcasted_iota(F32, (1, length, length), 1)
    cols = lax.broadcasted_iota(F32, (1, length, length), 2)
    spacing = rows - cols
    lower = jnp.where(spacing >= 0.0, jnp.exp(jnp.maximum(spacing, 0.0) * logs), 0.0)
    place = lax.broadcasted_iota(F32, (1, length), 1)
    rise = jnp.exp((place + 1.0) * logs[:, :, 0])
    fall = jnp.exp((length - place) * logs[:, :, 0])
    across = jnp.exp(length * logs[:, :, 0])
    scale = ((1.0 - decay) ** 2)[:, None, None]
    both = scale * jnp.einsum("zki,zkj->zij", lower, lower, precision=lax.Precision.HIGHEST)
    bend = scale[:, :, 0] * jnp.einsum("zki,zk->zi", lower, rise, precision=lax.Precision.HIGHEST)
    return lower[:, -1, :], both, bend, fall, across


def entering(ends, across, position, count, reverse):
    total = jnp.zeros_like(ends[0])
    for k in range(count):
        at = count - 1 - k if reverse else k
        reached = at > position if reverse else at < position
        total = jnp.where(reached, across * total + ends[at], total)
    return total


def neighbours(across, ends, starts, gain, position, count):
    forward = entering(ends, across, position, count, False)
    running = jnp.zeros_like(ends[0])
    full = []
    for k in range(count):
        full.append(starts[k] + gain * running)
        running = across * running + ends[k]
    return forward, entering(jnp.stack(full), across, position, count, True)


def per_device(source_mass, target_density, potential, dest_device, dest_tile, mass_counts, reach):
    planes, cells_x, cells_y = source_mass.shape
    tile_count, fanout = dest_device.shape[2:]
    grid_x, depth, inner = lax.axis_size("gx"), lax.axis_size("z"), lax.axis_size("x")
    columns = grid_x * inner
    device_count = columns * depth
    capacity = max(2, 3 * fanout * tile_count // (2 * device_count))
    capacity = -(-capacity // SUB) * SUB
    rows = depth * capacity + SUB
    planes_a = planes // 2
    tile_cells = 2 * LANES
    at_gx, at_z, at_x = lax.axis_index("gx"), lax.axis_index("z"), lax.axis_index("x")

    column = jnp.arange(columns, dtype=jnp.int32)
    level = (at_z - jnp.arange(depth, dtype=jnp.int32)) % depth
    block = (column // inner)[:, None] * (depth * inner) + level[None, :] * inner + (column % inner)[:, None]
    wanted_b = jnp.broadcast_to(block.reshape(-1, 1).astype(F32), (columns * depth, LANES))
    wanted_a = jnp.broadcast_to(block[:, :1].astype(F32), (columns, LANES))

    ring, packed_b = call(
        functools.partial(start_kernel, capacity, columns, depth, planes_a),
        (
            jax.ShapeDtypeStruct((planes_a * cells_x + 3 * SUB, LANES), F32),
            jax.ShapeDtypeStruct((columns, rows, (planes - planes_a) * tile_cells), F32),
        ),
        [pltpu.VMEM((columns * depth * capacity, tile_count), F32)],
    )(
        source_mass,
        dest_device.reshape(tile_count, fanout),
        dest_tile.reshape(tile_count, fanout),
        mass_counts.reshape(tile_count, fanout),
        wanted_b,
    )
    onward = [(i, (i + 1) % depth) for i in range(depth)]
    rings = [ring]
    for _ in range(depth - 1):
        rings.append(lax.ppermute(rings[-1], "z", onward))
    arrived_b = lax.all_to_all(packed_b, ("gx", "x"), 0, 0, tiled=True)
    packed_a = call(
        functools.partial(forward_kernel, capacity, columns, depth, planes_a, fanout),
        jax.ShapeDtypeStruct((columns, rows, planes_a * tile_cells), F32),
        [pltpu.VMEM((columns * capacity, tile_count), F32)],
    )(wanted_a, *rings)
    arrived_a = lax.all_to_all(packed_a, ("gx", "x"), 0, 0, tiled=True)
    sums = call(
        functools.partial(partial_kernel, capacity, depth),
        tuple(
            jax.ShapeDtypeStruct((tile_count, (planes - planes_a) * tile_cells), F32) for _ in range(depth)
        ),
    )(arrived_b)
    moving = sums[1 % depth]
    for r in range(2, depth + 1):
        moving = lax.ppermute(moving, "z", onward)
        if r < depth:
            moving = moving + sums[r]
    if depth == 1:
        moving = jnp.zeros_like(sums[0])
    pushed = call(
        functools.partial(pushed_kernel, capacity, depth, planes_a),
        jax.ShapeDtypeStruct(source_mass.shape, F32),
    )(arrived_a, moving, sums[0])

    last_x, both_x, bend_x, fall_x, across_x = line_tables(reach, cells_x)
    last_y, both_y, bend_y, fall_y, across_y = line_tables(reach, cells_y)
    high = lax.Precision.HIGHEST
    mismatch = target_density - pushed
    ends = jnp.einsum("zx,zxy->zy", last_x, mismatch, precision=high)
    base = jnp.einsum("zij,zjy->ziy", both_x, mismatch, precision=high)
    packed = jnp.stack([ends, base[:, 0, :]])
    packed = lax.all_gather(packed, "gx")
    forward, backward = neighbours(across_x, packed[:, 0], packed[:, 1], bend_x[:, :1], at_gx, grid_x)
    smoothed = base + bend_x[:, :, None] * forward[:, None, :] + fall_x[:, :, None] * backward[:, None, :]
    ends = jnp.einsum("zy,zxy->zx", last_y, smoothed, precision=high)
    base = jnp.einsum("zij,zxj->zxi", both_y, smoothed, precision=high)
    packed = jnp.stack([ends, base[:, :, 0]])
    everyone = depth * inner
    packed = lax.all_to_all(jnp.broadcast_to(packed[None], (everyone,) + packed.shape), ("z", "x"), 0, 0, tiled=True)
    forward, backward = neighbours(
        across_y, packed[:, 0], packed[:, 1], bend_y[:, :1], at_z * inner + at_x, everyone
    )
    correction = base + forward[:, :, None] * bend_y[:, None, :] + backward[:, :, None] * fall_y[:, None, :]
    return pushed, potential + correction


def solution(mesh):
    grid_x, grid_y = mesh.shape["gx"], mesh.shape["gy"]
    inner = grid_x // 2
    if inner < 1 or grid_y % inner:
        inner = 1
    split_mesh = Mesh(mesh.devices.reshape(grid_x, grid_y // inner, inner), ("gx", "z", "x"))
    field = P(None, "gx", ("z", "x"))
    table = P("gx", ("z", "x"), None, None)
    return jax.shard_map(
        per_device,
        mesh=split_mesh,
        in_specs=(field, field, field, table, table, table, P()),
        out_specs=(field, field),
        check_vma=False,
    )
```

time: 232 us -> 106 us (0.46)
  blocking collectives: 147 us -> 5.19 us
  waiting for transfers between devices: 1.25 us -> 42.9 us
  local copies, waits for them, and re-layouts: 43 us -> 14.2 us
  Pallas kernels: 0 us -> 8.25 us
  matrix products: 14.9 us -> 10.5 us
    all_gather x4 -> x1, blocking collectives: 81.4 us -> 5.19 us  [per_device(): packed = lax.all_gather(packed, 'gx')]
    unnamed x2 -> x0, blocking collectives: 65.1 us -> none
    ppermute x0 -> x6, waiting for transfers between devices: none -> 36.7 us  [the longest x3 18.8 us: per_device(): moving = lax.ppermute(moving, 'z', onward)]
    reshape x5 -> x0, local copies, waits for them, and re-layouts: 15.5 us -> none  [the longest x2 7.43 us: per_device(): source_mass.reshape(planes, tiles_x, TS, tiles_y, TS)]
    gather x3 -> x0, local copies, waits for them, and re-layouts: 13.7 us -> none  [the longest x1 5.01 us: per_device(): weights = jnp.where(filled, shares[owner_safe], 0.0)]
    pallas_call x0 -> x4, Pallas kernels: none -> 8.25 us  [the longest x1 2.48 us: per_device(): call(functools.partial(forward_kernel, capacity, columns, depth, planes_a...]
    unnamed x22 -> x57, local copies, waits for them, and re-layouts: 2.79 us -> 8.62 us
    all_to_all x2 -> x3, waiting for transfers between devices: 1.25 us -> 6.17 us  [the longest x1 6.16 us: per_device(): lax.all_to_all(jnp.broadcast_to(packed[None], (everyone,) + packed.shape)...]
  transfers between devices with their start and end apart: 2 -> 9, of which waited for: 1 -> 7; matrix products, arithmetic and copies ran while one was open for 13% -> 20% of each run, Pallas kernels for 0% -> 4%
where the time goes in v1:
time: 106 us; the launch traced here: 105 us
  waiting for transfers between devices  42.9 us (40%)
  starting transfers between devices  14.7 us (14%)
  local copies, waits for them, and re-layouts  14.2 us (13%)
  matrix products  10.5 us (10%)
  other arithmetic  8.37 us (8%)
  Pallas kernels  8.25 us (8%)
  blocking collectives  5.19 us (5%)
    ppermute x3, waiting for transfers between devices, per_device(): moving = lax.ppermute(moving, 'z', onward)  18.8 us
    ppermute x3, waiting for transfers between devices, per_device(): rings.append(lax.ppermute(rings[-1], 'z', onward))  17.9 us
    unnamed x57, local copies, waits for them, and re-layouts  8.62 us
    all_to_all x1, waiting for transfers between devices, per_device(): lax.all_to_all(jnp.broadcast_to(packed[None], (everyone,) + packed.shape)...  6.16 us
    all_gather x1, blocking collectives, per_device(): packed = lax.all_gather(packed, 'gx')  5.19 us
    dot_general x2, matrix products, line_tables(): jnp.einsum('zki,zkj->zij', lower, lower, precision=lax.Precision.HIGHEST)  4.28 us
    all_to_all x1, starting transfers between devices, per_device(): arrived_a = lax.all_to_all(packed_a, ('gx', 'x'), 0, 0, tiled=True)  3.97 us
    all_to_all x1, starting transfers between devices, per_device(): arrived_b = lax.all_to_all(packed_b, ('gx', 'x'), 0, 0, tiled=True)  3.86 us
  transfers between devices with their start and end apart: 9, of which 7 were waited for; matrix products, arithmetic and copies ran while one was open for 20% of the time, Pallas kernels for 4%

profile of v1, /device:TPU:0, one launch (start us, length us, event | category | flops | bytes accessed | tf_op | source)
XLA Modules:
  0.0 105.0 jit_solution(16585243632035408585)
XLA Ops:
  0.8 0.8 copy.35
  3.3 1.0 copy-done
  4.3 2.4 %shard_map.86 = (f32[536,128]{1,0:T(8,128)S(1)}, f32[8,104,512]{2,1,0:T(8,128)}) custom-call(f32[4,256,128]{2,1,0:T(8,128)S(1)} %copy-done, s32[128,4]{1,0:T(8,128)S(1)} %bitcast.233, s32[128,4]{1,0:T(8,128)S(1)} %bitcast.234, s32[128,4]{1,0:T(8,128)S(1)} %bitcast.235, f32[32,128]{1,0:T(8,128)S(1)} %broadcast_in_dim.34.wanted), custom_call_target="tpu_custom_call" | custom-call | tf_op jit(solution)/shard_map/pallas_call | solution.py:252
  6.7 3.0 %collective-permute-start = (f32[536,128]{1,0:T(8,128)S(1)}, f32[536,128]{1,0:T(8,128)S(1)}, u32[]{:S(2)}, u32[]{:S(2)}) collective-permute-start(f32[536,128]{1,0:T(8,128)S(1)} %get-tuple-element.8.refs_0_), channel_id=1, source_target_pairs={{0,2},{2,4},{4,6},{6,0},{1,3},{3,5},{5,7},{7,1},{8,10},{10,12},{12... | collective-permute-start | bytes 823304 | tf_op jit(solution)/shard_map/ppermute | solution.py:269
  9.7 3.9 %all-to-all-start.1 = ((f32[8,104,512]{2,1,0:T(8,128)}), f32[8,104,512]{2,1,0:T(8,128)S(1)}, u32[]{:S(2)}, u32[]{:S(2)}) async-start(f32[8,104,512]{2,1,0:T(8,128)} %get-tuple-element.9), calls=%async_computation.1 | async-start | bytes 3407872 | tf_op jit(solution)/shard_map/all_to_all | solution.py:270
  15.5 0.8 multiply_exponential_fusion.2
  17.1 1.2 %collective-permute-done.refs_1_ = f32[536,128]{1,0:T(8,128)S(1)} collective-permute-done((f32[536,128]{1,0:T(8,128)S(1)}, f32[536,128]{1,0:T(8,128)S(1)}, u32[]{:S(2)}, u32[]{:S(2)}) %collective-permute-start) | collective-permute-done | bytes 274464 | tf_op jit(solution)/shard_map/ppermute | solution.py:269
  18.9 9.0 %collective-permute-done.1.refs_2_ = f32[536,128]{1,0:T(8,128)S(1)} collective-permute-done((f32[536,128]{1,0:T(8,128)S(1)}, f32[536,128]{1,0:T(8,128)S(1)}, u32[]{:S(2)}, u32[]{:S(2)}) %collective-permute-start.1) | collective-permute-done | bytes 274464 | tf_op jit(solution)/shard_map/ppermute | solution.py:269
  28.0 0.9 exponential_select_fusion.1
  28.9 7.7 %collective-permute-done.2.refs_3_ = f32[536,128]{1,0:T(8,128)S(1)} collective-permute-done((f32[536,128]{1,0:T(8,128)S(1)}, f32[536,128]{1,0:T(8,128)S(1)}, u32[]{:S(2)}, u32[]{:S(2)}) %collective-permute-start.2) | collective-permute-done | bytes 274464 | tf_op jit(solution)/shard_map/ppermute | solution.py:269
  36.7 2.5 %shard_map.87 = f32[8,104,512]{2,1,0:T(8,128)} custom-call(f32[8,128]{1,0:T(8,128)S(1)} %broadcast_in_dim.33.wanted, f32[536,128]{1,0:T(8,128)S(1)} %get-tuple-element.8.refs_0_, f32[536,128]{1,0:T(8,128)S(1)} %collective-permute-done.refs_1_, f32[536,128]{1,0:T(8,128)S(1)} %collective-permute-done.1.refs_2_, f32[536,128]{1,0:T(8,128)S(1)} %collective-permute-done.2.refs_3_), custom_call_target="tpu_custom_call" | custom-call | tf_op jit(solution)/shard_map/pallas_call | solution.py:271
  39.2 4.0 %all-to-all-start = ((f32[8,104,512]{2,1,0:T(8,128)}), f32[8,104,512]{2,1,0:T(8,128)S(1)}, u32[]{:S(2)}, u32[]{:S(2)}) async-start(f32[8,104,512]{2,1,0:T(8,128)} %shard_map.87), calls=%async_computation | async-start | bytes 3407872 | tf_op jit(solution)/shard_map/all_to_all | solution.py:276
  43.7 1.3 %fusion.15 = f32[4,1,128]{2,1,0:T(1,128)S(1)} fusion(f32[4,128,1]{1,2,0:T(1,128)} %bitcast.240, f32[4,128,128]{2,0,1:T(4,128)} %exponential_select_fusion.1), kind=kOutput, calls=%fused_computation.22 | convolution fusion | flops 786432 | bytes 266240 | tf_op jit(solution)/shard_map/zki,zk->zi/dot_general | solution.py:210
  45.0 1.3 %shard_map.88 = (f32[128,512]{1,0:T(8,128)S(1)}, f32[128,512]{1,0:T(8,128)}, f32[128,512]{1,0:T(8,128)S(1)}, f32[128,512]{1,0:T(8,128)S(1)}) custom-call(f32[8,104,512]{2,1,0:T(8,128)S(1)} %all-to-all-done.1.arrived), custom_call_target="tpu_custom_call" | custom-call | tf_op jit(solution)/shard_map/pallas_call | solution.py:277
  48.3 1.3 %slice_bitcast_fusion.27 = f32[4]{0:T(128)} fusion(f32[4,256]{0,1:T(8,128)} %copy-done.14), kind=kLoop, calls=%fused_computation.127 | loop fusion | bytes 32 | tf_op jit(solution)/shard_map/mul | solution.py:228
  49.7 9.3 %collective-permute-done.3 = f32[128,512]{1,0:T(8,128)S(1)} collective-permute-done((f32[128,512]{1,0:T(8,128)}, f32[128,512]{1,0:T(8,128)S(1)}, u32[]{:S(2)}, u32[]{:S(2)}) %collective-permute-start.3) | collective-permute-done | bytes 262176 | tf_op jit(solution)/shard_map/ppermute | solution.py:285
  59.1 1.8 %add.427 = f32[128,512]{1,0:T(8,128)} add(f32[128,512]{1,0:T(8,128)S(1)} %collective-permute-done.3, f32[128,512]{1,0:T(8,128)} %copy-done.3) | non-fusion elementwise | flops 65536 | bytes 786432 | tf_op jit(solution)/shard_map/add | solution.py:287
  61.4 1.0 copy.40
  62.4 1.5 %copy.44 = f32[4,128]{1,0:T(4,128)} copy(f32[4,128]{0,1:T(8,128)} %copy-done.15) | data formatting | bytes 4096 | tf_op jit(solution)/shard_map/mul | solution.py:210
  63.9 2.0 %copy.45 = f32[4,256,128]{1,2,0:T(8,128)} copy(f32[4,256,128]{2,1,0:T(8,128)} %param.9) | data formatting | bytes 1048576 | tf_op args[2]
  66.0 1.3 %convolution_multiply_fusion.1 = f32[4,128,128]{2,1,0:T(8,128)} fusion(f32[4,128,128]{2,0,1:T(4,128)S(1)} %copy-done.10, f32[4]{0:T(128)S(1)} %get-tuple-element.30), kind=kOutput, calls=%fused_computation.1 | convolution fusion | flops 100728832 | bytes 524304 | tf_op jit(solution)/shard_map/zki,zkj->zij/dot_general | solution.py:209
  67.3 3.6 %collective-permute-done.4 = f32[128,512]{1,0:T(8,128)} collective-permute-done((f32[128,512]{1,0:T(8,128)}, f32[128,512]{1,0:T(8,128)}, u32[]{:S(2)}, u32[]{:S(2)}) %collective-permute-start.4) | collective-permute-done | bytes 262176 | tf_op jit(solution)/shard_map/ppermute | solution.py:285
  70.9 1.0 add.428
  72.0 3.0 %convolution_multiply_fusion = f32[4,256,256]{2,1,0:T(8,128)} fusion(f32[4,256,256]{2,0,1:T(4,128)S(1)} %copy-done.7, f32[4]{0:T(128)S(1)} %get-tuple-element.30), kind=kOutput, calls=%fused_computation | convolution fusion | flops 805568512 | bytes 2097168 | tf_op jit(solution)/shard_map/zki,zkj->zij/dot_general | solution.py:209
  74.9 5.8 %collective-permute-done.5.ring_sum = f32[128,512]{1,0:T(8,128)S(1)} collective-permute-done((f32[128,512]{1,0:T(8,128)S(1)}, f32[128,512]{1,0:T(8,128)S(1)}, u32[]{:S(2)}, u32[]{:S(2)}) %collective-permute-start.5) | collective-permute-done | bytes 262176 | tf_op jit(solution)/shard_map/ppermute | solution.py:285
  80.8 2.1 %shard_map.89 = f32[4,256,128]{2,1,0:T(8,128)} custom-call(f32[8,104,512]{2,1,0:T(8,128)S(1)} %all-to-all-done.arrived, f32[128,512]{1,0:T(8,128)S(1)} %collective-permute-done.5.ring_sum, f32[128,512]{1,0:T(8,128)S(1)} %copy-done.5), custom_call_target="tpu_custom_call" | custom-call | tf_op jit(solution)/shard_map/pallas_call | solution.py:290
  83.0 2.2 %fusion.20 = f32[4,256,128]{2,1,0:T(8,128)S(1)} fusion(f32[4,256,256]{2,1,0:T(8,128)S(1)} %copy-done.9, f32[4,256,128]{2,1,0:T(8,128)S(1)} %copy-done.11, f32[4,256,128]{2,1,0:T(8,128)} %shard_map.89), kind=kOutput, calls=%fused_computation.27 | convolution fusion | flops 402784256 | bytes 2621440 | tf_op jit(solution)/shard_map/zij,zjy->ziy/dot_general | solution.py:300
  85.6 5.2 %all-gather = f32[8,4,128]{2,1,0:T(4,128)S(1)} all-gather(f32[2,4,128]{2,1,0:T(4,128)S(1)} %pad_maximum_fusion.1), channel_id=2, replica_groups=mesh['gx'=4,'z'=4,'x'=2] {'gx'}, dimensions={0}, use_global_device_ids=true | all-gather | bytes 20480 | tf_op jit(solution)/shard_map/all_gather | solution.py:302
  91.8 0.9 fusion.4
  93.4 3.3 %all-to-all-start.2 = ((f32[8,2,4,256]{3,2,1,0:T(4,128)}), f32[8,2,4,256]{3,2,1,0:T(4,128)S(1)}, u32[]{:S(2)}, u32[]{:S(2)}) async-start(f32[8,2,4,256]{3,2,1,0:T(4,128)} %broadcast_in_dim.39), calls=%async_computation.2 | async-start | bytes 131072 | tf_op jit(solution)/shard_map/all_to_all | solution.py:309
  97.4 6.2 %all-to-all-done.2 = f32[8,2,4,256]{3,2,1,0:T(4,128)S(1)} async-done(((f32[8,2,4,256]{3,2,1,0:T(4,128)}), f32[8,2,4,256]{3,2,1,0:T(4,128)S(1)}, u32[]{:S(2)}, u32[]{:S(2)}) %all-to-all-start.2) | async-done | bytes 65568 | tf_op jit(solution)/shard_map/all_to_all | solution.py:309
  104.0 1.0 copy.46
  (103 shorter events, 11.8 us)
Async XLA Ops:
  6.7 11.6 %collective-permute-start = (f32[536,128]{1,0:T(8,128)S(1)}, f32[536,128]{1,0:T(8,128)S(1)}, u32[]{:S(2)}, u32[]{:S(2)}) collective-permute-start(f32[536,128]{1,0:T(8,128)S(1)} %get-tuple-element.8.refs_0_), channel_id=1, source_target_pairs={{0,2},{2,4},{4,6},{6,0},{1,3},{3,5},{5,7},{7,1},{8,10},{10,12},{12... | collective-permute-start | bytes 823304 | tf_op jit(solution)/shard_map/ppermute | solution.py:269
  9.7 4.0 %copy-start.25 = (f32[4]{0:T(128)S(1)}, f32[4]{0:T(128)}, u32[]{:S(2)}) copy-start(f32[4]{0:T(128)} %param.13) | copy-start | bytes 52
  9.7 29.5 %all-to-all-start.1 = ((f32[8,104,512]{2,1,0:T(8,128)}), f32[8,104,512]{2,1,0:T(8,128)S(1)}, u32[]{:S(2)}, u32[]{:S(2)}) async-start(f32[8,104,512]{2,1,0:T(8,128)} %get-tuple-element.9), calls=%async_computation.1 | async-start | bytes 3407872 | tf_op jit(solution)/shard_map/all_to_all | solution.py:270
  15.4 1.7 %copy-start.6 = (f32[4,256,256]{2,0,1:T(4,128)}, f32[4,256,256]{2,0,1:T(4,128)S(1)}, u32[]{:S(2)}) copy-start(f32[4,256,256]{2,0,1:T(4,128)S(1)} %exponential_select_fusion) | copy-start | bytes 3145732
  18.3 9.6 %collective-permute-start.1 = (f32[536,128]{1,0:T(8,128)S(1)}, f32[536,128]{1,0:T(8,128)S(1)}, u32[]{:S(2)}, u32[]{:S(2)}) collective-permute-start(f32[536,128]{1,0:T(8,128)S(1)} %collective-permute-done.refs_1_), channel_id=1, source_target_pairs={{0,2},{2,4},{4,6},{6,0},{1,3},{3,5},{5,7},{7,1},{8,10},{10,12},{12... | collective-permute-start | bytes 823304 | tf_op jit(solution)/shard_map/ppermute | solution.py:269
  18.9 24.2 %copy-start.14 = (f32[4,256]{0,1:T(8,128)}, f32[4,256]{0,1:T(8,128)S(1)}, u32[]{:S(2)}) copy-start(f32[4,256]{0,1:T(8,128)S(1)} %bitcast_multiply_fusion) | copy-start | bytes 12292
  27.9 8.7 %collective-permute-start.2 = (f32[536,128]{1,0:T(8,128)S(1)}, f32[536,128]{1,0:T(8,128)S(1)}, u32[]{:S(2)}, u32[]{:S(2)}) collective-permute-start(f32[536,128]{1,0:T(8,128)S(1)} %collective-permute-done.1.refs_2_), channel_id=1, source_target_pairs={{0,2},{2,4},{4,6},{6,0},{1,3},{3,5},{5,7},{7,1},{8,10},{10,12},{12... | collective-permute-start | bytes 823304 | tf_op jit(solution)/shard_map/ppermute | solution.py:269
  39.2 41.6 %all-to-all-start = ((f32[8,104,512]{2,1,0:T(8,128)}), f32[8,104,512]{2,1,0:T(8,128)S(1)}, u32[]{:S(2)}, u32[]{:S(2)}) async-start(f32[8,104,512]{2,1,0:T(8,128)} %shard_map.87), calls=%async_computation | async-start | bytes 3407872 | tf_op jit(solution)/shard_map/all_to_all | solution.py:276
  48.3 17.6 %copy-start.10 = (f32[4,128,128]{2,0,1:T(4,128)S(1)}, f32[4,128,128]{2,0,1:T(4,128)}, u32[]{:S(2)}) copy-start(f32[4,128,128]{2,0,1:T(4,128)} %exponential_select_fusion.1) | copy-start | bytes 786436
  48.3 22.6 %copy-start.2 = (f32[128,512]{1,0:T(8,128)S(1)}, f32[128,512]{1,0:T(8,128)}, u32[]{:S(2)}) copy-start(f32[128,512]{1,0:T(8,128)} %copy-done.1) | copy-start | bytes 786436
  48.3 10.7 %collective-permute-start.3 = (f32[128,512]{1,0:T(8,128)}, f32[128,512]{1,0:T(8,128)S(1)}, u32[]{:S(2)}, u32[]{:S(2)}) collective-permute-start(f32[128,512]{1,0:T(8,128)} %get-tuple-element.10), channel_id=1, source_target_pairs={{0,2},{2,4},{4,6},{6,0},{1,3},{3,5},{5,7},{7,1},{8,10},{10,12},{12... | collective-permute-start | bytes 786440 | tf_op jit(solution)/shard_map/ppermute | solution.py:285
  49.7 11.1 %copy-start.15 = (f32[4,128]{0,1:T(8,128)}, f32[4,128]{0,1:T(8,128)S(1)}, u32[]{:S(2)}) copy-start(f32[4,128]{0,1:T(8,128)S(1)} %bitcast_multiply_fusion.1) | copy-start | bytes 6148
  59.1 12.9 %copy-start.7 = (f32[4,256,256]{2,0,1:T(4,128)S(1)}, f32[4,256,256]{2,0,1:T(4,128)}, u32[]{:S(2)}) copy-start(f32[4,256,256]{2,0,1:T(4,128)} %copy-done.6) | copy-start | bytes 3145732
  60.8 10.0 %collective-permute-start.4 = (f32[128,512]{1,0:T(8,128)}, f32[128,512]{1,0:T(8,128)}, u32[]{:S(2)}, u32[]{:S(2)}) collective-permute-start(f32[128,512]{1,0:T(8,128)} %add.427), channel_id=1, source_target_pairs={{0,2},{2,4},{4,6},{6,0},{1,3},{3,5},{5,7},{7,1},{8,10},{10,12},{12... | collective-permute-start | bytes 786440 | tf_op jit(solution)/shard_map/ppermute | solution.py:285
  66.0 14.8 %copy-start.5 = (f32[128,512]{1,0:T(8,128)S(1)}, f32[128,512]{1,0:T(8,128)}, u32[]{:S(2)}) copy-start(f32[128,512]{1,0:T(8,128)} %copy-done.4) | copy-start | bytes 786436
  71.9 8.9 %collective-permute-start.5 = (f32[128,512]{1,0:T(8,128)S(1)}, f32[128,512]{1,0:T(8,128)S(1)}, u32[]{:S(2)}, u32[]{:S(2)}) collective-permute-start(f32[128,512]{1,0:T(8,128)S(1)} %add.428), channel_id=1, source_target_pairs={{0,2},{2,4},{4,6},{6,0},{1,3},{3,5},{5,7},{7,1},{8,10},{10,12},{12... | collective-permute-start | bytes 786440 | tf_op jit(solution)/shard_map/ppermute | solution.py:285
  74.9 8.0 %copy-start.9 = (f32[4,256,256]{2,1,0:T(8,128)S(1)}, f32[4,256,256]{2,1,0:T(8,128)}, u32[]{:S(2)}) copy-start(f32[4,256,256]{2,1,0:T(8,128)} %convolution_multiply_fusion) | copy-start | bytes 3145732
  80.8 2.1 %copy-start.11 = (f32[4,256,128]{2,1,0:T(8,128)S(1)}, f32[4,256,128]{2,1,0:T(8,128)}, u32[]{:S(2)}) copy-start(f32[4,256,128]{2,1,0:T(8,128)} %param.8) | copy-start | bytes 1572868
  82.9 2.3 %copy-start.8 = (f32[4,256,128]{2,1,0:T(8,128)S(1)}, f32[4,256,128]{2,1,0:T(8,128)}, u32[]{:S(2)}) copy-start(f32[4,256,128]{2,1,0:T(8,128)} %shard_map.89) | copy-start | bytes 1572868
  82.9 7.9 %copy-start.19 = (f32[4]{0:T(128)S(1)}, f32[4]{0:T(128)}, u32[]{:S(2)}) copy-start(f32[4]{0:T(128)} %get-tuple-element.27) | copy-start | bytes 52
  82.9 7.9 %copy-start.20 = (f32[4]{0:T(128)S(1)}, f32[4]{0:T(128)}, u32[]{:S(2)}) copy-start(f32[4]{0:T(128)} %get-tuple-element.28) | copy-start | bytes 52
  82.9 8.0 %copy-start.23 = (f32[4]{0:T(128)S(1)}, f32[4]{0:T(128)}, u32[]{:S(2)}) copy-start(f32[4]{0:T(128)} %broadcast_multiply_fusion.2) | copy-start | bytes 52
  82.9 8.0 %copy-start.24 = (f32[4]{0:T(128)S(1)}, f32[4]{0:T(128)}, u32[]{:S(2)}) copy-start(f32[4]{0:T(128)} %slice_bitcast_fusion.27) | copy-start | bytes 52
  82.9 8.1 %slice-start = ((f32[4,128,128]{2,0,1:T(4,128)}), f32[4,1,128]{2,0,1:T(4,128)S(1)}, s32[]{:S(2)}) async-start(f32[4,128,128]{2,0,1:T(4,128)} %exponential_select_fusion.1), calls=%async_computation.3 | async-start | bytes 4096 | tf_op jit(solution)/shard_map/slice | solution.py:211
  83.0 8.9 %copy-start.13 = (f32[4,128,128]{2,1,0:T(8,128)S(1)}, f32[4,128,128]{2,1,0:T(8,128)}, u32[]{:S(2)}) copy-start(f32[4,128,128]{2,1,0:T(8,128)} %convolution_multiply_fusion.1) | copy-start | bytes 786436
  85.2 18.4 %copy-start.18 = (f32[4]{0:T(128)S(1)}, f32[4]{0:T(128)}, u32[]{:S(2)}) copy-start(f32[4]{0:T(128)} %get-tuple-element.26) | copy-start | bytes 52
  85.2 18.4 %copy-start.21 = (f32[4]{0:T(128)S(1)}, f32[4]{0:T(128)}, u32[]{:S(2)}) copy-start(f32[4]{0:T(128)} %get-tuple-element.22) | copy-start | bytes 52
  85.2 18.5 %copy-start.22 = (f32[4]{0:T(128)S(1)}, f32[4]{0:T(128)}, u32[]{:S(2)}) copy-start(f32[4]{0:T(128)} %broadcast_multiply_fusion) | copy-start | bytes 52
  85.2 18.6 %copy-start.12 = (f32[4,256,128]{1,2,0:T(8,128)S(1)}, f32[4,256,128]{1,2,0:T(8,128)}, u32[]{:S(2)}) copy-start(f32[4,256,128]{1,2,0:T(8,128)} %copy.45) | copy-start | bytes 1572868
  85.2 18.6 %copy-start.16 = (f32[4,128]{1,0:T(4,128)S(1)}, f32[4,128]{1,0:T(4,128)}, u32[]{:S(2)}) copy-start(f32[4,128]{1,0:T(4,128)} %copy.44) | copy-start | bytes 6148
  85.2 18.6 %copy-start.17 = (f32[4,128]{1,0:T(4,128)S(1)}, f32[4,128]{1,0:T(4,128)}, u32[]{:S(2)}) copy-start(f32[4,128]{1,0:T(4,128)} %get-tuple-element.32) | copy-start | bytes 6148
  93.4 10.2 %all-to-all-start.2 = ((f32[8,2,4,256]{3,2,1,0:T(4,128)}), f32[8,2,4,256]{3,2,1,0:T(4,128)S(1)}, u32[]{:S(2)}, u32[]{:S(2)}) async-start(f32[8,2,4,256]{3,2,1,0:T(4,128)} %broadcast_in_dim.39), calls=%async_computation.2 | async-start | bytes 131072 | tf_op jit(solution)/shard_map/all_to_all | solution.py:309
  (4 other events, 3.1 us)

commit v2 on v1

v2 whole, which is shorter than its diff:
```python
import functools

import jax
import jax.numpy as jnp
from jax import lax
from jax.experimental import pallas as pl
from jax.experimental.pallas import tpu as pltpu
from jax.sharding import Mesh
from jax.sharding import PartitionSpec as P

TS = 16
SUB = 8
LANES = 128
F32 = jnp.float32
BF16 = jnp.bfloat16
BYTES_A_MICRO = 3_690_000
VMEM_LIMIT = 48 * 1024 * 1024


def split(x):
    high = x.astype(BF16)
    return high, (x - high.astype(F32)).astype(BF16)


def mm(a, b):
    return jnp.dot(a, b, preferred_element_type=F32)


def mm_t(a, b):
    return lax.dot_general(a, b, (((0,), (0,)), ((), ())), preferred_element_type=F32)


def dot3(a, b):
    a_high, a_low = split(a)
    b_high, b_low = split(b)
    return mm(a_high, b_high) + mm(a_high, b_low) + mm(a_low, b_high)


def swap_blocks(x):
    rows = x.shape[0]
    x = x.reshape(rows // SUB, SUB, LANES)
    sub = lax.broadcasted_iota(jnp.int32, x.shape, 1)
    block = lax.broadcasted_iota(jnp.int32, x.shape, 2) // TS
    for k in (4, 2, 1):
        up = pltpu.roll(pltpu.roll(x, SUB - k, 1), TS * k, 2)
        down = up if 2 * k == SUB else pltpu.roll(pltpu.roll(x, k, 1), LANES - TS * k, 2)
        moved = jnp.where((sub & k) == 0, up, down)
        x = jnp.where((sub & k) == (block & k), x, moved)
    return x.reshape(rows, LANES)


def tile_columns(tiled, planes, tiles_x):
    grouped = tiled.reshape(planes, tiles_x, 2, SUB, LANES)
    columns = [grouped[z, :, h].reshape(tiles_x * SUB, LANES) for z in range(planes) for h in range(2)]
    return jnp.concatenate(columns, axis=1)


def tile_rows(columns, planes, tiles_x):
    parts = [
        columns[:, i * LANES:(i + 1) * LANES].reshape(1, tiles_x, 1, SUB, LANES) for i in range(2 * planes)
    ]
    planes_of = [jnp.concatenate(parts[2 * z:2 * z + 2], axis=2) for z in range(planes)]
    return jnp.concatenate(planes_of, axis=0).reshape(planes * tiles_x * TS, LANES)


def route_rows(names, tiles, shares, wanted):
    fanout, count = names.shape
    member = jnp.zeros(wanted.shape, F32)
    weight = jnp.zeros(wanted.shape, F32)
    label = jnp.zeros(wanted.shape, F32)
    for k in range(fanout):
        hit = names[k:k + 1, :] == wanted
        member = member + jnp.where(hit, 1.0, 0.0)
        weight = weight + jnp.where(hit, shares[k:k + 1, :], 0.0)
        label = label + jnp.where(hit, tiles[k:k + 1, :], 0.0)
    return member, weight, label


def ranked(member):
    count = member.shape[1]
    before = lax.broadcasted_iota(jnp.int32, (count, count), 0) < lax.broadcasted_iota(
        jnp.int32, (count, count), 1
    )
    rank = mm(member.astype(BF16), jnp.where(before, 1.0, 0.0).astype(BF16))
    return jnp.where(member > 0.0, rank, 2.0 * count)


def slots_of(rank, weight, label, capacity):
    slot = lax.broadcasted_iota(jnp.int32, (capacity, rank.shape[1]), 0).astype(F32)
    chosen = rank == slot
    picked = jnp.where(chosen, weight, 0.0)
    labels = jnp.sum(jnp.where(chosen, label, 0.0), axis=1, keepdims=True)
    return picked, labels


def place_labels(board, labels, first):
    lane = lax.broadcasted_iota(jnp.int32, board.shape, 1)
    for g in range(labels.shape[0] // SUB):
        board = jnp.where(lane == first + g, labels[g * SUB:(g + 1) * SUB], board)
    return board


def read_labels(board, first, capacity):
    lane = lax.broadcasted_iota(jnp.int32, (SUB, LANES), 1).astype(F32)
    rows = [
        jnp.where(board[:, first + g:first + g + 1] == lane, 1.0, 0.0) for g in range(capacity // SUB)
    ]
    return jnp.concatenate(rows, axis=0)


def turned_by(at, steps, size):
    at = at + steps
    return jnp.where(at >= size, at - size, at)


def columns_wanted(shape, depth, inner, level, steps):
    row = lax.broadcasted_iota(jnp.int32, shape, 0)
    column, steps = (row // depth, row % depth) if steps is None else (row, steps)
    level = turned_by(level, depth - steps, depth)
    return (column // inner * (depth * inner) + level * inner + column % inner).astype(F32)


def ring_kernel(planes_a, source, routes, ring, tiled):
    planes, cells_x, _ = source.shape
    half = planes_a * cells_x
    fanout = routes.shape[1]
    ring[:half, :] = swap_blocks(source[:planes_a].reshape(half, LANES))
    ring[half:, :] = jnp.zeros((3 * SUB, LANES), F32)
    ring[half:half + fanout, :] = routes[0]
    ring[half + SUB:half + SUB + fanout, :] = routes[1]
    ring[half + 2 * SUB:half + 2 * SUB + fanout, :] = routes[2] / jnp.sum(routes[2], axis=0, keepdims=True)
    tiled[...] = swap_blocks(source[planes_a:].reshape(tiled.shape[0], LANES))


def start_kernel(capacity, columns, depth, inner, planes_a, fanout, at, ring, tiled, pack_out, picked):
    cells_x = (ring.shape[0] - 3 * SUB) // planes_a
    rest = tiled.shape[0] // cells_x
    names, tiles, shares = routing(ring, fanout)
    wanted = columns_wanted((columns * depth, LANES), depth, inner, at[1], None)
    member, weight, label = route_rows(names, tiles, shares, wanted)
    rank = ranked(member)
    for j in range(columns):
        board = jnp.zeros((SUB, LANES), F32)
        for r in range(depth):
            n = j * depth + r
            rows, labels = slots_of(rank[n:n + 1], weight[n:n + 1], label[n:n + 1], capacity)
            picked[n * capacity:(n + 1) * capacity, :] = rows
            board = place_labels(board, labels, r * (capacity // SUB))
        pack_out[j, depth * capacity:, :] = jnp.zeros((SUB, pack_out.shape[2]), F32)
        pack_out[j, depth * capacity:, :LANES] = board
    packed = dot3(picked[...], tile_columns(tiled[...], rest, cells_x // TS))
    pack_out[:, :depth * capacity, :] = packed.reshape(columns, depth * capacity, packed.shape[1])


def routing(ring, fanout):
    first = ring.shape[0] - 3 * SUB
    return [ring[first + k * SUB:first + k * SUB + fanout, :] for k in range(3)]


def forward_kernel(capacity, columns, depth, inner, planes_a, fanout, at, *refs):
    rings, edges, (pack_out, picked) = refs[:depth], refs[depth:-2], refs[-2:]
    half = rings[0].shape[0] - 3 * SUB
    tiles_x = half // planes_a // TS
    boards = [jnp.zeros((SUB, LANES), F32) for _ in range(columns)]
    wanted = columns_wanted((columns, LANES), depth, inner, at[1], 0)
    for s in range(depth):
        member, weight, label = route_rows(*routing(rings[s], fanout), wanted)
        rank = ranked(member)
        for j in range(columns):
            rows, labels = slots_of(rank[j:j + 1], weight[j:j + 1], label[j:j + 1], capacity)
            picked[j * capacity:(j + 1) * capacity, :] = rows
            boards[j] = place_labels(boards[j], labels, s * (capacity // SUB))
        packed = dot3(picked[...], tile_columns(rings[s][:half, :], planes_a, tiles_x))
        pack_out[:, s * capacity:(s + 1) * capacity, :] = packed.reshape(columns, capacity, packed.shape[1])
    value = edges[0][...]
    for part in edges[1:]:
        value = value + part[...]
    for i in range(value.shape[1] // SUB):
        first = (1 + i) * LANES
        pack_out[:, depth * capacity:, first:first + LANES] = value[:, i * SUB:(i + 1) * SUB, :]
    for j in range(columns):
        pack_out[j, depth * capacity:, :LANES] = boards[j]


def gather_sum(arrived, capacity, groups):
    columns, rows, _ = arrived.shape
    total = rows - SUB
    heads, cells = [], []
    for j in range(columns):
        board = arrived[j, total:, :LANES]
        for g in groups:
            heads.append(read_labels(board, g * (capacity // SUB), capacity))
            cells.append(arrived[j, g * capacity:(g + 1) * capacity, :])
    head = jnp.concatenate(heads, axis=0).astype(BF16)
    high, low = split(jnp.concatenate(cells, axis=0))
    return mm_t(head, high) + mm_t(head, low)


def partial_kernel(capacity, arrived, *outs):
    for r, out in enumerate(outs):
        out[...] = gather_sum(arrived, capacity, [r])


def edge_sums(proj, weight, label, tiles_x, tiles_y, logs, part):
    label = label.astype(jnp.int32)
    tile_x, tile_y = label // tiles_y, label % tiles_y
    place, other, size = (tile_y, tile_x, tiles_x) if part == 0 else (tile_x, tile_y, tiles_y)
    per = tiles_y if part == 0 else tiles_x
    blocks = weight.shape[0]
    proj = proj[:, part * LANES:(part + 1) * LANES]
    owner = lax.broadcasted_iota(jnp.int32, proj.shape, 1) // TS
    row = lax.broadcasted_iota(jnp.int32, (per, weight.shape[1]), 0)
    here = [place[n:n + 1] == row for n in range(blocks)]
    planes = len(logs)
    left, right = [], []
    for kind in range(2):
        gap = (size - 1 - other if kind == 0 else other).astype(F32)
        for z in range(planes):
            value = weight * jnp.exp(gap * (TS * logs[z]))
            left.append(
                jnp.concatenate([jnp.where(here[n], value[n:n + 1], 0.0) for n in range(blocks)], axis=0)
            )
            right.append(jnp.where(owner == kind * planes + z, proj, 0.0))
    a_high, a_low = split(jnp.concatenate(left, axis=1))
    b_high, b_low = split(jnp.concatenate(right, axis=0))
    both = mm(a_high, jnp.concatenate([b_high, b_low], axis=1))
    total = both[:, :LANES] + both[:, LANES:] + mm(a_low, b_high)
    return total.reshape(blocks, per, LANES)


def line_carries(ends, starts, across, first):
    forward, full, running = [], [], jnp.zeros_like(ends[0])
    for end, start in zip(ends, starts):
        forward.append(running)
        full.append(start + first * running)
        running = across * running + end
    backward, running = [], jnp.zeros_like(ends[0])
    for start in full[::-1]:
        backward.append(running)
        running = across * running + start
    return forward, backward[::-1]


def end_start(both, gain, back):
    half = both.shape[1] // 2
    end = both[:, :half]
    return end, gain[:half] * both[:, half:] - back[:half] * end


def edge_kernel(grid_x, depth, inner, planes, fanout, at, logs_in, target, table, lines, coef, both_x, ring, tiled,
                earlier, later, *refs):
    del earlier, later
    outs, carries = refs[:-1], refs[-1]
    _, cells_x, cells_y = target.shape
    tiles_x, tiles_y = cells_x // TS, cells_y // TS
    half = ring.shape[0] - 3 * SUB
    planes_a = half // cells_x
    logs = [logs_in[z] for z in range(planes)]
    names, tiles, shares = routing(ring, fanout)
    cells = [tile_columns(ring[:half, :], planes_a, tiles_x), tile_columns(tiled[...], planes - planes_a, tiles_x)]
    proj = dot3(jnp.concatenate(cells, axis=1), table[...])
    cells = swap_blocks(target[...].reshape(planes * cells_x, LANES))
    own = dot3(tile_columns(cells, planes, tiles_x), table[...])
    tile_count = names.shape[1]
    along = depth * inner
    blocks = grid_x * along
    wanted = lax.broadcasted_iota(jnp.int32, (blocks, tile_count), 0).astype(F32)
    _, weight, label = route_rows(names, tiles, shares, wanted)
    mine = lax.broadcasted_iota(jnp.int32, (1, tile_count), 1).astype(F32)
    one = jnp.ones((1, tile_count), F32)
    here = at[0] * along + at[1] * inner + at[2]
    edges = []
    for part in range(2):
        sums = edge_sums(proj, weight, label, tiles_x, tiles_y, logs, part)
        plus = edge_sums(own, one, mine, tiles_x, tiles_y, logs, part)
        is_here = lax.broadcasted_iota(jnp.int32, sums.shape, 0) == here
        sums = jnp.where(is_here, plus, 0.0) - sums
        edges.append(swap_blocks(sums.reshape(-1, LANES)).reshape(blocks, sums.shape[1] // SUB, SUB, LANES))
    gain, across_x, first_x, back_x, across_y, first_y, back_y = [coef[i][:, :1] for i in range(7)]

    ends, starts = zip(*[
        end_start(edges[0][p * along:(p + 1) * along, 0], gain, back_x) for p in range(grid_x)
    ])
    forward, backward = line_carries(ends, starts, across_x[:planes], first_x[:planes])
    for p in range(grid_x):
        rows = jnp.concatenate([forward[p], backward[p]], axis=1).reshape(depth, inner, SUB, LANES)
        carries[:, p * inner:(p + 1) * inner, :SUB, :] = rows

    side = jnp.concatenate([edges[1][:, i] for i in range(edges[1].shape[1])], axis=2)
    flat = side.reshape(blocks * SUB, cells_x)
    local = jnp.zeros_like(flat)
    for z in range(planes):
        local = local + dot3(masked(flat, planes, z), both_x[z])
    local = local.reshape(side.shape)
    ends = jnp.sum(side * lines[0], axis=2, keepdims=True)
    starts = jnp.sum(side * lines[1], axis=2, keepdims=True)
    forward, backward = line_carries(
        [ends[p * along:(p + 1) * along] for p in range(grid_x)],
        [starts[p * along:(p + 1) * along] for p in range(grid_x)],
        across_x,
        first_x,
    )
    smooth = [
        local[p * along:(p + 1) * along] + forward[p] * lines[2] + backward[p] * lines[3] for p in range(grid_x)
    ]
    smooth = jnp.stack(smooth)
    ends, starts = zip(*[end_start(smooth[:, q], gain, back_y) for q in range(along)])
    forward, backward = line_carries(ends, starts, across_y[:planes], first_y[:planes])
    for q in range(along):
        rows = jnp.concatenate([forward[q], backward[q]], axis=1)
        for p in range(grid_x):
            for i in range(cells_x // LANES):
                carries[q // inner, p * inner + q % inner, (1 + i) * SUB:(2 + i) * SUB, :] = (
                    rows[p, :, i * LANES:(i + 1) * LANES]
                )
    for o, out in enumerate(outs):
        out[...] = carries[turned_by(at[1], o, depth)]


def masked(rows, planes, z):
    row = lax.broadcasted_iota(jnp.int32, rows.shape, 0)
    return jnp.where(row % planes == z, rows, 0.0)


def outer(a, b):
    a_high, a_low = split(a)
    b_high, b_low = split(b)
    return mm_t(a_high, b_high) + mm_t(a_high, b_low) + mm_t(a_low, b_high)


def base_kernel(target, potential, both_x, both_y, out):
    for z in range(target.shape[0]):
        out[z] = potential[z] + dot3(dot3(both_x[z], target[z]), both_y[z])


def solve(pushed, before, both_x, both_y):
    return before - dot3(dot3(both_x, pushed), both_y)


def near_kernel(capacity, depth, arrived, base, both_x, both_y, curve_x, curve_y, pushed_out, next_out, rest_out):
    planes, planes_a = base.shape[0], pushed_out.shape[0]
    cells_x = pushed_out.shape[1]
    columns, rows, width = arrived.shape
    carries = arrived[0, rows - SUB:, :]
    for j in range(1, columns):
        carries = carries + arrived[j, rows - SUB:, :]
    carry_x, carry_y = carries[:, LANES:2 * LANES], carries[:, 2 * LANES:2 * LANES + cells_x]
    total = gather_sum(arrived, capacity, list(range(depth)))
    pushed = swap_blocks(tile_rows(total, planes_a, cells_x // TS)).reshape(planes_a, cells_x, LANES)
    pushed_out[...] = pushed
    for z in range(planes):
        left = jnp.concatenate([masked(curve_x[...], planes, z), masked(carry_y, planes, z)], axis=0)
        right = jnp.concatenate([dot3(carry_x, both_y[z]), curve_y[...]], axis=0)
        before = base[z] + outer(left, right)
        if z < planes_a:
            next_out[z] = solve(pushed[z], before, both_x[z], both_y[z])
        else:
            rest_out[z - planes_a] = before


def far_kernel(first, pushed_in, next_in, base, both_x, both_y, *refs):
    del pushed_in, next_in
    sums, (pushed_out, next_out) = refs[:-2], refs[-2:]
    count, cells_x, _ = pushed_out.shape
    total = sums[0][...]
    for part in sums[1:]:
        total = total + part[...]
    pushed = swap_blocks(tile_rows(total, count, cells_x // TS)).reshape(count, cells_x, LANES)
    for z in range(count):
        pushed_out[z] = pushed[z]
        next_out[z] = solve(pushed[z], base[z], both_x[first + z], both_y[first + z])


def call(micros, body, out_shape, in_specs=None, scratch=(), **extra):
    if in_specs is not None:
        extra["in_specs"] = in_specs
    return pl.pallas_call(
        body,
        out_shape=out_shape,
        scratch_shapes=list(scratch),
        compiler_params=pltpu.CompilerParams(vmem_limit_bytes=VMEM_LIMIT),
        cost_estimate=pl.CostEstimate(flops=0, bytes_accessed=int(micros * BYTES_A_MICRO), transcendentals=0),
        **extra,
    )


def table_kernel(planes, decay_in, logs_in, earlier, table, lines, coef, curve_x, curve_y, both_x, both_y):
    del earlier
    row = lax.broadcasted_iota(jnp.int32, (2 * planes, LANES), 0)
    decay, rate = jnp.zeros(row.shape, F32), jnp.zeros(row.shape, F32)
    for z in range(planes):
        decay = jnp.where(row % planes == z, decay_in[z], decay)
        rate = jnp.where(row % planes == z, logs_in[z], rate)
    gain = (1.0 - decay) / (1.0 + decay)
    coef[0] = gain
    for i, (curve, both) in enumerate(((curve_x, both_x), (curve_y, both_y))):
        length = curve.shape[1]
        across = jnp.exp(length * rate)
        coef[1 + 3 * i] = across
        coef[2 + 3 * i] = gain * decay * (1.0 - across * across)
        coef[3 + 3 * i] = gain * decay * across
        slope, width, turn = rate[:, :1], gain[:, :1], (gain * decay)[:, :1]
        place = lax.broadcasted_iota(jnp.int32, curve.shape, 1).astype(F32)
        risen = jnp.exp(place * slope) - jnp.exp((2.0 * length - place) * slope)
        fall = jnp.exp((length - place) * slope)
        bend = turn * risen
        curve[...] = jnp.where(lax.broadcasted_iota(jnp.int32, curve.shape, 0) < planes, bend, fall)
        if i == 0:
            lines[0] = jnp.exp((length - 1.0 - place) * slope)
            lines[1] = width * risen
            lines[2] = bend
            lines[3] = fall
        rows = lax.broadcasted_iota(jnp.int32, (length, length), 0).astype(F32)
        cols = lax.broadcasted_iota(jnp.int32, (length, length), 1).astype(F32)
        apart, down = jnp.abs(rows - cols), length - rows[:, :1]
        for z in range(planes):
            log = logs_in[z]
            both[z] = width[z:z + 1] * (jnp.exp(apart * log) - jnp.exp(down * log) * fall[z:z + 1])
    cells = TS * TS
    shape = (cells, table.shape[1])
    row, col = lax.broadcasted_iota(jnp.int32, shape, 0), lax.broadcasted_iota(jnp.int32, shape, 1)
    along_y, kind = col // (2 * planes * TS) == 1, col // (planes * TS) % 2
    owner, cell = col // TS % planes, col % TS
    at_x, at_y = row // TS, row % TS
    summed, kept = jnp.where(along_y, at_y, at_x), jnp.where(along_y, at_x, at_y)
    steps = jnp.where(kind == 0, TS - 1 - summed, summed).astype(F32)
    for z in range(planes):
        power = jnp.exp(steps * logs_in[z])
        table[z * cells:(z + 1) * cells, :] = jnp.where((owner == z) & (kept == cell), power, 0.0)


def per_device(source_mass, target_density, potential, dest_device, dest_tile, mass_counts, reach):
    planes, cells_x, cells_y = source_mass.shape
    tile_count, fanout = dest_device.shape[2:]
    tiles_x, tiles_y = cells_x // TS, cells_y // TS
    grid_x, depth, inner = lax.axis_size("gx"), lax.axis_size("z"), lax.axis_size("x")
    columns = grid_x * inner
    device_count = columns * depth
    capacity = max(2, 3 * fanout * tile_count // (2 * device_count))
    capacity = -(-capacity // SUB) * SUB
    rows = depth * capacity + SUB
    planes_a = planes // 2
    rest = planes - planes_a
    tile_cells = 2 * LANES
    at = jnp.stack([lax.axis_index("gx"), lax.axis_index("z"), lax.axis_index("x")])
    scalars, near = pl.BlockSpec(memory_space=pltpu.SMEM), pl.BlockSpec(memory_space=pltpu.VMEM)
    far = pl.BlockSpec(memory_space=pl.ANY)

    def array(*shape):
        return jax.ShapeDtypeStruct(shape, F32)

    def turn(x, axis, steps):
        size = lax.axis_size(axis)
        return lax.ppermute(x, axis, [(i, (i + steps) % size) for i in range(size)])

    routes = jnp.stack([x.reshape(tile_count, fanout).T for x in (dest_device, dest_tile, mass_counts)])
    ring, tiled = call(
        0.8, functools.partial(ring_kernel, planes_a),
        [array(planes_a * cells_x + 3 * SUB, LANES), array(rest * cells_x, LANES)],
    )(source_mass, routes.astype(F32))
    packed_b = call(
        2.7, functools.partial(start_kernel, capacity, columns, depth, inner, planes_a, fanout),
        array(columns, rows, rest * tile_cells),
        [scalars] + [near] * 2,
        [pltpu.VMEM((columns * depth * capacity, tile_count), F32)],
    )(at, ring, tiled)
    arrived_b = lax.all_to_all(packed_b, ("gx", "x"), 0, 0, tiled=True)
    rings = [ring] + [None] * (depth - 1)
    for s in range(1, depth // 2 + 1):
        rings[s] = turn(rings[s - 1], "z", 1)
        if s < depth - s:
            rings[depth - s] = turn(rings[(depth - s + 1) % depth], "z", -1)

    decay = 1.0 - 1.0 / reach
    logs = jnp.log(decay)
    eight = 2 * planes
    table, lines, coef, curve_x, curve_y, both_x, both_y = call(
        1.2, functools.partial(table_kernel, planes),
        [
            array(planes * TS * TS, 4 * planes * TS), array(4, eight, cells_x), array(7, eight, LANES),
            array(eight, cells_x), array(eight, cells_y), array(planes, cells_x, cells_x),
            array(planes, cells_y, cells_y),
        ],
        [scalars] * 2 + [far],
    )(decay, logs, packed_b)
    edge_rows = tiles_x + tiles_y
    edges = call(
        4.7, functools.partial(edge_kernel, grid_x, depth, inner, planes, fanout),
        [array(columns, edge_rows, LANES)] * depth,
        [scalars] * 2 + [near] * 7 + [far] * 2,
        [pltpu.VMEM((depth, columns, edge_rows, LANES), F32)],
    )(at, logs, target_density, table, lines, coef, both_x, ring, tiled, rings[1], rings[-1])
    edges = [edges[0]] + [turn(edges[o], "z", o) for o in range(1, depth)]
    packed_a = call(
        1.9, functools.partial(forward_kernel, capacity, columns, depth, inner, planes_a, fanout),
        array(columns, rows, planes_a * tile_cells),
        [scalars] + [near] * (depth + len(edges)),
        [pltpu.VMEM((columns * capacity, tile_count), F32)],
    )(at, *rings, *edges)
    arrived_a = lax.all_to_all(packed_a, ("gx", "x"), 0, 0, tiled=True)
    sums = call(1.4, functools.partial(partial_kernel, capacity), [array(tile_count, rest * tile_cells)] * depth)(arrived_b)
    moving = [sums[0]] + [turn(sums[r], "z", -r) for r in range(1, depth)]
    base = call(1.3, base_kernel, array(*potential.shape))(target_density, potential, both_x, both_y)
    field = (planes_a, cells_x, cells_y)
    shapes = [array(*source_mass.shape), array(*potential.shape)]
    part = pl.BlockSpec(field, lambda i: (0, 0, 0))
    *outs, base = call(
        3.9, functools.partial(near_kernel, capacity, depth), shapes + [array(rest, cells_x, cells_y)], [near] * 6,
        out_specs=[part, part, near], grid=(1,),
    )(arrived_a, base, both_x, both_y, curve_x, curve_y)
    part = pl.BlockSpec(field, lambda i: (1, 0, 0))
    outs = call(
        1.7, functools.partial(far_kernel, planes_a), shapes, [far, far] + [near] * (3 + depth),
        out_specs=[part, part], grid=(1,), input_output_aliases={0: 0, 1: 1},
    )(*outs, base, both_x, both_y, *moving)
    return tuple(outs)


def solution(mesh):
    grid_x, grid_y = mesh.shape["gx"], mesh.shape["gy"]
    inner = grid_x // 2
    if inner < 1 or grid_y % inner:
        inner = 1
    depth = grid_y // inner
    split_mesh = Mesh(mesh.devices.reshape(grid_x, depth, inner), ("gx", "z", "x"))
    field = P(None, "gx", ("z", "x"))
    table = P("gx", ("z", "x"), None, None)
    return jax.shard_map(
        per_device,
        mesh=split_mesh,
        in_specs=(field, field, field, table, table, table, P()),
        out_specs=(field, field),
        check_vma=False,
    )
```

time: 106 us -> 80.9 us (0.76)
  local copies, waits for them, and re-layouts: 14.2 us -> 2.28 us
  Pallas kernels: 8.25 us -> 19.3 us
  matrix products: 10.5 us -> 0 us
  waiting for transfers between devices: 42.9 us -> 33 us
  starting transfers between devices: 14.7 us -> 24.3 us
  other arithmetic: 8.37 us -> 0.8 us
  blocking collectives: 5.19 us -> 0 us
    ppermute x6 -> x9, waiting for transfers between devices: 36.7 us -> 17.8 us  [turn(): return lax.ppermute(x, axis, [(i, (i + steps) % size) for i in range(size)])]
    all_to_all x1, waiting for transfers between devices: 0.01 us -> 15.3 us  [per_device(): arrived_a = lax.all_to_all(packed_a, ('gx', 'x'), 0, 0, tiled=True)]
    ppermute x6 -> x9, starting transfers between devices: 3.51 us -> 14.7 us  [turn(): return lax.ppermute(x, axis, [(i, (i + steps) % size) for i in range(size)])]
    pallas_call x4 -> x9, Pallas kernels: 8.25 us -> 19.3 us  [the longest x1 4.66 us: per_device(): call(4.7, functools.partial(edge_kernel, grid_x, depth, inner, planes, fa...]
    dot_general x8 -> x0, matrix products: 10.5 us -> none  [the longest x2 4.28 us: line_tables(): jnp.einsum('zki,zkj->zij', lower, lower, precision=lax.Precision.HIGHEST)]
    unnamed x57 -> x20, local copies, waits for them, and re-layouts: 8.62 us -> 2.28 us
    all_to_all x1 -> x0, waiting for transfers between devices: 6.16 us -> none  [per_device(): lax.all_to_all(jnp.broadcast_to(packed[None], (everyone,) + packed.shape)...]
    all_gather x1 -> x0, blocking collectives: 5.19 us -> none  [per_device(): packed = lax.all_gather(packed, 'gx')]
  transfers between devices with their start and end apart: 9 -> 11, of which waited for: 7 -> 6; matrix products, arithmetic and copies ran while one was open for 20% -> 0% of each run, Pallas kernels for 4% -> 18%
where the time goes in v2:
time: 80.9 us; the launch traced here: 80.6 us
  waiting for transfers between devices  33 us (41%)
  starting transfers between devices  24.3 us (30%)
  Pallas kernels  19.3 us (24%)
  local copies, waits for them, and re-layouts  2.28 us (3%)
    ppermute x9, waiting for transfers between devices, turn(): return lax.ppermute(x, axis, [(i, (i + steps) % size) for i in range(size)])  17.8 us
    all_to_all x1, waiting for transfers between devices, per_device(): arrived_a = lax.all_to_all(packed_a, ('gx', 'x'), 0, 0, tiled=True)  15.3 us
    ppermute x9, starting transfers between devices, turn(): return lax.ppermute(x, axis, [(i, (i + steps) % size) for i in range(size)])  14.7 us
    all_to_all x1, starting transfers between devices, per_device(): arrived_b = lax.all_to_all(packed_b, ('gx', 'x'), 0, 0, tiled=True)  5.3 us
    pallas_call x1, Pallas kernels, per_device(): call(4.7, functools.partial(edge_kernel, grid_x, depth, inner, planes, fa...  4.66 us
    all_to_all x1, starting transfers between devices, per_device(): arrived_a = lax.all_to_all(packed_a, ('gx', 'x'), 0, 0, tiled=True)  4.31 us
    pallas_call x1, Pallas kernels, per_device(): call(3.9, functools.partial(near_kernel, capacity, depth), shapes + [arra...  3.85 us
    pallas_call x1, Pallas kernels, per_device(): call(2.7, functools.partial(start_kernel, capacity, columns, depth, inner...  2.66 us
  transfers between devices with their start and end apart: 11, of which 6 were waited for; matrix products, arithmetic and copies ran while one was open for 0% of the time, Pallas kernels for 18%

profile of v2, /device:TPU:0, one launch (start us, length us, event | category | flops | bytes accessed | tf_op | source)
XLA Modules:
  0.0 80.6 jit_solution(3716787591284158902)
XLA Ops:
  0.6 0.7 add_convert_fusion.routes
  1.4 1.0 %copy-done.3 = f32[4,256,128]{2,1,0:T(8,128)S(1)} copy-done((f32[4,256,128]{2,1,0:T(8,128)S(1)}, f32[4,256,128]{2,1,0:T(8,128)}, u32[]{:S(2)}) %copy-start.3) | copy-done | bytes 524312
  2.4 0.8 shard_map.86
  3.2 0.1 pad_add_fusion.at
  3.2 2.7 %shard_map.87.earlier = f32[8,104,512]{2,1,0:T(8,128)} custom-call(s32[3]{0:T(128)S(1)} %pad_add_fusion.at, f32[536,128]{1,0:T(8,128)S(1)} %get-tuple-element.22.ring.refs_0_, f32[512,128]{1,0:T(8,128)S(1)} %get-tuple-element.23.tiled), custom_call_target="tpu_custom_call" | custom-call | bytes 9963000 | tf_op jit(solution)/shard_map/pallas_call | solution.py:461
  5.9 5.3 %all-to-all-start.1 = ((f32[8,104,512]{2,1,0:T(8,128)}), f32[8,104,512]{2,1,0:T(8,128)S(1)}, u32[]{:S(2)}, u32[]{:S(2)}) async-start(f32[8,104,512]{2,1,0:T(8,128)} %shard_map.87.earlier), calls=%async_computation.1 | async-start | bytes 3407872 | tf_op jit(solution)/shard_map/all_to_all | solution.py:467
  11.2 1.6 %collective-permute-start = (f32[536,128]{1,0:T(8,128)S(1)}, f32[536,128]{1,0:T(8,128)S(1)}, u32[]{:S(2)}, u32[]{:S(2)}) collective-permute-start(f32[536,128]{1,0:T(8,128)S(1)} %get-tuple-element.22.ring.refs_0_), channel_id=1, source_target_pairs={{0,2},{2,4},{4,6},{6,0},{1,3},{3,5},{5,7},{7,1},{8,10},{10,12},{12... | collective-permute-start | bytes 823304 | tf_op jit(solution)/shard_map/ppermute | solution.py:454
  12.8 2.2 %collective-permute-start.2 = (f32[536,128]{1,0:T(8,128)S(1)}, f32[536,128]{1,0:T(8,128)S(1)}, u32[]{:S(2)}, u32[]{:S(2)}) collective-permute-start(f32[536,128]{1,0:T(8,128)S(1)} %get-tuple-element.22.ring.refs_0_), channel_id=1, source_target_pairs={{0,6},{2,0},{4,2},{6,4},{1,7},{3,1},{5,3},{7,5},{8,14},{10,8},{12,... | collective-permute-start | bytes 823304 | tf_op jit(solution)/shard_map/ppermute | solution.py:454
  15.1 7.4 %collective-permute-done.earlier.refs_1_ = f32[536,128]{1,0:T(8,128)S(1)} collective-permute-done((f32[536,128]{1,0:T(8,128)S(1)}, f32[536,128]{1,0:T(8,128)S(1)}, u32[]{:S(2)}, u32[]{:S(2)}) %collective-permute-start) | collective-permute-done | bytes 274464 | tf_op jit(solution)/shard_map/ppermute | solution.py:454
  22.5 1.2 %shard_map.88 = (f32[1024,256]{1,0:T(8,128)S(1)}, f32[4,8,256]{2,1,0:T(8,128)S(1)}, f32[7,8,128]{2,1,0:T(8,128)S(1)}, f32[8,256]{1,0:T(8,128)S(1)}, f32[8,128]{1...) custom-call(f32[4]{0:T(128)S(1)} %get-tuple-element.43.decay_in, ...), custom_call_target="tpu_custom_call" | custom-call | bytes 4428000 | tf_op jit(solution)/shard_map/pallas_call | solution.py:477
  23.7 0.0 copy-start.5
  23.7 3.7 %collective-permute-done.2.later.refs_3_ = f32[536,128]{1,0:T(8,128)S(1)} collective-permute-done((f32[536,128]{1,0:T(8,128)S(1)}, f32[536,128]{1,0:T(8,128)S(1)}, u32[]{:S(2)}, u32[]{:S(2)}) %collective-permute-start.2) | collective-permute-done | bytes 274464 | tf_op jit(solution)/shard_map/ppermute | solution.py:454
  27.4 4.7 %shard_map.89 = (f32[8,24,128]{2,1,0:T(8,128)S(1)}, f32[8,24,128]{2,1,0:T(8,128)S(1)}, f32[8,24,128]{2,1,0:T(8,128)S(1)}, f32[8,24,128]{2,1,0:T(8,128)S(1)}) custom-call(s32[3]{0:T(128)S(1)} %pad_add_fusion.at, f32[4]{0:T(128)S(1)} %get-tuple-element.42.logs_in, f32[4,256,128]{2,1,0:T(8,128)S(1)} %copy-done.1, f32[1024,256]{1,0:T(8,128)S(1)} %get-tuple-element.24.table, ...), custom_call_target="tpu_custom_call" | custom-call | bytes 17343000 | tf_op jit(solution)/shard_map/pallas_call | solution.py:487
  32.1 2.8 %collective-permute-start.3 = (f32[8,24,128]{2,1,0:T(8,128)S(1)}, f32[8,24,128]{2,1,0:T(8,128)S(1)}, u32[]{:S(2)}, u32[]{:S(2)}) collective-permute-start(f32[8,24,128]{2,1,0:T(8,128)S(1)} %get-tuple-element.29), channel_id=1, source_target_pairs={{0,2},{2,4},{4,6},{6,0},{1,3},{3,5},{5,7},{7,1},{8,10},{10,12},{12... | collective-permute-start | bytes 294920 | tf_op jit(solution)/shard_map/ppermute | solution.py:454
  34.8 1.2 %collective-permute-start.4 = (f32[8,24,128]{2,1,0:T(8,128)S(1)}, f32[8,24,128]{2,1,0:T(8,128)S(1)}, u32[]{:S(2)}, u32[]{:S(2)}) collective-permute-start(f32[8,24,128]{2,1,0:T(8,128)S(1)} %get-tuple-element.30), channel_id=1, source_target_pairs={{0,4},{2,6},{4,0},{6,2},{1,5},{3,7},{5,1},{7,3},{8,12},{10,14},{12... | collective-permute-start | bytes 294920 | tf_op jit(solution)/shard_map/ppermute | solution.py:454
  36.1 2.8 %collective-permute-start.5 = (f32[8,24,128]{2,1,0:T(8,128)S(1)}, f32[8,24,128]{2,1,0:T(8,128)S(1)}, u32[]{:S(2)}, u32[]{:S(2)}) collective-permute-start(f32[8,24,128]{2,1,0:T(8,128)S(1)} %get-tuple-element.31), channel_id=1, source_target_pairs={{0,6},{2,0},{4,2},{6,4},{1,7},{3,1},{5,3},{7,5},{8,14},{10,8},{12,... | collective-permute-start | bytes 294920 | tf_op jit(solution)/shard_map/ppermute | solution.py:454
  38.9 0.8 collective-permute-done.3.refs_5_
  39.7 3.0 %collective-permute-done.4.refs_6_ = f32[8,24,128]{2,1,0:T(8,128)S(1)} collective-permute-done((f32[8,24,128]{2,1,0:T(8,128)S(1)}, f32[8,24,128]{2,1,0:T(8,128)S(1)}, u32[]{:S(2)}, u32[]{:S(2)}) %collective-permute-start.4) | collective-permute-done | bytes 98336 | tf_op jit(solution)/shard_map/ppermute | solution.py:454
  42.7 1.8 %shard_map.90 = f32[8,104,512]{2,1,0:T(8,128)S(1)} custom-call(s32[3]{0:T(128)S(1)} %pad_add_fusion.at, f32[536,128]{1,0:T(8,128)S(1)} %get-tuple-element.22.ring.refs_0_, f32[536,128]{1,0:T(8,128)S(1)} %collective-permute-done.earlier.refs_1_, f32[536,128]{1,0:T(8,128)S(1)} %collective-permute-done.1.refs_2_, ...), custom_call_target="tpu_custom_call" | custom-call | bytes 7011000 | tf_op jit(solution)/shard_map/pallas_call | solution.py:494
  44.5 1.2 %copy-done = f32[8,104,512]{2,1,0:T(8,128)} copy-done((f32[8,104,512]{2,1,0:T(8,128)}, f32[8,104,512]{2,1,0:T(8,128)S(1)}, u32[]{:S(2)}) %copy-start) | copy-done | bytes 1703960
  45.7 4.3 %all-to-all-start = ((f32[8,104,512]{2,1,0:T(8,128)}), f32[8,104,512]{2,1,0:T(8,128)}, u32[]{:S(2)}, u32[]{:S(2)}) async-start(f32[8,104,512]{2,1,0:T(8,128)} %copy-done), calls=%async_computation | async-start | bytes 3407872 | tf_op jit(solution)/shard_map/all_to_all | solution.py:500
  50.0 0.0 copy-start.2
  50.0 0.0 copy-start.4
  50.0 1.4 %shard_map.93 = (f32[128,512]{1,0:T(8,128)S(1)}, f32[128,512]{1,0:T(8,128)}, f32[128,512]{1,0:T(8,128)}, f32[128,512]{1,0:T(8,128)S(1)}) custom-call(f32[8,104,512]{2,1,0:T(8,128)S(1)} %all-to-all-done.1.arrived), custom_call_target="tpu_custom_call" | custom-call | bytes 5166000 | tf_op jit(solution)/shard_map/pallas_call | solution.py:501
  51.4 3.4 %collective-permute-start.6 = (f32[128,512]{1,0:T(8,128)}, f32[128,512]{1,0:T(8,128)S(1)}, u32[]{:S(2)}, u32[]{:S(2)}) collective-permute-start(f32[128,512]{1,0:T(8,128)} %get-tuple-element.39), channel_id=1, source_target_pairs={{0,6},{2,0},{4,2},{6,4},{1,7},{3,1},{5,3},{7,5},{8,14},{10,8},{12,... | collective-permute-start | bytes 786440 | tf_op jit(solution)/shard_map/ppermute | solution.py:454
  54.8 0.4 collective-permute-start.7
  55.2 0.2 collective-permute-start.8
  55.4 1.3 %shard_map.91.base = f32[4,256,128]{2,1,0:T(8,128)S(1)} custom-call(f32[4,256,128]{2,1,0:T(8,128)S(1)} %copy-done.2, f32[4,256,128]{2,1,0:T(8,128)S(1)} %copy-done.4, f32[4,256,256]{2,1,0:T(8,128)S(1)} %get-tuple-element.27.both_x, f32[4,128,128]{2,1,0:T(8,128)S(1)} %get-tuple-element.32.both_y), custom_call_target="tpu_custom_call" | custom-call | bytes 4797000 | tf_op jit(solution)/shard_map/pallas_call | solution.py:503
  56.7 15.3 %all-to-all-done.arrived = f32[8,104,512]{2,1,0:T(8,128)} async-done(((f32[8,104,512]{2,1,0:T(8,128)}), f32[8,104,512]{2,1,0:T(8,128)}, u32[]{:S(2)}, u32[]{:S(2)}) %all-to-all-start) | async-done | bytes 1703968 | tf_op jit(solution)/shard_map/all_to_all | solution.py:500
  72.0 3.9 %shard_map.92 = (f32[4,256,128]{2,1,0:T(8,128)}, f32[4,256,128]{2,1,0:T(8,128)}, f32[2,256,128]{2,1,0:T(8,128)S(1)}) custom-call(f32[8,104,512]{2,1,0:T(8,128)} %all-to-all-done.arrived, f32[4,256,128]{2,1,0:T(8,128)S(1)} %shard_map.91.base, f32[4,256,256]{2,1,0:T(8,128)S(1)} %get-tuple-element.27.both_x, f32[4,128,128]{2,1,0:T(8,128)S(1)} %get-tuple-element.32.both_y, ...), custom_call_target="tpu_custom_call" | custom-call | bytes 14391000 | tf_op jit(solution)/shard_map/pallas_call | solution.py:507
  75.8 3.0 %collective-permute-done.7.refs_2_ = f32[128,512]{1,0:T(8,128)S(1)} collective-permute-done((f32[128,512]{1,0:T(8,128)}, f32[128,512]{1,0:T(8,128)S(1)}, u32[]{:S(2)}, u32[]{:S(2)}) %collective-permute-start.7) | collective-permute-done | bytes 262176 | tf_op jit(solution)/shard_map/ppermute | solution.py:454
  78.8 1.7 %shard_map.94 = (f32[4,256,128]{2,1,0:T(8,128)}, f32[4,256,128]{2,1,0:T(8,128)}) custom-call(f32[4,256,128]{2,1,0:T(8,128)} %get-tuple-element.35.pushed_in, f32[4,256,128]{2,1,0:T(8,128)} %get-tuple-element.36.next_in, f32[2,256,128]{2,1,0:T(8,128)S(1)} %get-tuple-element.37.base, ...), custom_call_target="tpu_custom_call", output_to_operand_aliasing={{0}: (0, {}), {1}: (1, {})} | custom-call | bytes 6273000 | tf_op jit(solution)/shard_map/pallas_call | solution.py:512
  (22 shorter events, 0.1 us)
Async XLA Ops:
  1.4 1.0 %copy-start.3 = (f32[4,256,128]{2,1,0:T(8,128)S(1)}, f32[4,256,128]{2,1,0:T(8,128)}, u32[]{:S(2)}) copy-start(f32[4,256,128]{2,1,0:T(8,128)} %source.1) | copy-start | bytes 1572868
  5.9 16.6 %copy-start.9 = (f32[4]{0:T(128)S(1)}, f32[4]{0:T(128)}, u32[]{:S(2)}) copy-start(f32[4]{0:T(128)} %param.13) | copy-start | bytes 52
  5.9 39.8 %all-to-all-start.1 = ((f32[8,104,512]{2,1,0:T(8,128)}), f32[8,104,512]{2,1,0:T(8,128)S(1)}, u32[]{:S(2)}, u32[]{:S(2)}) async-start(f32[8,104,512]{2,1,0:T(8,128)} %shard_map.87.earlier), calls=%async_computation.1 | async-start | bytes 3407872 | tf_op jit(solution)/shard_map/all_to_all | solution.py:467
  11.2 16.2 %copy-start.1 = (f32[4,256,128]{2,1,0:T(8,128)S(1)}, f32[4,256,128]{2,1,0:T(8,128)}, u32[]{:S(2)}) copy-start(f32[4,256,128]{2,1,0:T(8,128)} %target.3) | copy-start | bytes 1572868
  11.2 11.3 %collective-permute-start = (f32[536,128]{1,0:T(8,128)S(1)}, f32[536,128]{1,0:T(8,128)S(1)}, u32[]{:S(2)}, u32[]{:S(2)}) collective-permute-start(f32[536,128]{1,0:T(8,128)S(1)} %get-tuple-element.22.ring.refs_0_), channel_id=1, source_target_pairs={{0,2},{2,4},{4,6},{6,0},{1,3},{3,5},{5,7},{7,1},{8,10},{10,12},{12... | collective-permute-start | bytes 823304 | tf_op jit(solution)/shard_map/ppermute | solution.py:454
  12.8 14.5 %collective-permute-start.2 = (f32[536,128]{1,0:T(8,128)S(1)}, f32[536,128]{1,0:T(8,128)S(1)}, u32[]{:S(2)}, u32[]{:S(2)}) collective-permute-start(f32[536,128]{1,0:T(8,128)S(1)} %get-tuple-element.22.ring.refs_0_), channel_id=1, source_target_pairs={{0,6},{2,0},{4,2},{6,4},{1,7},{3,1},{5,3},{7,5},{8,14},{10,8},{12,... | collective-permute-start | bytes 823304 | tf_op jit(solution)/shard_map/ppermute | solution.py:454
  22.5 20.2 %collective-permute-start.1 = (f32[536,128]{1,0:T(8,128)S(1)}, f32[536,128]{1,0:T(8,128)S(1)}, u32[]{:S(2)}, u32[]{:S(2)}) collective-permute-start(f32[536,128]{1,0:T(8,128)S(1)} %collective-permute-done.earlier.refs_1_), channel_id=1, source_target_pairs={{0,2},{2,4},{4,6},{6,0},{1,3},{3,5},{5,7},{7,1},{8,10},{10,12},{12... | collective-permute-start | bytes 823304 | tf_op jit(solution)/shard_map/ppermute | solution.py:454
  23.7 8.4 %copy-start.5 = (f32[8,256]{1,0:T(8,128)}, f32[8,256]{1,0:T(8,128)S(1)}, u32[]{:S(2)}) copy-start(f32[8,256]{1,0:T(8,128)S(1)} %get-tuple-element.33.curve_x) | copy-start | bytes 24580
  23.7 8.3 %copy-start.7 = (f32[8,128]{1,0:T(8,128)}, f32[8,128]{1,0:T(8,128)S(1)}, u32[]{:S(2)}) copy-start(f32[8,128]{1,0:T(8,128)S(1)} %get-tuple-element.34.curve_y) | copy-start | bytes 12292
  32.1 7.6 %collective-permute-start.3 = (f32[8,24,128]{2,1,0:T(8,128)S(1)}, f32[8,24,128]{2,1,0:T(8,128)S(1)}, u32[]{:S(2)}, u32[]{:S(2)}) collective-permute-start(f32[8,24,128]{2,1,0:T(8,128)S(1)} %get-tuple-element.29), channel_id=1, source_target_pairs={{0,2},{2,4},{4,6},{6,0},{1,3},{3,5},{5,7},{7,1},{8,10},{10,12},{12... | collective-permute-start | bytes 294920 | tf_op jit(solution)/shard_map/ppermute | solution.py:454
  34.8 7.8 %collective-permute-start.4 = (f32[8,24,128]{2,1,0:T(8,128)S(1)}, f32[8,24,128]{2,1,0:T(8,128)S(1)}, u32[]{:S(2)}, u32[]{:S(2)}) collective-permute-start(f32[8,24,128]{2,1,0:T(8,128)S(1)} %get-tuple-element.30), channel_id=1, source_target_pairs={{0,4},{2,6},{4,0},{6,2},{1,5},{3,7},{5,1},{7,3},{8,12},{10,14},{12... | collective-permute-start | bytes 294920 | tf_op jit(solution)/shard_map/ppermute | solution.py:454
  36.1 6.6 %collective-permute-start.5 = (f32[8,24,128]{2,1,0:T(8,128)S(1)}, f32[8,24,128]{2,1,0:T(8,128)S(1)}, u32[]{:S(2)}, u32[]{:S(2)}) collective-permute-start(f32[8,24,128]{2,1,0:T(8,128)S(1)} %get-tuple-element.31), channel_id=1, source_target_pairs={{0,6},{2,0},{4,2},{6,4},{1,7},{3,1},{5,3},{7,5},{8,14},{10,8},{12,... | collective-permute-start | bytes 294920 | tf_op jit(solution)/shard_map/ppermute | solution.py:454
  44.5 1.2 %copy-start = (f32[8,104,512]{2,1,0:T(8,128)}, f32[8,104,512]{2,1,0:T(8,128)S(1)}, u32[]{:S(2)}) copy-start(f32[8,104,512]{2,1,0:T(8,128)S(1)} %shard_map.90) | copy-start | bytes 5111812
  45.7 26.3 %all-to-all-start = ((f32[8,104,512]{2,1,0:T(8,128)}), f32[8,104,512]{2,1,0:T(8,128)}, u32[]{:S(2)}, u32[]{:S(2)}) async-start(f32[8,104,512]{2,1,0:T(8,128)} %copy-done), calls=%async_computation | async-start | bytes 3407872 | tf_op jit(solution)/shard_map/all_to_all | solution.py:500
  50.0 5.4 %copy-start.2 = (f32[4,256,128]{2,1,0:T(8,128)S(1)}, f32[4,256,128]{2,1,0:T(8,128)}, u32[]{:S(2)}) copy-start(f32[4,256,128]{2,1,0:T(8,128)} %target.3) | copy-start | bytes 1572868
  50.0 5.4 %copy-start.4 = (f32[4,256,128]{2,1,0:T(8,128)S(1)}, f32[4,256,128]{2,1,0:T(8,128)}, u32[]{:S(2)}) copy-start(f32[4,256,128]{2,1,0:T(8,128)} %potential.1) | copy-start | bytes 1572868
  51.4 20.6 %copy-start.6 = (f32[8,256]{1,0:T(8,128)S(1)}, f32[8,256]{1,0:T(8,128)}, u32[]{:S(2)}) copy-start(f32[8,256]{1,0:T(8,128)} %copy-done.5) | copy-start | bytes 24580
  51.4 20.6 %copy-start.8 = (f32[8,128]{1,0:T(8,128)S(1)}, f32[8,128]{1,0:T(8,128)}, u32[]{:S(2)}) copy-start(f32[8,128]{1,0:T(8,128)} %copy-done.7) | copy-start | bytes 12292
  51.4 24.4 %collective-permute-start.6 = (f32[128,512]{1,0:T(8,128)}, f32[128,512]{1,0:T(8,128)S(1)}, u32[]{:S(2)}, u32[]{:S(2)}) collective-permute-start(f32[128,512]{1,0:T(8,128)} %get-tuple-element.39), channel_id=1, source_target_pairs={{0,6},{2,0},{4,2},{6,4},{1,7},{3,1},{5,3},{7,5},{8,14},{10,8},{12,... | collective-permute-start | bytes 786440 | tf_op jit(solution)/shard_map/ppermute | solution.py:454
  54.8 24.0 %collective-permute-start.7 = (f32[128,512]{1,0:T(8,128)}, f32[128,512]{1,0:T(8,128)S(1)}, u32[]{:S(2)}, u32[]{:S(2)}) collective-permute-start(f32[128,512]{1,0:T(8,128)} %get-tuple-element.40), channel_id=1, source_target_pairs={{0,4},{2,6},{4,0},{6,2},{1,5},{3,7},{5,1},{7,3},{8,12},{10,14},{12... | collective-permute-start | bytes 786440 | tf_op jit(solution)/shard_map/ppermute | solution.py:454
  55.2 23.6 %collective-permute-start.8 = (f32[128,512]{1,0:T(8,128)S(1)}, f32[128,512]{1,0:T(8,128)S(1)}, u32[]{:S(2)}, u32[]{:S(2)}) collective-permute-start(f32[128,512]{1,0:T(8,128)S(1)} %get-tuple-element.41), channel_id=1, source_target_pairs={{0,2},{2,4},{4,6},{6,0},{1,3},{3,5},{5,7},{7,1},{8,10},{10,12},{12... | collective-permute-start | bytes 786440 | tf_op jit(solution)/shard_map/ppermute | solution.py:454

commit v3 on v2

--- a/solution.py
+++ b/solution.py
@@ -9,11 +9,14 @@
 from jax.sharding import PartitionSpec as P
 
 TS = 16
+MXU = 256
 SUB = 8
 LANES = 128
 F32 = jnp.float32
 BF16 = jnp.bfloat16
-BYTES_A_MICRO = 3_690_000
+FLOPS_A_MICRO = 1_100_000_000
+COST = {'ring': 0.8, 'start': 2.5, 'table': 20, 'edge': 60, 'partial': 1.4, 'sum': 1.2, 'near': 3.5, 'far': 1.6, 'base': 1, 'pack': 1.8, 'early': 1.8}
+FLAG = {'edge': ('A1', 'packB'), 'table': ('ring',), 'rs2': True}
 VMEM_LIMIT = 48 * 1024 * 1024
 
 
@@ -30,10 +33,29 @@
     return lax.dot_general(a, b, (((0,), (0,)), ((), ())), preferred_element_type=F32)
 
 
+def beside(*parts):
+    return jnp.concatenate(parts, axis=1)
+
+
+def stacked(*parts):
+    return jnp.concatenate(parts, axis=0)
+
+
 def dot3(a, b):
     a_high, a_low = split(a)
     b_high, b_low = split(b)
-    return mm(a_high, b_high) + mm(a_high, b_low) + mm(a_low, b_high)
+    deep, wide = a.shape[1], b.shape[1]
+    if 2 * deep <= MXU and 2 * wide <= MXU:
+        both = mm(beside(a_high, a_low), stacked(beside(b_high, b_low), beside(b_high, jnp.zeros_like(b_low))))
+        return both[:, :wide] + both[:, wide:]
+    if 2 * wide <= MXU:
+        both = mm(a_high, beside(b_high, b_low))
+        return both[:, :wide] + both[:, wide:] + mm(a_low, b_high)
+    if 2 * deep <= MXU:
+        return mm(beside(a_high, a_low), stacked(b_high, b_high)) + mm(a_high, b_low)
+    rows = a.shape[0]
+    both = mm(stacked(a_high, a_low), b_high)
+    return both[:rows] + both[rows:] + mm(a_high, b_low)
 
 
 def swap_blocks(x):
@@ -157,29 +179,32 @@
     return [ring[first + k * SUB:first + k * SUB + fanout, :] for k in range(3)]
 
 
-def forward_kernel(capacity, columns, depth, inner, planes_a, fanout, at, *refs):
-    rings, edges, (pack_out, picked) = refs[:depth], refs[depth:-2], refs[-2:]
+def forward_kernel(capacity, columns, depth, inner, planes_a, fanout, count, at, *refs):
+    rings, edges, (pack_out, picked) = refs[:count], refs[count:-2], refs[-2:]
     half = rings[0].shape[0] - 3 * SUB
     tiles_x = half // planes_a // TS
     boards = [jnp.zeros((SUB, LANES), F32) for _ in range(columns)]
     wanted = columns_wanted((columns, LANES), depth, inner, at[1], 0)
-    for s in range(depth):
-        member, weight, label = route_rows(*routing(rings[s], fanout), wanted)
+    for s, ring in enumerate(rings):
+        member, weight, label = route_rows(*routing(ring, fanout), wanted)
         rank = ranked(member)
         for j in range(columns):
             rows, labels = slots_of(rank[j:j + 1], weight[j:j + 1], label[j:j + 1], capacity)
             picked[j * capacity:(j + 1) * capacity, :] = rows
             boards[j] = place_labels(boards[j], labels, s * (capacity // SUB))
-        packed = dot3(picked[...], tile_columns(rings[s][:half, :], planes_a, tiles_x))
+        packed = dot3(picked[...], tile_columns(ring[:half, :], planes_a, tiles_x))
         pack_out[:, s * capacity:(s + 1) * capacity, :] = packed.reshape(columns, capacity, packed.shape[1])
-    value = edges[0][...]
-    for part in edges[1:]:
-        value = value + part[...]
-    for i in range(value.shape[1] // SUB):
-        first = (1 + i) * LANES
-        pack_out[:, depth * capacity:, first:first + LANES] = value[:, i * SUB:(i + 1) * SUB, :]
+    if edges:
+        value = edges[0][...]
+        for part in edges[1:]:
+            value = value + part[...]
+        for i in range(value.shape[1] // SUB):
+            first = (1 + i) * LANES
+            pack_out[:, count * capacity:, first:first + LANES] = value[:, i * SUB:(i + 1) * SUB, :]
+    else:
+        pack_out[:, count * capacity:, :] = jnp.zeros((columns, SUB, pack_out.shape[2]), F32)
     for j in range(columns):
-        pack_out[j, depth * capacity:, :LANES] = boards[j]
+        pack_out[j, count * capacity:, :LANES] = boards[j]
 
 
 def gather_sum(arrived, capacity, groups):
@@ -217,15 +242,27 @@
         gap = (size - 1 - other if kind == 0 else other).astype(F32)
         for z in range(planes):
             value = weight * jnp.exp(gap * (TS * logs[z]))
-            left.append(
-                jnp.concatenate([jnp.where(here[n], value[n:n + 1], 0.0) for n in range(blocks)], axis=0)
-            )
+            left.append(stacked(*[jnp.where(here[n], value[n:n + 1], 0.0) for n in range(blocks)]))
             right.append(jnp.where(owner == kind * planes + z, proj, 0.0))
-    a_high, a_low = split(jnp.concatenate(left, axis=1))
-    b_high, b_low = split(jnp.concatenate(right, axis=0))
-    both = mm(a_high, jnp.concatenate([b_high, b_low], axis=1))
-    total = both[:, :LANES] + both[:, LANES:] + mm(a_low, b_high)
-    return total.reshape(blocks, per, LANES)
+    return dot3(beside(*left), stacked(*right)).reshape(blocks, per, LANES)
+
+
+def own_edges(proj, tiles_x, tiles_y, logs):
+    lane = lax.broadcasted_iota(jnp.int32, (SUB, LANES), 1) // TS
+    sub = lax.broadcasted_iota(jnp.int32, (SUB, LANES), 0)
+    planes = len(logs)
+    rate = jnp.zeros((SUB, LANES), F32)
+    for z in range(planes):
+        rate = jnp.where(lane % planes == z, TS * logs[z], rate)
+    to_end = lane < planes
+    near = jnp.exp(jnp.where(to_end, tiles_y - 1 - sub, sub).astype(F32) * rate)
+    along_x, along_y = jnp.zeros((SUB, LANES), F32), []
+    for i in range(tiles_x):
+        rows = proj[i * tiles_y:(i + 1) * tiles_y]
+        steps = jnp.where(to_end, tiles_x - 1 - i, i).astype(F32)
+        along_x = along_x + rows[:, :LANES] * jnp.exp(steps * rate)
+        along_y.append(jnp.sum(rows[:, LANES:] * near, axis=0, keepdims=True))
+    return along_x[None], stacked(*along_y)[None]
 
 
 def line_carries(ends, starts, across, first):
@@ -248,8 +285,7 @@
 
 
 def edge_kernel(grid_x, depth, inner, planes, fanout, at, logs_in, target, table, lines, coef, both_x, ring, tiled,
-                earlier, later, *refs):
-    del earlier, later
+                *refs):
     outs, carries = refs[:-1], refs[-1]
     _, cells_x, cells_y = target.shape
     tiles_x, tiles_y = cells_x // TS, cells_y // TS
@@ -258,23 +294,22 @@
     logs = [logs_in[z] for z in range(planes)]
     names, tiles, shares = routing(ring, fanout)
     cells = [tile_columns(ring[:half, :], planes_a, tiles_x), tile_columns(tiled[...], planes - planes_a, tiles_x)]
-    proj = dot3(jnp.concatenate(cells, axis=1), table[...])
-    cells = swap_blocks(target[...].reshape(planes * cells_x, LANES))
-    own = dot3(tile_columns(cells, planes, tiles_x), table[...])
+    cells = beside(*cells)
+    own_cells = tile_columns(swap_blocks(target[...].reshape(planes * cells_x, LANES)), planes, tiles_x)
+    proj = dot3(stacked(cells, own_cells), table[...])
+    own = own_edges(proj[cells.shape[0]:], tiles_x, tiles_y, logs)
+    proj = proj[:cells.shape[0]]
     tile_count = names.shape[1]
     along = depth * inner
     blocks = grid_x * along
     wanted = lax.broadcasted_iota(jnp.int32, (blocks, tile_count), 0).astype(F32)
     _, weight, label = route_rows(names, tiles, shares, wanted)
-    mine = lax.broadcasted_iota(jnp.int32, (1, tile_count), 1).astype(F32)
-    one = jnp.ones((1, tile_count), F32)
     here = at[0] * along + at[1] * inner + at[2]
     edges = []
     for part in range(2):
         sums = edge_sums(proj, weight, label, tiles_x, tiles_y, logs, part)
-        plus = edge_sums(own, one, mine, tiles_x, tiles_y, logs, part)
         is_here = lax.broadcasted_iota(jnp.int32, sums.shape, 0) == here
-        sums = jnp.where(is_here, plus, 0.0) - sums
+        sums = jnp.where(is_here, own[part], 0.0) - sums
         edges.append(swap_blocks(sums.reshape(-1, LANES)).reshape(blocks, sums.shape[1] // SUB, SUB, LANES))
     gain, across_x, first_x, back_x, across_y, first_y, back_y = [coef[i][:, :1] for i in range(7)]
 
@@ -325,7 +360,7 @@
 def outer(a, b):
     a_high, a_low = split(a)
     b_high, b_low = split(b)
-    return mm_t(a_high, b_high) + mm_t(a_high, b_low) + mm_t(a_low, b_high)
+    return mm_t(stacked(a_high, a_high, a_low), stacked(b_high, b_low, b_high))
 
 
 def base_kernel(target, potential, both_x, both_y, out):
@@ -337,7 +372,12 @@
     return before - dot3(dot3(both_x, pushed), both_y)
 
 
-def near_kernel(capacity, depth, arrived, base, both_x, both_y, curve_x, curve_y, pushed_out, next_out, rest_out):
+def sum_kernel(capacity, count, arrived, out):
+    out[...] = gather_sum(arrived, capacity, list(range(count)))
+
+
+def near_kernel(capacity, count, arrived, base, both_x, both_y, curve_x, curve_y, *refs):
+    earlier, (pushed_out, next_out, rest_out) = refs[:-3], refs[-3:]
     planes, planes_a = base.shape[0], pushed_out.shape[0]
     cells_x = pushed_out.shape[1]
     columns, rows, width = arrived.shape
@@ -345,7 +385,9 @@
     for j in range(1, columns):
         carries = carries + arrived[j, rows - SUB:, :]
     carry_x, carry_y = carries[:, LANES:2 * LANES], carries[:, 2 * LANES:2 * LANES + cells_x]
-    total = gather_sum(arrived, capacity, list(range(depth)))
+    total = gather_sum(arrived, capacity, list(range(count)))
+    for part in earlier:
+        total = total + part[...]
     pushed = swap_blocks(tile_rows(total, planes_a, cells_x // TS)).reshape(planes_a, cells_x, LANES)
     pushed_out[...] = pushed
     for z in range(planes):
@@ -371,21 +413,31 @@
         next_out[z] = solve(pushed[z], base[z], both_x[first + z], both_y[first + z])
 
 
-def call(micros, body, out_shape, in_specs=None, scratch=(), **extra):
-    if in_specs is not None:
-        extra["in_specs"] = in_specs
-    return pl.pallas_call(
-        body,
-        out_shape=out_shape,
-        scratch_shapes=list(scratch),
-        compiler_params=pltpu.CompilerParams(vmem_limit_bytes=VMEM_LIMIT),
-        cost_estimate=pl.CostEstimate(flops=0, bytes_accessed=int(micros * BYTES_A_MICRO), transcendentals=0),
-        **extra,
-    )
-
-
-def table_kernel(planes, decay_in, logs_in, earlier, table, lines, coef, curve_x, curve_y, both_x, both_y):
-    del earlier
+def call(name, body, out_shape, in_specs=None, scratch=(), wait=(), **extra):
+    def run(*args):
+        count, unread = len(args), len(wait)
+
+        def kernel(*refs):
+            body(*refs[:count], *refs[count + unread:])
+
+        near = pl.BlockSpec(memory_space=pltpu.VMEM)
+        specs = [near] * count if in_specs is None else list(in_specs)
+        return pl.pallas_call(
+            kernel,
+            out_shape=out_shape,
+            in_specs=specs + [pl.BlockSpec(memory_space=pl.ANY)] * unread,
+            scratch_shapes=list(scratch),
+            compiler_params=pltpu.CompilerParams(vmem_limit_bytes=VMEM_LIMIT),
+            cost_estimate=pl.CostEstimate(
+                flops=int(COST[name] * FLOPS_A_MICRO), bytes_accessed=0, transcendentals=0
+            ),
+            **extra,
+        )(*args, *wait)
+
+    return run
+
+
+def table_kernel(planes, decay_in, logs_in, table, lines, coef, curve_x, curve_y, both_x, both_y):
     row = lax.broadcasted_iota(jnp.int32, (2 * planes, LANES), 0)
     decay, rate = jnp.zeros(row.shape, F32), jnp.zeros(row.shape, F32)
     for z in range(planes):
@@ -455,62 +507,96 @@
 
     routes = jnp.stack([x.reshape(tile_count, fanout).T for x in (dest_device, dest_tile, mass_counts)])
     ring, tiled = call(
-        0.8, functools.partial(ring_kernel, planes_a),
+        "ring", functools.partial(ring_kernel, planes_a),
         [array(planes_a * cells_x + 3 * SUB, LANES), array(rest * cells_x, LANES)],
     )(source_mass, routes.astype(F32))
-    packed_b = call(
-        2.7, functools.partial(start_kernel, capacity, columns, depth, inner, planes_a, fanout),
-        array(columns, rows, rest * tile_cells),
-        [scalars] + [near] * 2,
-        [pltpu.VMEM((columns * depth * capacity, tile_count), F32)],
-    )(at, ring, tiled)
-    arrived_b = lax.all_to_all(packed_b, ("gx", "x"), 0, 0, tiled=True)
     rings = [ring] + [None] * (depth - 1)
     for s in range(1, depth // 2 + 1):
         rings[s] = turn(rings[s - 1], "z", 1)
         if s < depth - s:
             rings[depth - s] = turn(rings[(depth - s + 1) % depth], "z", -1)
-
+    have = {"A1": rings[1], "A3": rings[-1], "ring": ring}
+
+    def wait_of(name):
+        return [have[x] for x in FLAG.get(name, ())]
+
+    packed_b = call(
+        "start", functools.partial(start_kernel, capacity, columns, depth, inner, planes_a, fanout),
+        array(columns, rows, rest * tile_cells),
+        [scalars] + [near] * 2,
+        [pltpu.VMEM((columns * depth * capacity, tile_count), F32)],
+        wait_of("start"),
+    )(at, ring, tiled)
+    arrived_b = lax.all_to_all(packed_b, ("gx", "x"), 0, 0, tiled=True)
+    have["B"] = arrived_b
+    have["packB"] = packed_b
     decay = 1.0 - 1.0 / reach
     logs = jnp.log(decay)
     eight = 2 * planes
     table, lines, coef, curve_x, curve_y, both_x, both_y = call(
-        1.2, functools.partial(table_kernel, planes),
+        "table", functools.partial(table_kernel, planes),
         [
             array(planes * TS * TS, 4 * planes * TS), array(4, eight, cells_x), array(7, eight, LANES),
             array(eight, cells_x), array(eight, cells_y), array(planes, cells_x, cells_x),
             array(planes, cells_y, cells_y),
         ],
-        [scalars] * 2 + [far],
-    )(decay, logs, packed_b)
+        [scalars] * 2,
+        (),
+        wait_of("table"),
+    )(decay, logs)
     edge_rows = tiles_x + tiles_y
     edges = call(
-        4.7, functools.partial(edge_kernel, grid_x, depth, inner, planes, fanout),
+        "edge", functools.partial(edge_kernel, grid_x, depth, inner, planes, fanout),
         [array(columns, edge_rows, LANES)] * depth,
-        [scalars] * 2 + [near] * 7 + [far] * 2,
+        [scalars] * 2 + [near] * 7,
         [pltpu.VMEM((depth, columns, edge_rows, LANES), F32)],
-    )(at, logs, target_density, table, lines, coef, both_x, ring, tiled, rings[1], rings[-1])
+        wait_of("edge"),
+    )(at, logs, target_density, table, lines, coef, both_x, ring, tiled)
+    have["edge"] = edges[0]
     edges = [edges[0]] + [turn(edges[o], "z", o) for o in range(1, depth)]
-    packed_a = call(
-        1.9, functools.partial(forward_kernel, capacity, columns, depth, inner, planes_a, fanout),
-        array(columns, rows, planes_a * tile_cells),
-        [scalars] + [near] * (depth + len(edges)),
-        [pltpu.VMEM((columns * capacity, tile_count), F32)],
-    )(at, *rings, *edges)
-    arrived_a = lax.all_to_all(packed_a, ("gx", "x"), 0, 0, tiled=True)
-    sums = call(1.4, functools.partial(partial_kernel, capacity), [array(tile_count, rest * tile_cells)] * depth)(arrived_b)
-    moving = [sums[0]] + [turn(sums[r], "z", -r) for r in range(1, depth)]
-    base = call(1.3, base_kernel, array(*potential.shape))(target_density, potential, both_x, both_y)
+    sums = call(
+        "partial", functools.partial(partial_kernel, capacity), [array(tile_count, rest * tile_cells)] * depth,
+        None, (), wait_of("partial"),
+    )(arrived_b)
+    have["sums"] = sums[1]
+    if FLAG.get("rs2"):
+        moving = [sums[0], turn(sums[1] + turn(sums[2], "z", -1), "z", -1), turn(sums[3], "z", 1)]
+    else:
+        moving = [sums[0]] + [turn(sums[r], "z", -r) for r in range(1, depth)]
+    last = depth // 2
+    groups = [[s for s in range(depth) if s != last], [last]] if FLAG.get("split") else [list(range(depth))]
+    arrived_a = []
+    for group in groups:
+        more = edges if group is groups[-1] else []
+        rows = len(group) * capacity + SUB
+        name = "pack" if more else "early"
+        packed_a = call(
+            name,
+            functools.partial(forward_kernel, capacity, columns, depth, inner, planes_a, fanout, len(group)),
+            array(columns, rows, planes_a * tile_cells),
+            [scalars] + [near] * (len(group) + len(more)),
+            [pltpu.VMEM((columns * capacity, tile_count), F32)],
+            wait_of(name),
+        )(at, *[rings[s] for s in group], *more)
+        arrived_a.append(lax.all_to_all(packed_a, ("gx", "x"), 0, 0, tiled=True))
+    earlier = [
+        call("sum", functools.partial(sum_kernel, capacity, len(group)), array(tile_count, planes_a * tile_cells))(x)
+        for group, x in zip(groups[:-1], arrived_a)
+    ]
+    base = call("base", base_kernel, array(*potential.shape), None, (), wait_of("base"))(
+        target_density, potential, both_x, both_y
+    )
     field = (planes_a, cells_x, cells_y)
     shapes = [array(*source_mass.shape), array(*potential.shape)]
     part = pl.BlockSpec(field, lambda i: (0, 0, 0))
     *outs, base = call(
-        3.9, functools.partial(near_kernel, capacity, depth), shapes + [array(rest, cells_x, cells_y)], [near] * 6,
+        "near", functools.partial(near_kernel, capacity, len(groups[-1])),
+        shapes + [array(rest, cells_x, cells_y)], None,
         out_specs=[part, part, near], grid=(1,),
-    )(arrived_a, base, both_x, both_y, curve_x, curve_y)
+    )(arrived_a[-1], base, both_x, both_y, curve_x, curve_y, *earlier)
     part = pl.BlockSpec(field, lambda i: (1, 0, 0))
     outs = call(
-        1.7, functools.partial(far_kernel, planes_a), shapes, [far, far] + [near] * (3 + depth),
+        "far", functools.partial(far_kernel, planes_a), shapes, [far, far] + [near] * (3 + len(moving)),
         out_specs=[part, part], grid=(1,), input_output_aliases={0: 0, 1: 1},
     )(*outs, base, both_x, both_y, *moving)
     return tuple(outs)

time: 80.9 us -> 69 us (0.85)
  waiting for transfers between devices: 33 us -> 14.3 us
  starting transfers between devices: 24.3 us -> 29.5 us
  local copies, waits for them, and re-layouts: 2.28 us -> 4.48 us
  Pallas kernels: 19.3 us -> 18 us
    all_to_all x1, waiting for transfers between devices: 15.3 us -> 4.96 us  [per_device(): arrived_a.append(lax.all_to_all(packed_a, ('gx', 'x'), 0, 0, tiled=True))]
    ppermute x9, waiting for transfers between devices: 17.8 us -> 9.32 us  [turn(): return lax.ppermute(x, axis, [(i, (i + steps) % size) for i in range(size)])]
    ppermute x9, starting transfers between devices: 14.7 us -> 21.7 us  [turn(): return lax.ppermute(x, axis, [(i, (i + steps) % size) for i in range(size)])]
    unnamed x20 -> x30, local copies, waits for them, and re-layouts: 2.28 us -> 4.48 us
    pallas_call x9, Pallas kernels: 19.3 us -> 18 us  [run(): pl.pallas_call(kernel, out_shape=out_shape, in_specs=specs + [pl.BlockSpe...]
    all_to_all x1, starting transfers between devices: 5.3 us -> 4.01 us  [per_device(): arrived_b = lax.all_to_all(packed_b, ('gx', 'x'), 0, 0, tiled=True)]
  transfers between devices with their start and end apart: 11 -> 11, of which waited for: 6 -> 4; matrix products, arithmetic and copies ran while one was open for 0% -> 1% of each run, Pallas kernels for 18% -> 23%
where the time goes in v3:
time: 69 us; the launch traced here: 68.6 us
  starting transfers between devices  29.5 us (43%)
  Pallas kernels  18 us (26%)
  waiting for transfers between devices  14.3 us (21%)
  local copies, waits for them, and re-layouts  4.48 us (6%)
  other arithmetic  1.54 us (2%)
  between operations  0.79 us (1%)
    ppermute x9, starting transfers between devices, turn(): return lax.ppermute(x, axis, [(i, (i + steps) % size) for i in range(size)])  21.7 us
    pallas_call x9, Pallas kernels, run(): pl.pallas_call(kernel, out_shape=out_shape, in_specs=specs + [pl.BlockSpe...  18 us
    ppermute x9, waiting for transfers between devices, turn(): return lax.ppermute(x, axis, [(i, (i + steps) % size) for i in range(size)])  9.32 us
    all_to_all x1, waiting for transfers between devices, per_device(): arrived_a.append(lax.all_to_all(packed_a, ('gx', 'x'), 0, 0, tiled=True))  4.96 us
    unnamed x30, local copies, waits for them, and re-layouts  4.48 us
    all_to_all x1, starting transfers between devices, per_device(): arrived_b = lax.all_to_all(packed_b, ('gx', 'x'), 0, 0, tiled=True)  4.01 us
    all_to_all x1, starting transfers between devices, per_device(): arrived_a.append(lax.all_to_all(packed_a, ('gx', 'x'), 0, 0, tiled=True))  3.84 us
  transfers between devices with their start and end apart: 11, of which 4 were waited for; matrix products, arithmetic and copies ran while one was open for 1% of the time, Pallas kernels for 23%

profile of v3, /device:TPU:0, one launch (start us, length us, event | category | flops | bytes accessed | tf_op | source)
XLA Modules:
  0.0 68.6 jit_solution(7183155276239046726)
XLA Ops:
  0.6 0.7 %add_convert_fusion.refs_1_ = f32[3,4,128]{2,1,0:T(4,128)S(1)} fusion(s32[1,4,128]{2,1,0:T(4,128)} %bitcast.18, s32[1,4,128]{2,1,0:T(4,128)} %bitcast.19, s32[1,4,128]{2,1,0:T(4,128)} %bitcast.20), kind=kLoop, calls=%fused_computation | loop fusion | flops 4608 | bytes 12288 | tf_op jit(solution)/shard_map/convert_element_type | solution.py:512
  1.4 1.0 %copy-done = f32[4,256,128]{2,1,0:T(8,128)S(1)} copy-done((f32[4,256,128]{2,1,0:T(8,128)S(1)}, f32[4,256,128]{2,1,0:T(8,128)}, u32[]{:S(2)}) %copy-start) | copy-done | bytes 524312
  2.4 0.8 %shard_map.86 = (f32[536,128]{1,0:T(8,128)S(1)}, f32[512,128]{1,0:T(8,128)S(1)}) custom-call(f32[4,256,128]{2,1,0:T(8,128)S(1)} %copy-done, f32[3,4,128]{2,1,0:T(4,128)S(1)} %add_convert_fusion.refs_1_), custom_call_target="tpu_custom_call" | custom-call | flops 880000000 | tf_op jit(solution)/shard_map/pallas_call | solution.py:425
  3.1 3.1 %collective-permute-start = (f32[536,128]{1,0:T(8,128)S(1)}, f32[536,128]{1,0:T(8,128)S(1)}, u32[]{:S(2)}, u32[]{:S(2)}) collective-permute-start(f32[536,128]{1,0:T(8,128)S(1)} %get-tuple-element.22.refs_2_.refs_1_.refs_7_), channel_id=1, source_target_pairs={{0,2},{2,4},{4,6},{6,0},{1,3},{3,5},{5,7},{7,1},{8,10},{10,12},{12... | collective-permute-start | bytes 823304 | tf_op jit(solution)/shard_map/ppermute | solution.py:506
  6.2 2.1 %collective-permute-start.2 = (f32[536,128]{1,0:T(8,128)S(1)}, f32[536,128]{1,0:T(8,128)S(1)}, u32[]{:S(2)}, u32[]{:S(2)}) collective-permute-start(f32[536,128]{1,0:T(8,128)S(1)} %get-tuple-element.22.refs_2_.refs_1_.refs_7_), channel_id=1, source_target_pairs={{0,6},{2,0},{4,2},{6,4},{1,7},{3,1},{5,3},{7,5},{8,14},{10,8},{12,... | collective-permute-start | bytes 823304 | tf_op jit(solution)/shard_map/ppermute | solution.py:506
  8.3 0.1 pad_add_fusion.refs_0_
  8.4 2.4 %shard_map.88.refs_10_ = f32[8,104,512]{2,1,0:T(8,128)} custom-call(s32[3]{0:T(128)S(1)} %pad_add_fusion.refs_0_, f32[536,128]{1,0:T(8,128)S(1)} %get-tuple-element.22.refs_2_.refs_1_.refs_7_, f32[512,128]{1,0:T(8,128)S(1)} %get-tuple-element.27.refs_2_.refs_8_), custom_call_target="tpu_custom_call" | custom-call | flops 2750000128 | tf_op jit(solution)/shard_map/pallas_call | solution.py:425
  10.8 4.0 %all-to-all-start.1 = ((f32[8,104,512]{2,1,0:T(8,128)}), f32[8,104,512]{2,1,0:T(8,128)S(1)}, u32[]{:S(2)}, u32[]{:S(2)}) async-start(f32[8,104,512]{2,1,0:T(8,128)} %shard_map.88.refs_10_), calls=%async_computation.1 | async-start | bytes 3407872 | tf_op jit(solution)/shard_map/all_to_all | solution.py:530
  14.9 0.0 copy-start.1
  14.9 1.2 %shard_map.87 = (f32[1024,256]{1,0:T(8,128)S(1)}, f32[4,8,256]{2,1,0:T(8,128)S(1)}, f32[7,8,128]{2,1,0:T(8,128)S(1)}, f32[8,256]{1,0:T(8,128)S(1)}, f32[8,128]{1...) custom-call(f32[4]{0:T(128)S(1)} %get-tuple-element.43.refs_0_, f32[4]{0:T(128)S(1)} %get-tuple-element.42.refs_1_, ...), custom_call_target="tpu_custom_call" | custom-call | flops 22000001024 | tf_op jit(solution)/shard_map/pallas_call | solution.py:425
  16.1 0.7 %copy-done.9 = f32[4,128,128]{2,1,0:T(8,128)} copy-done((f32[4,128,128]{2,1,0:T(8,128)}, f32[4,128,128]{2,1,0:T(8,128)S(1)}, u32[]{:S(2)}) %copy-start.9) | copy-done | bytes 262168
  16.8 4.4 %shard_map.89 = (f32[8,24,128]{2,1,0:T(8,128)S(1)}, f32[8,24,128]{2,1,0:T(8,128)S(1)}, f32[8,24,128]{2,1,0:T(8,128)S(1)}, f32[8,24,128]{2,1,0:T(8,128)S(1)}) custom-call(s32[3]{0:T(128)S(1)} %pad_add_fusion.refs_0_, f32[4]{0:T(128)S(1)} %get-tuple-element.42.refs_1_, f32[4,256,128]{2,1,0:T(8,128)S(1)} %copy-done.1, ...), custom_call_target="tpu_custom_call" | custom-call | flops 65999998976 | tf_op jit(solution)/shard_map/pallas_call | solution.py:425
  21.2 5.1 %collective-permute-start.3 = (f32[8,24,128]{2,1,0:T(8,128)S(1)}, f32[8,24,128]{2,1,0:T(8,128)S(1)}, u32[]{:S(2)}, u32[]{:S(2)}) collective-permute-start(f32[8,24,128]{2,1,0:T(8,128)S(1)} %get-tuple-element.29), channel_id=1, source_target_pairs={{0,2},{2,4},{4,6},{6,0},{1,3},{3,5},{5,7},{7,1},{8,10},{10,12},{12... | collective-permute-start | bytes 294920 | tf_op jit(solution)/shard_map/ppermute | solution.py:506
  26.3 1.2 %collective-permute-start.4 = (f32[8,24,128]{2,1,0:T(8,128)S(1)}, f32[8,24,128]{2,1,0:T(8,128)S(1)}, u32[]{:S(2)}, u32[]{:S(2)}) collective-permute-start(f32[8,24,128]{2,1,0:T(8,128)S(1)} %get-tuple-element.30), channel_id=1, source_target_pairs={{0,4},{2,6},{4,0},{6,2},{1,5},{3,7},{5,1},{7,3},{8,12},{10,14},{12... | collective-permute-start | bytes 294920 | tf_op jit(solution)/shard_map/ppermute | solution.py:506
  27.5 2.8 %collective-permute-start.5 = (f32[8,24,128]{2,1,0:T(8,128)S(1)}, f32[8,24,128]{2,1,0:T(8,128)S(1)}, u32[]{:S(2)}, u32[]{:S(2)}) collective-permute-start(f32[8,24,128]{2,1,0:T(8,128)S(1)} %get-tuple-element.31), channel_id=1, source_target_pairs={{0,6},{2,0},{4,2},{6,4},{1,7},{3,1},{5,3},{7,5},{8,14},{10,8},{12,... | collective-permute-start | bytes 294920 | tf_op jit(solution)/shard_map/ppermute | solution.py:506
  30.4 0.7 collective-permute-done.3.refs_6_
  31.0 3.0 %collective-permute-done.4.refs_7_ = f32[8,24,128]{2,1,0:T(8,128)S(1)} collective-permute-done((f32[8,24,128]{2,1,0:T(8,128)S(1)}, f32[8,24,128]{2,1,0:T(8,128)S(1)}, u32[]{:S(2)}, u32[]{:S(2)}) %collective-permute-start.4) | collective-permute-done | bytes 98336 | tf_op jit(solution)/shard_map/ppermute | solution.py:506
  34.1 2.9 %shard_map.90 = f32[8,104,512]{2,1,0:T(8,128)} custom-call(s32[3]{0:T(128)S(1)} %pad_add_fusion.refs_0_, f32[536,128]{1,0:T(8,128)S(1)} %get-tuple-element.22.refs_2_.refs_1_.refs_7_, f32[536,128]{1,0:T(8,128)S(1)} %collective-permute-done.refs_9_.refs_2_, f32[536,128]{1,0:T(8,128)S(1)} %collective-permute-done.1.refs_3_, ...), custom_call_target="tpu_custom_call" | custom-call | flops 1980000000 | tf_op jit(solution)/shard_map/pallas_call | solution.py:425
  37.0 3.8 %all-to-all-start = ((f32[8,104,512]{2,1,0:T(8,128)}), f32[8,104,512]{2,1,0:T(8,128)S(1)}, u32[]{:S(2)}, u32[]{:S(2)}) async-start(f32[8,104,512]{2,1,0:T(8,128)} %shard_map.90), calls=%async_computation | async-start | bytes 3407872 | tf_op jit(solution)/shard_map/all_to_all | solution.py:581
  40.8 1.5 %shard_map.93 = (f32[128,512]{1,0:T(8,128)S(1)}, f32[128,512]{1,0:T(8,128)S(1)}, f32[128,512]{1,0:T(8,128)S(1)}, f32[128,512]{1,0:T(8,128)}) custom-call(f32[8,104,512]{2,1,0:T(8,128)S(1)} %all-to-all-done.1.refs_0_), custom_call_target="tpu_custom_call" | custom-call | flops 1540000000 | tf_op jit(solution)/shard_map/pallas_call | solution.py:425
  42.3 0.7 %copy-done.12 = f32[128,512]{1,0:T(8,128)} copy-done((f32[128,512]{1,0:T(8,128)}, f32[128,512]{1,0:T(8,128)S(1)}, u32[]{:S(2)}) %copy-start.12) | copy-done | bytes 262168
  43.0 3.0 %collective-permute-start.6 = (f32[128,512]{1,0:T(8,128)S(1)}, f32[128,512]{1,0:T(8,128)S(1)}, u32[]{:S(2)}, u32[]{:S(2)}) collective-permute-start(f32[128,512]{1,0:T(8,128)S(1)} %get-tuple-element.40), channel_id=1, source_target_pairs={{0,6},{2,0},{4,2},{6,4},{1,7},{3,1},{5,3},{7,5},{8,14},{10,8},{12,... | collective-permute-start | bytes 786440 | tf_op jit(solution)/shard_map/ppermute | solution.py:506
  46.1 1.0 %shard_map.91.refs_1_ = f32[4,256,128]{2,1,0:T(8,128)S(1)} custom-call(f32[4,256,128]{2,1,0:T(8,128)S(1)} %copy-done.2, f32[4,256,128]{2,1,0:T(8,128)S(1)} %copy-done.3, f32[4,256,256]{2,1,0:T(8,128)S(1)} %copy-done.5, f32[4,128,128]{2,1,0:T(8,128)S(1)} %copy-done.10), custom_call_target="tpu_custom_call" | custom-call | flops 1100000000 | tf_op jit(solution)/shard_map/pallas_call | solution.py:425
  47.1 0.1 collective-permute-start.8
  47.2 5.6 %collective-permute-done.6 = f32[128,512]{1,0:T(8,128)S(1)} collective-permute-done((f32[128,512]{1,0:T(8,128)S(1)}, f32[128,512]{1,0:T(8,128)S(1)}, u32[]{:S(2)}, u32[]{:S(2)}) %collective-permute-start.6) | collective-permute-done | bytes 262176 | tf_op jit(solution)/shard_map/ppermute | solution.py:506
  52.8 0.7 %add.3 = f32[128,512]{1,0:T(8,128)} add(f32[128,512]{1,0:T(8,128)S(1)} %get-tuple-element.39, f32[128,512]{1,0:T(8,128)S(1)} %collective-permute-done.6) | non-fusion elementwise | flops 65536 | bytes 786432 | tf_op jit(solution)/shard_map/add | solution.py:563
  53.5 4.3 %collective-permute-start.7 = (f32[128,512]{1,0:T(8,128)}, f32[128,512]{1,0:T(8,128)S(1)}, u32[]{:S(2)}, u32[]{:S(2)}) collective-permute-start(f32[128,512]{1,0:T(8,128)} %add.3), channel_id=1, source_target_pairs={{0,6},{2,0},{4,2},{6,4},{1,7},{3,1},{5,3},{7,5},{8,14},{10,8},{12,... | collective-permute-start | bytes 786440 | tf_op jit(solution)/shard_map/ppermute | solution.py:506
  57.8 5.0 %all-to-all-done.refs_0_ = f32[8,104,512]{2,1,0:T(8,128)S(1)} async-done(((f32[8,104,512]{2,1,0:T(8,128)}), f32[8,104,512]{2,1,0:T(8,128)S(1)}, u32[]{:S(2)}, u32[]{:S(2)}) %all-to-all-start) | async-done | bytes 1703968 | tf_op jit(solution)/shard_map/all_to_all | solution.py:581
  62.8 1.0 %copy-done.8 = f32[4,256,128]{2,1,0:T(8,128)S(1)} copy-done((f32[4,256,128]{2,1,0:T(8,128)S(1)}, f32[4,256,128]{2,1,0:T(8,128)}, u32[]{:S(2)}) %copy-start.8) | copy-done | bytes 524312
  63.8 0.9 %copy-done.11 = f32[4,128,128]{2,1,0:T(8,128)S(1)} copy-done((f32[4,128,128]{2,1,0:T(8,128)S(1)}, f32[4,128,128]{2,1,0:T(8,128)}, u32[]{:S(2)}) %copy-start.11) | copy-done | bytes 262168
  64.7 2.2 %shard_map.92 = (f32[4,256,128]{2,1,0:T(8,128)}, f32[4,256,128]{2,1,0:T(8,128)}, f32[2,256,128]{2,1,0:T(8,128)S(1)}) custom-call(f32[8,104,512]{2,1,0:T(8,128)S(1)} %all-to-all-done.refs_0_, f32[4,256,128]{2,1,0:T(8,128)S(1)} %copy-done.8, f32[4,256,256]{2,1,0:T(8,128)S(1)} %copy-done.6, f32[4,128,128]{2,1,0:T(8,128)S(1)} %copy-done.11, ...), custom_call_target="tpu_custom_call" | custom-call | flops 3849999872 | tf_op jit(solution)/shard_map/pallas_call | solution.py:425
  67.0 1.6 %shard_map.94 = (f32[4,256,128]{2,1,0:T(8,128)}, f32[4,256,128]{2,1,0:T(8,128)}) custom-call(f32[4,256,128]{2,1,0:T(8,128)} %get-tuple-element.35.refs_0_, f32[4,256,128]{2,1,0:T(8,128)} %get-tuple-element.36.refs_1_, f32[2,256,128]{2,1,0:T(8,128)S(1)} %get-tuple-element.37.refs_2_, ...), custom_call_target="tpu_custom_call", output_to_operand_aliasing={{0}: (0, {}), {1}: (1, {})} | custom-call | flops 1760000000 | tf_op jit(solution)/shard_map/pallas_call | solution.py:425
  (33 shorter events, 0.1 us)
Async XLA Ops:
  1.3 1.0 %copy-start = (f32[4,256,128]{2,1,0:T(8,128)S(1)}, f32[4,256,128]{2,1,0:T(8,128)}, u32[]{:S(2)}) copy-start(f32[4,256,128]{2,1,0:T(8,128)} %refs_0_.2) | copy-start | bytes 1572868
  3.1 13.6 %collective-permute-start = (f32[536,128]{1,0:T(8,128)S(1)}, f32[536,128]{1,0:T(8,128)S(1)}, u32[]{:S(2)}, u32[]{:S(2)}) collective-permute-start(f32[536,128]{1,0:T(8,128)S(1)} %get-tuple-element.22.refs_2_.refs_1_.refs_7_), channel_id=1, source_target_pairs={{0,2},{2,4},{4,6},{6,0},{1,3},{3,5},{5,7},{7,1},{8,10},{10,12},{12... | collective-permute-start | bytes 823304 | tf_op jit(solution)/shard_map/ppermute | solution.py:506
  6.2 24.1 %collective-permute-start.2 = (f32[536,128]{1,0:T(8,128)S(1)}, f32[536,128]{1,0:T(8,128)S(1)}, u32[]{:S(2)}, u32[]{:S(2)}) collective-permute-start(f32[536,128]{1,0:T(8,128)S(1)} %get-tuple-element.22.refs_2_.refs_1_.refs_7_), channel_id=1, source_target_pairs={{0,6},{2,0},{4,2},{6,4},{1,7},{3,1},{5,3},{7,5},{8,14},{10,8},{12,... | collective-permute-start | bytes 823304 | tf_op jit(solution)/shard_map/ppermute | solution.py:506
  10.8 4.0 %copy-start.14 = (f32[4]{0:T(128)S(1)}, f32[4]{0:T(128)}, u32[]{:S(2)}) copy-start(f32[4]{0:T(128)} %param.13) | copy-start | bytes 52
  10.8 26.1 %all-to-all-start.1 = ((f32[8,104,512]{2,1,0:T(8,128)}), f32[8,104,512]{2,1,0:T(8,128)S(1)}, u32[]{:S(2)}, u32[]{:S(2)}) async-start(f32[8,104,512]{2,1,0:T(8,128)} %shard_map.88.refs_10_), calls=%async_computation.1 | async-start | bytes 3407872 | tf_op jit(solution)/shard_map/all_to_all | solution.py:530
  14.9 1.9 %copy-start.1 = (f32[4,256,128]{2,1,0:T(8,128)S(1)}, f32[4,256,128]{2,1,0:T(8,128)}, u32[]{:S(2)}) copy-start(f32[4,256,128]{2,1,0:T(8,128)} %refs_0_.3) | copy-start | bytes 1572868
  16.1 0.7 %copy-start.9 = (f32[4,128,128]{2,1,0:T(8,128)}, f32[4,128,128]{2,1,0:T(8,128)S(1)}, u32[]{:S(2)}) copy-start(f32[4,128,128]{2,1,0:T(8,128)S(1)} %get-tuple-element.32.refs_3_.refs_4_) | copy-start | bytes 786436
  16.8 4.4 %copy-start.4 = (f32[4,256,256]{2,1,0:T(8,128)}, f32[4,256,256]{2,1,0:T(8,128)S(1)}, u32[]{:S(2)}) copy-start(f32[4,256,256]{2,1,0:T(8,128)S(1)} %get-tuple-element.26.refs_6_.refs_2_.refs_3_) | copy-start | bytes 3145732
  16.8 17.3 %collective-permute-start.1 = (f32[536,128]{1,0:T(8,128)S(1)}, f32[536,128]{1,0:T(8,128)S(1)}, u32[]{:S(2)}, u32[]{:S(2)}) collective-permute-start(f32[536,128]{1,0:T(8,128)S(1)} %collective-permute-done.refs_9_.refs_2_), channel_id=1, source_target_pairs={{0,2},{2,4},{4,6},{6,0},{1,3},{3,5},{5,7},{7,1},{8,10},{10,12},{12... | collective-permute-start | bytes 823304 | tf_op jit(solution)/shard_map/ppermute | solution.py:506
  21.2 9.8 %collective-permute-start.3 = (f32[8,24,128]{2,1,0:T(8,128)S(1)}, f32[8,24,128]{2,1,0:T(8,128)S(1)}, u32[]{:S(2)}, u32[]{:S(2)}) collective-permute-start(f32[8,24,128]{2,1,0:T(8,128)S(1)} %get-tuple-element.29), channel_id=1, source_target_pairs={{0,2},{2,4},{4,6},{6,0},{1,3},{3,5},{5,7},{7,1},{8,10},{10,12},{12... | collective-permute-start | bytes 294920 | tf_op jit(solution)/shard_map/ppermute | solution.py:506
  26.3 7.8 %collective-permute-start.4 = (f32[8,24,128]{2,1,0:T(8,128)S(1)}, f32[8,24,128]{2,1,0:T(8,128)S(1)}, u32[]{:S(2)}, u32[]{:S(2)}) collective-permute-start(f32[8,24,128]{2,1,0:T(8,128)S(1)} %get-tuple-element.30), channel_id=1, source_target_pairs={{0,4},{2,6},{4,0},{6,2},{1,5},{3,7},{5,1},{7,3},{8,12},{10,14},{12... | collective-permute-start | bytes 294920 | tf_op jit(solution)/shard_map/ppermute | solution.py:506
  27.5 6.5 %collective-permute-start.5 = (f32[8,24,128]{2,1,0:T(8,128)S(1)}, f32[8,24,128]{2,1,0:T(8,128)S(1)}, u32[]{:S(2)}, u32[]{:S(2)}) collective-permute-start(f32[8,24,128]{2,1,0:T(8,128)S(1)} %get-tuple-element.31), channel_id=1, source_target_pairs={{0,6},{2,0},{4,2},{6,4},{1,7},{3,1},{5,3},{7,5},{8,14},{10,8},{12,... | collective-permute-start | bytes 294920 | tf_op jit(solution)/shard_map/ppermute | solution.py:506
  37.0 25.8 %all-to-all-start = ((f32[8,104,512]{2,1,0:T(8,128)}), f32[8,104,512]{2,1,0:T(8,128)S(1)}, u32[]{:S(2)}, u32[]{:S(2)}) async-start(f32[8,104,512]{2,1,0:T(8,128)} %shard_map.90), calls=%async_computation | async-start | bytes 3407872 | tf_op jit(solution)/shard_map/all_to_all | solution.py:581
  40.8 5.3 %copy-start.2 = (f32[4,256,128]{2,1,0:T(8,128)S(1)}, f32[4,256,128]{2,1,0:T(8,128)}, u32[]{:S(2)}) copy-start(f32[4,256,128]{2,1,0:T(8,128)} %refs_0_.3) | copy-start | bytes 1572868
  40.8 5.3 %copy-start.3 = (f32[4,256,128]{2,1,0:T(8,128)S(1)}, f32[4,256,128]{2,1,0:T(8,128)}, u32[]{:S(2)}) copy-start(f32[4,256,128]{2,1,0:T(8,128)} %refs_1_.1) | copy-start | bytes 1572868
  40.8 5.2 %copy-start.5 = (f32[4,256,256]{2,1,0:T(8,128)S(1)}, f32[4,256,256]{2,1,0:T(8,128)}, u32[]{:S(2)}) copy-start(f32[4,256,256]{2,1,0:T(8,128)} %copy-done.4) | copy-start | bytes 3145732
  40.8 5.2 %copy-start.10 = (f32[4,128,128]{2,1,0:T(8,128)S(1)}, f32[4,128,128]{2,1,0:T(8,128)}, u32[]{:S(2)}) copy-start(f32[4,128,128]{2,1,0:T(8,128)} %copy-done.9) | copy-start | bytes 786436
  42.3 0.7 %copy-start.12 = (f32[128,512]{1,0:T(8,128)}, f32[128,512]{1,0:T(8,128)S(1)}, u32[]{:S(2)}) copy-start(f32[128,512]{1,0:T(8,128)S(1)} %get-tuple-element.38.refs_5_) | copy-start | bytes 786436
  43.0 9.7 %collective-permute-start.6 = (f32[128,512]{1,0:T(8,128)S(1)}, f32[128,512]{1,0:T(8,128)S(1)}, u32[]{:S(2)}, u32[]{:S(2)}) collective-permute-start(f32[128,512]{1,0:T(8,128)S(1)} %get-tuple-element.40), channel_id=1, source_target_pairs={{0,6},{2,0},{4,2},{6,4},{1,7},{3,1},{5,3},{7,5},{8,14},{10,8},{12,... | collective-permute-start | bytes 786440 | tf_op jit(solution)/shard_map/ppermute | solution.py:506
  46.1 16.7 %copy-start.6 = (f32[4,256,256]{2,1,0:T(8,128)S(1)}, f32[4,256,256]{2,1,0:T(8,128)}, u32[]{:S(2)}) copy-start(f32[4,256,256]{2,1,0:T(8,128)} %copy-done.4) | copy-start | bytes 3145732
  47.1 6.4 %copy-start.7 = (f32[4,256,128]{2,1,0:T(8,128)}, f32[4,256,128]{2,1,0:T(8,128)S(1)}, u32[]{:S(2)}) copy-start(f32[4,256,128]{2,1,0:T(8,128)S(1)} %shard_map.91.refs_1_) | copy-start | bytes 1572868
  47.1 19.9 %collective-permute-start.8 = (f32[128,512]{1,0:T(8,128)}, f32[128,512]{1,0:T(8,128)S(1)}, u32[]{:S(2)}, u32[]{:S(2)}) collective-permute-start(f32[128,512]{1,0:T(8,128)} %get-tuple-element.41), channel_id=1, source_target_pairs={{0,2},{2,4},{4,6},{6,0},{1,3},{3,5},{5,7},{7,1},{8,10},{10,12},{12... | collective-permute-start | bytes 786440 | tf_op jit(solution)/shard_map/ppermute | solution.py:506
  53.5 13.5 %collective-permute-start.7 = (f32[128,512]{1,0:T(8,128)}, f32[128,512]{1,0:T(8,128)S(1)}, u32[]{:S(2)}, u32[]{:S(2)}) collective-permute-start(f32[128,512]{1,0:T(8,128)} %add.3), channel_id=1, source_target_pairs={{0,6},{2,0},{4,2},{6,4},{1,7},{3,1},{5,3},{7,5},{8,14},{10,8},{12,... | collective-permute-start | bytes 786440 | tf_op jit(solution)/shard_map/ppermute | solution.py:506
  62.8 1.0 %copy-start.8 = (f32[4,256,128]{2,1,0:T(8,128)S(1)}, f32[4,256,128]{2,1,0:T(8,128)}, u32[]{:S(2)}) copy-start(f32[4,256,128]{2,1,0:T(8,128)} %copy-done.7) | copy-start | bytes 1572868
  63.8 0.9 %copy-start.11 = (f32[4,128,128]{2,1,0:T(8,128)S(1)}, f32[4,128,128]{2,1,0:T(8,128)}, u32[]{:S(2)}) copy-start(f32[4,128,128]{2,1,0:T(8,128)} %copy-done.9) | copy-start | bytes 786436
  64.7 2.3 %copy-start.13 = (f32[128,512]{1,0:T(8,128)S(1)}, f32[128,512]{1,0:T(8,128)}, u32[]{:S(2)}) copy-start(f32[128,512]{1,0:T(8,128)} %copy-done.12) | copy-start | bytes 786436

commit v4 on v3

--- a/solution.py
+++ b/solution.py
@@ -15,9 +15,11 @@
 F32 = jnp.float32
 BF16 = jnp.bfloat16
 FLOPS_A_MICRO = 1_100_000_000
-COST = {'ring': 0.8, 'start': 2.5, 'table': 20, 'edge': 60, 'partial': 1.4, 'sum': 1.2, 'near': 3.5, 'far': 1.6, 'base': 1, 'pack': 1.8, 'early': 1.8}
-FLAG = {'edge': ('A1', 'packB'), 'table': ('ring',), 'rs2': True}
-VMEM_LIMIT = 48 * 1024 * 1024
+COST = {
+    "ring": 0.8, "start": 2.5, "table": 20.0, "edge": 60.0, "partial": 1.4, "base": 1.0, "early": 1.8, "pack": 1.8,
+    "near": 3.5, "far": 1.6,
+}
+VMEM_LIMIT = 20 * 1024 * 1024
 
 
 def split(x):
@@ -168,10 +170,16 @@
             rows, labels = slots_of(rank[n:n + 1], weight[n:n + 1], label[n:n + 1], capacity)
             picked[n * capacity:(n + 1) * capacity, :] = rows
             board = place_labels(board, labels, r * (capacity // SUB))
-        pack_out[j, depth * capacity:, :] = jnp.zeros((SUB, pack_out.shape[2]), F32)
-        pack_out[j, depth * capacity:, :LANES] = board
+        pack_out[j, pack_out.shape[1] - SUB:, :] = board
     packed = dot3(picked[...], tile_columns(tiled[...], rest, cells_x // TS))
-    pack_out[:, :depth * capacity, :] = packed.reshape(columns, depth * capacity, packed.shape[1])
+    put(pack_out, packed.reshape(columns, depth * capacity, packed.shape[1]))
+
+
+def put(out, slots, first=0, size=None):
+    count = slots.shape[1]
+    size = count if size is None else size
+    for c in range(slots.shape[2] // LANES):
+        out[:, c * size + first:c * size + first + count, :] = slots[:, :, c * LANES:(c + 1) * LANES]
 
 
 def routing(ring, fanout):
@@ -179,51 +187,88 @@
     return [ring[first + k * SUB:first + k * SUB + fanout, :] for k in range(3)]
 
 
-def forward_kernel(capacity, columns, depth, inner, planes_a, fanout, count, at, *refs):
-    rings, edges, (pack_out, picked) = refs[:count], refs[count:-2], refs[-2:]
-    half = rings[0].shape[0] - 3 * SUB
-    tiles_x = half // planes_a // TS
-    boards = [jnp.zeros((SUB, LANES), F32) for _ in range(columns)]
-    wanted = columns_wanted((columns, LANES), depth, inner, at[1], 0)
+def pack(capacity, columns, depth, inner, fanout, level, rings, picked, pack_out, boards, first, size):
+    wanted = columns_wanted((columns, LANES), depth, inner, level, 0)
     for s, ring in enumerate(rings):
+        half = ring.shape[0] - 3 * SUB
         member, weight, label = route_rows(*routing(ring, fanout), wanted)
         rank = ranked(member)
         for j in range(columns):
             rows, labels = slots_of(rank[j:j + 1], weight[j:j + 1], label[j:j + 1], capacity)
             picked[j * capacity:(j + 1) * capacity, :] = rows
-            boards[j] = place_labels(boards[j], labels, s * (capacity // SUB))
-        packed = dot3(picked[...], tile_columns(ring[:half, :], planes_a, tiles_x))
-        pack_out[:, s * capacity:(s + 1) * capacity, :] = packed.reshape(columns, capacity, packed.shape[1])
-    if edges:
-        value = edges[0][...]
-        for part in edges[1:]:
-            value = value + part[...]
-        for i in range(value.shape[1] // SUB):
-            first = (1 + i) * LANES
-            pack_out[:, count * capacity:, first:first + LANES] = value[:, i * SUB:(i + 1) * SUB, :]
-    else:
-        pack_out[:, count * capacity:, :] = jnp.zeros((columns, SUB, pack_out.shape[2]), F32)
+            boards[j] = place_labels(boards[j], labels, (first + s) * (capacity // SUB))
+        planes = pack_out.shape[1] // size // 2
+        cells = tile_columns(ring[:half, :], planes, half // planes // TS)
+        packed = dot3(picked[...], cells)
+        put(pack_out, packed.reshape(columns, capacity, packed.shape[1]), s * capacity, size)
+    return boards
+
+
+def send(pairs, gone):
+    copies = [pltpu.make_async_copy(near, far, gone.at[i]) for i, (near, far) in enumerate(pairs)]
+    for copy in copies:
+        copy.start()
+    for copy in copies:
+        copy.wait()
+
+
+def early_kernel(capacity, columns, depth, inner, fanout, total, at, *refs):
+    rings, (far, boards_out, picked, out, gone) = refs[:-5], refs[-5:]
+    size = len(rings) * capacity
+    boards = [jnp.zeros((SUB, LANES), F32) for _ in range(columns)]
+    boards = pack(capacity, columns, depth, inner, fanout, at[1], rings, picked, out, boards, 0, size)
     for j in range(columns):
-        pack_out[j, count * capacity:, :LANES] = boards[j]
-
-
-def gather_sum(arrived, capacity, groups):
-    columns, rows, _ = arrived.shape
-    total = rows - SUB
+        boards_out[j] = boards[j]
+    send(
+        [
+            (out.at[:, c * size:(c + 1) * size], far.at[:, c * total:c * total + size])
+            for c in range(out.shape[1] // size)
+        ],
+        gone,
+    )
+
+
+def forward_kernel(capacity, columns, depth, inner, fanout, total, at, far_in, boards_in, ring, *refs):
+    edges, (far, picked, out, tail, gone) = refs[:-5], refs[-5:]
+    del far_in
+    boards = [boards_in[j] for j in range(columns)]
+    boards = pack(
+        capacity, columns, depth, inner, fanout, at[1], [ring], picked, out, boards, total // capacity - 1, capacity
+    )
+    for j in range(columns):
+        tail[j, :SUB, :] = boards[j]
+    value = edges[0][...]
+    for part in edges[1:]:
+        value = value + part[...]
+    tail[:, SUB:, :] = value
+    parts = out.shape[1] // capacity
+    send(
+        [
+            (out.at[:, c * capacity:(c + 1) * capacity], far.at[:, (c + 1) * total - capacity:(c + 1) * total])
+            for c in range(parts)
+        ] + [(tail, far.at[:, parts * total:])],
+        gone,
+    )
+
+
+def gather_sum(arrived, capacity, groups, total, parts):
     heads, cells = [], []
-    for j in range(columns):
-        board = arrived[j, total:, :LANES]
+    for j in range(arrived.shape[0]):
+        board = arrived[j, parts * total:parts * total + SUB, :]
         for g in groups:
             heads.append(read_labels(board, g * (capacity // SUB), capacity))
-            cells.append(arrived[j, g * capacity:(g + 1) * capacity, :])
-    head = jnp.concatenate(heads, axis=0).astype(BF16)
-    high, low = split(jnp.concatenate(cells, axis=0))
+            first = g * capacity
+            cells.append(beside(*[
+                arrived[j, c * total + first:c * total + first + capacity, :] for c in range(parts)
+            ]))
+    head = stacked(*heads).astype(BF16)
+    high, low = split(stacked(*cells))
     return mm_t(head, high) + mm_t(head, low)
 
 
 def partial_kernel(capacity, arrived, *outs):
     for r, out in enumerate(outs):
-        out[...] = gather_sum(arrived, capacity, [r])
+        out[...] = gather_sum(arrived, capacity, [r], len(outs) * capacity, out.shape[1] // LANES)
 
 
 def edge_sums(proj, weight, label, tiles_x, tiles_y, logs, part):
@@ -372,22 +417,17 @@
     return before - dot3(dot3(both_x, pushed), both_y)
 
 
-def sum_kernel(capacity, count, arrived, out):
-    out[...] = gather_sum(arrived, capacity, list(range(count)))
-
-
-def near_kernel(capacity, count, arrived, base, both_x, both_y, curve_x, curve_y, *refs):
-    earlier, (pushed_out, next_out, rest_out) = refs[:-3], refs[-3:]
+def near_kernel(capacity, depth, arrived, base, both_x, both_y, curve_x, curve_y, pushed_out, next_out, rest_out):
     planes, planes_a = base.shape[0], pushed_out.shape[0]
     cells_x = pushed_out.shape[1]
-    columns, rows, width = arrived.shape
-    carries = arrived[0, rows - SUB:, :]
-    for j in range(1, columns):
-        carries = carries + arrived[j, rows - SUB:, :]
-    carry_x, carry_y = carries[:, LANES:2 * LANES], carries[:, 2 * LANES:2 * LANES + cells_x]
-    total = gather_sum(arrived, capacity, list(range(count)))
-    for part in earlier:
-        total = total + part[...]
+    total, parts = depth * capacity, 2 * planes_a
+    first = parts * total + SUB
+    carries = arrived[0, first:, :]
+    for j in range(1, arrived.shape[0]):
+        carries = carries + arrived[j, first:, :]
+    carry_x = carries[:SUB]
+    carry_y = beside(*[carries[i:i + SUB] for i in range(SUB, carries.shape[0], SUB)])
+    total = gather_sum(arrived, capacity, list(range(depth)), total, parts)
     pushed = swap_blocks(tile_rows(total, planes_a, cells_x // TS)).reshape(planes_a, cells_x, LANES)
     pushed_out[...] = pushed
     for z in range(planes):
@@ -490,7 +530,7 @@
     device_count = columns * depth
     capacity = max(2, 3 * fanout * tile_count // (2 * device_count))
     capacity = -(-capacity // SUB) * SUB
-    rows = depth * capacity + SUB
+    slots = depth * capacity
     planes_a = planes // 2
     rest = planes - planes_a
     tile_cells = 2 * LANES
@@ -515,21 +555,14 @@
         rings[s] = turn(rings[s - 1], "z", 1)
         if s < depth - s:
             rings[depth - s] = turn(rings[(depth - s + 1) % depth], "z", -1)
-    have = {"A1": rings[1], "A3": rings[-1], "ring": ring}
-
-    def wait_of(name):
-        return [have[x] for x in FLAG.get(name, ())]
 
     packed_b = call(
         "start", functools.partial(start_kernel, capacity, columns, depth, inner, planes_a, fanout),
-        array(columns, rows, rest * tile_cells),
+        array(columns, 2 * rest * slots + SUB, LANES),
         [scalars] + [near] * 2,
         [pltpu.VMEM((columns * depth * capacity, tile_count), F32)],
-        wait_of("start"),
     )(at, ring, tiled)
     arrived_b = lax.all_to_all(packed_b, ("gx", "x"), 0, 0, tiled=True)
-    have["B"] = arrived_b
-    have["packB"] = packed_b
     decay = 1.0 - 1.0 / reach
     logs = jnp.log(decay)
     eight = 2 * planes
@@ -542,7 +575,7 @@
         ],
         [scalars] * 2,
         (),
-        wait_of("table"),
+        [ring],
     )(decay, logs)
     edge_rows = tiles_x + tiles_y
     edges = call(
@@ -550,50 +583,59 @@
         [array(columns, edge_rows, LANES)] * depth,
         [scalars] * 2 + [near] * 7,
         [pltpu.VMEM((depth, columns, edge_rows, LANES), F32)],
-        wait_of("edge"),
+        [rings[1], packed_b],
     )(at, logs, target_density, table, lines, coef, both_x, ring, tiled)
-    have["edge"] = edges[0]
     edges = [edges[0]] + [turn(edges[o], "z", o) for o in range(1, depth)]
     sums = call(
         "partial", functools.partial(partial_kernel, capacity), [array(tile_count, rest * tile_cells)] * depth,
-        None, (), wait_of("partial"),
+        None, (),
     )(arrived_b)
-    have["sums"] = sums[1]
-    if FLAG.get("rs2"):
-        moving = [sums[0], turn(sums[1] + turn(sums[2], "z", -1), "z", -1), turn(sums[3], "z", 1)]
-    else:
-        moving = [sums[0]] + [turn(sums[r], "z", -r) for r in range(1, depth)]
+    moving = {r: sums[r] for r in range(depth)}
+    for r in range(depth // 2, 0, -1):
+        moving[r - 1] = turn(moving[r], "z", -1) if r == 1 else moving[r - 1] + turn(moving[r], "z", -1)
+    moving = [sums[0], moving[0]]
+    if depth > 2:
+        more = sums[depth // 2 + 1]
+        for r in range(depth // 2 + 1, depth):
+            more = turn(more, "z", 1)
+            if r < depth - 1:
+                more = more + sums[r + 1]
+        moving.append(more)
     last = depth // 2
-    groups = [[s for s in range(depth) if s != last], [last]] if FLAG.get("split") else [list(range(depth))]
-    arrived_a = []
-    for group in groups:
-        more = edges if group is groups[-1] else []
-        rows = len(group) * capacity + SUB
-        name = "pack" if more else "early"
-        packed_a = call(
-            name,
-            functools.partial(forward_kernel, capacity, columns, depth, inner, planes_a, fanout, len(group)),
-            array(columns, rows, planes_a * tile_cells),
-            [scalars] + [near] * (len(group) + len(more)),
-            [pltpu.VMEM((columns * capacity, tile_count), F32)],
-            wait_of(name),
-        )(at, *[rings[s] for s in group], *more)
-        arrived_a.append(lax.all_to_all(packed_a, ("gx", "x"), 0, 0, tiled=True))
-    earlier = [
-        call("sum", functools.partial(sum_kernel, capacity, len(group)), array(tile_count, planes_a * tile_cells))(x)
-        for group, x in zip(groups[:-1], arrived_a)
-    ]
-    base = call("base", base_kernel, array(*potential.shape), None, (), wait_of("base"))(
+    order = [s for s in range(depth) if s != last]
+    parts = 2 * planes_a
+    packed_a, boards = call(
+        "early", functools.partial(early_kernel, capacity, columns, depth, inner, fanout, slots),
+        [array(columns, parts * slots + SUB + edge_rows, LANES), array(columns, SUB, LANES)],
+        [scalars] + [near] * len(order),
+        [
+            pltpu.VMEM((columns * capacity, tile_count), F32),
+            pltpu.VMEM((columns, parts * (slots - capacity), LANES), F32),
+            pltpu.SemaphoreType.DMA((parts,)),
+        ],
+        out_specs=[far, near],
+    )(at, *[rings[s] for s in order])
+    packed_a = call(
+        "pack", functools.partial(forward_kernel, capacity, columns, depth, inner, fanout, slots),
+        array(*packed_a.shape), [scalars, far] + [near] * (2 + len(edges)),
+        [
+            pltpu.VMEM((columns * capacity, tile_count), F32), pltpu.VMEM((columns, parts * capacity, LANES), F32),
+            pltpu.VMEM((columns, SUB + edge_rows, LANES), F32), pltpu.SemaphoreType.DMA((parts + 1,)),
+        ],
+        out_specs=far, input_output_aliases={1: 0},
+    )(at, packed_a, boards, rings[last], *edges)
+    arrived_a = lax.all_to_all(packed_a, ("gx", "x"), 0, 0, tiled=True)
+    base = call("base", base_kernel, array(*potential.shape))(
         target_density, potential, both_x, both_y
     )
     field = (planes_a, cells_x, cells_y)
     shapes = [array(*source_mass.shape), array(*potential.shape)]
     part = pl.BlockSpec(field, lambda i: (0, 0, 0))
     *outs, base = call(
-        "near", functools.partial(near_kernel, capacity, len(groups[-1])),
+        "near", functools.partial(near_kernel, capacity, depth),
         shapes + [array(rest, cells_x, cells_y)], None,
         out_specs=[part, part, near], grid=(1,),
-    )(arrived_a[-1], base, both_x, both_y, curve_x, curve_y, *earlier)
+    )(arrived_a, base, both_x, both_y, curve_x, curve_y)
     part = pl.BlockSpec(field, lambda i: (1, 0, 0))
     outs = call(
         "far", functools.partial(far_kernel, planes_a), shapes, [far, far] + [near] * (3 + len(moving)),

time: 69 us -> 66.9 us (0.970)
  waiting for transfers between devices: 14.3 us -> 11.7 us
  Pallas kernels: 18 us -> 19.4 us
  local copies, waits for them, and re-layouts: 4.48 us -> 3.62 us
    ppermute x9, waiting for transfers between devices: 9.32 us -> 5.95 us  [turn(): return lax.ppermute(x, axis, [(i, (i + steps) % size) for i in range(size)])]
    pallas_call x9 -> x10, Pallas kernels: 18 us -> 19.4 us  [run(): pl.pallas_call(kernel, out_shape=out_shape, in_specs=specs + [pl.BlockSpe...]
    unnamed x30, local copies, waits for them, and re-layouts: 4.48 us -> 3.62 us
    all_to_all x1, waiting for transfers between devices: 4.96 us -> 5.7 us  [per_device(): arrived_a = lax.all_to_all(packed_a, ('gx', 'x'), 0, 0, tiled=True)]
  transfers between devices with their start and end apart: 11 -> 11, of which waited for: 4 -> 3; matrix products, arithmetic and copies ran while one was open for 1% -> 1% of each run, Pallas kernels for 23% -> 26%
where the time goes in v4:
time: 66.9 us; the launch traced here: 66.5 us
  starting transfers between devices  29.5 us (44%)
  Pallas kernels  19.4 us (29%)
  waiting for transfers between devices  11.7 us (17%)
  local copies, waits for them, and re-layouts  3.62 us (5%)
  other arithmetic  1.53 us (2%)
  between operations  0.82 us (1%)
    ppermute x9, starting transfers between devices, turn(): return lax.ppermute(x, axis, [(i, (i + steps) % size) for i in range(size)])  21.6 us
    pallas_call x10, Pallas kernels, run(): pl.pallas_call(kernel, out_shape=out_shape, in_specs=specs + [pl.BlockSpe...  19.4 us
    ppermute x9, waiting for transfers between devices, turn(): return lax.ppermute(x, axis, [(i, (i + steps) % size) for i in range(size)])  5.95 us
    all_to_all x1, waiting for transfers between devices, per_device(): arrived_a = lax.all_to_all(packed_a, ('gx', 'x'), 0, 0, tiled=True)  5.7 us
    all_to_all x1, starting transfers between devices, per_device(): arrived_b = lax.all_to_all(packed_b, ('gx', 'x'), 0, 0, tiled=True)  4.01 us
    all_to_all x1, starting transfers between devices, per_device(): arrived_a = lax.all_to_all(packed_a, ('gx', 'x'), 0, 0, tiled=True)  3.86 us
    unnamed x30, local copies, waits for them, and re-layouts  3.62 us
  transfers between devices with their start and end apart: 11, of which 3 were waited for; matrix products, arithmetic and copies ran while one was open for 1% of the time, Pallas kernels for 26%

profile of v4, /device:TPU:0, one launch (start us, length us, event | category | flops | bytes accessed | tf_op | source)
XLA Modules:
  0.0 66.5 jit_solution(9225197098472235735)
XLA Ops:
  0.6 0.7 %add_convert_fusion.refs_1_ = f32[3,4,128]{2,1,0:T(4,128)S(1)} fusion(s32[1,4,128]{2,1,0:T(4,128)} %bitcast.18, s32[1,4,128]{2,1,0:T(4,128)} %bitcast.19, s32[1,4,128]{2,1,0:T(4,128)} %bitcast.20), kind=kLoop, calls=%fused_computation | loop fusion | flops 4608 | bytes 12288 | tf_op jit(solution)/shard_map/convert_element_type | solution.py:552
  1.4 1.0 %copy-done = f32[4,256,128]{2,1,0:T(8,128)S(1)} copy-done((f32[4,256,128]{2,1,0:T(8,128)S(1)}, f32[4,256,128]{2,1,0:T(8,128)}, u32[]{:S(2)}) %copy-start) | copy-done | bytes 524312
  2.4 0.8 %shard_map.86 = (f32[536,128]{1,0:T(8,128)S(1)}, f32[512,128]{1,0:T(8,128)S(1)}) custom-call(f32[4,256,128]{2,1,0:T(8,128)S(1)} %copy-done, f32[3,4,128]{2,1,0:T(4,128)S(1)} %add_convert_fusion.refs_1_), custom_call_target="tpu_custom_call" | custom-call | flops 880000000 | tf_op jit(solution)/shard_map/pallas_call | solution.py:465
  3.1 3.1 %collective-permute-start = (f32[536,128]{1,0:T(8,128)S(1)}, f32[536,128]{1,0:T(8,128)S(1)}, u32[]{:S(2)}, u32[]{:S(2)}) collective-permute-start(f32[536,128]{1,0:T(8,128)S(1)} %get-tuple-element.24.refs_1_.refs_2_.refs_7_), channel_id=1, source_target_pairs={{0,2},{2,4},{4,6},{6,0},{1,3},{3,5},{5,7},{7,1},{8,10},{10,12},{12... | collective-permute-start | bytes 823304 | tf_op jit(solution)/shard_map/ppermute | solution.py:546
  6.2 2.1 %collective-permute-start.1 = (f32[536,128]{1,0:T(8,128)S(1)}, f32[536,128]{1,0:T(8,128)S(1)}, u32[]{:S(2)}, u32[]{:S(2)}) collective-permute-start(f32[536,128]{1,0:T(8,128)S(1)} %get-tuple-element.24.refs_1_.refs_2_.refs_7_), channel_id=1, source_target_pairs={{0,6},{2,0},{4,2},{6,4},{1,7},{3,1},{5,3},{7,5},{8,14},{10,8},{12,... | collective-permute-start | bytes 823304 | tf_op jit(solution)/shard_map/ppermute | solution.py:546
  8.3 0.1 pad_add_fusion.refs_0_
  8.4 2.4 %shard_map.89.refs_10_ = f32[8,392,128]{2,1,0:T(8,128)} custom-call(s32[3]{0:T(128)S(1)} %pad_add_fusion.refs_0_, f32[536,128]{1,0:T(8,128)S(1)} %get-tuple-element.24.refs_1_.refs_2_.refs_7_, f32[512,128]{1,0:T(8,128)S(1)} %get-tuple-element.31.refs_2_.refs_8_), custom_call_target="tpu_custom_call" | custom-call | flops 2750000128 | tf_op jit(solution)/shard_map/pallas_call | solution.py:465
  10.8 4.0 %all-to-all-start.1 = ((f32[8,392,128]{2,1,0:T(8,128)}), f32[8,392,128]{2,1,0:T(8,128)S(1)}, u32[]{:S(2)}, u32[]{:S(2)}) async-start(f32[8,392,128]{2,1,0:T(8,128)} %shard_map.89.refs_10_), calls=%async_computation.1 | async-start | bytes 3211264 | tf_op jit(solution)/shard_map/all_to_all | solution.py:565
  14.9 0.0 copy-start.1
  14.9 1.2 %shard_map.88 = (f32[1024,256]{1,0:T(8,128)S(1)}, f32[4,8,256]{2,1,0:T(8,128)S(1)}, f32[7,8,128]{2,1,0:T(8,128)S(1)}, f32[8,256]{1,0:T(8,128)S(1)}, f32[8,128]{1...) custom-call(f32[4]{0:T(128)S(1)} %get-tuple-element.47.refs_0_, f32[4]{0:T(128)S(1)} %get-tuple-element.46.refs_1_, ...), custom_call_target="tpu_custom_call" | custom-call | flops 22000001024 | tf_op jit(solution)/shard_map/pallas_call | solution.py:465
  16.1 0.7 %copy-done.9 = f32[4,128,128]{2,1,0:T(8,128)} copy-done((f32[4,128,128]{2,1,0:T(8,128)}, f32[4,128,128]{2,1,0:T(8,128)S(1)}, u32[]{:S(2)}) %copy-start.9) | copy-done | bytes 262168
  16.8 4.4 %shard_map.90 = (f32[8,24,128]{2,1,0:T(8,128)S(1)}, f32[8,24,128]{2,1,0:T(8,128)S(1)}, f32[8,24,128]{2,1,0:T(8,128)S(1)}, f32[8,24,128]{2,1,0:T(8,128)S(1)}) custom-call(s32[3]{0:T(128)S(1)} %pad_add_fusion.refs_0_, f32[4]{0:T(128)S(1)} %get-tuple-element.46.refs_1_, f32[4,256,128]{2,1,0:T(8,128)S(1)} %copy-done.1, ...), custom_call_target="tpu_custom_call" | custom-call | flops 65999998976 | tf_op jit(solution)/shard_map/pallas_call | solution.py:465
  21.2 5.1 %collective-permute-start.3 = (f32[8,24,128]{2,1,0:T(8,128)S(1)}, f32[8,24,128]{2,1,0:T(8,128)S(1)}, u32[]{:S(2)}, u32[]{:S(2)}) collective-permute-start(f32[8,24,128]{2,1,0:T(8,128)S(1)} %get-tuple-element.33), channel_id=1, source_target_pairs={{0,2},{2,4},{4,6},{6,0},{1,3},{3,5},{5,7},{7,1},{8,10},{10,12},{12... | collective-permute-start | bytes 294920 | tf_op jit(solution)/shard_map/ppermute | solution.py:546
  26.2 1.2 %collective-permute-start.4 = (f32[8,24,128]{2,1,0:T(8,128)S(1)}, f32[8,24,128]{2,1,0:T(8,128)S(1)}, u32[]{:S(2)}, u32[]{:S(2)}) collective-permute-start(f32[8,24,128]{2,1,0:T(8,128)S(1)} %get-tuple-element.34), channel_id=1, source_target_pairs={{0,4},{2,6},{4,0},{6,2},{1,5},{3,7},{5,1},{7,3},{8,12},{10,14},{12... | collective-permute-start | bytes 294920 | tf_op jit(solution)/shard_map/ppermute | solution.py:546
  27.5 2.8 %collective-permute-start.5 = (f32[8,24,128]{2,1,0:T(8,128)S(1)}, f32[8,24,128]{2,1,0:T(8,128)S(1)}, u32[]{:S(2)}, u32[]{:S(2)}) collective-permute-start(f32[8,24,128]{2,1,0:T(8,128)S(1)} %get-tuple-element.35), channel_id=1, source_target_pairs={{0,6},{2,0},{4,2},{6,4},{1,7},{3,1},{5,3},{7,5},{8,14},{10,8},{12,... | collective-permute-start | bytes 294920 | tf_op jit(solution)/shard_map/ppermute | solution.py:546
  30.3 2.6 %shard_map.87 = (f32[8,416,128]{2,1,0:T(8,128)}, f32[8,8,128]{2,1,0:T(8,128)S(1)}) custom-call(s32[3]{0:T(128)S(1)} %pad_add_fusion.refs_0_, f32[536,128]{1,0:T(8,128)S(1)} %get-tuple-element.24.refs_1_.refs_2_.refs_7_, f32[536,128]{1,0:T(8,128)S(1)} %collective-permute-done.refs_2_.refs_9_, f32[536,128]{1,0:T(8,128)S(1)} %collective-permute-done.1.refs_3_), custom_call_target="tpu_custom_call" | custom-call | flops 1980000000 | tf_op jit(solution)/shard_map/pallas_call | solution.py:465
  32.9 1.1 %collective-permute-done.4.refs_6_ = f32[8,24,128]{2,1,0:T(8,128)S(1)} collective-permute-done((f32[8,24,128]{2,1,0:T(8,128)S(1)}, f32[8,24,128]{2,1,0:T(8,128)S(1)}, u32[]{:S(2)}, u32[]{:S(2)}) %collective-permute-start.4) | collective-permute-done | bytes 98336 | tf_op jit(solution)/shard_map/ppermute | solution.py:546
  34.0 1.8 %shard_map.91 = f32[8,416,128]{2,1,0:T(8,128)} custom-call(s32[3]{0:T(128)S(1)} %pad_add_fusion.refs_0_, f32[8,416,128]{2,1,0:T(8,128)} %get-tuple-element.25.refs_1_, f32[8,8,128]{2,1,0:T(8,128)S(1)} %get-tuple-element.26.refs_2_, f32[536,128]{1,0:T(8,128)S(1)} %collective-permute-done.2.refs_3_, ...), custom_call_target="tpu_custom_call", output_to_operand_aliasing={{}: (1, {})} | custom-call | flops 1980000000 | tf_op jit(solution)/shard_map/pallas_call | solution.py:465
  35.9 3.9 %all-to-all-start = ((f32[8,416,128]{2,1,0:T(8,128)}), f32[8,416,128]{2,1,0:T(8,128)S(1)}, u32[]{:S(2)}, u32[]{:S(2)}) async-start(f32[8,416,128]{2,1,0:T(8,128)} %shard_map.91), calls=%async_computation | async-start | bytes 3407872 | tf_op jit(solution)/shard_map/all_to_all | solution.py:627
  39.7 1.5 %shard_map.94 = (f32[128,512]{1,0:T(8,128)S(1)}, f32[128,512]{1,0:T(8,128)S(1)}, f32[128,512]{1,0:T(8,128)S(1)}, f32[128,512]{1,0:T(8,128)}) custom-call(f32[8,392,128]{2,1,0:T(8,128)S(1)} %all-to-all-done.1.refs_0_), custom_call_target="tpu_custom_call" | custom-call | flops 1540000000 | tf_op jit(solution)/shard_map/pallas_call | solution.py:465
  41.2 3.0 %collective-permute-start.6 = (f32[128,512]{1,0:T(8,128)S(1)}, f32[128,512]{1,0:T(8,128)S(1)}, u32[]{:S(2)}, u32[]{:S(2)}) collective-permute-start(f32[128,512]{1,0:T(8,128)S(1)} %get-tuple-element.44), channel_id=1, source_target_pairs={{0,6},{2,0},{4,2},{6,4},{1,7},{3,1},{5,3},{7,5},{8,14},{10,8},{12,... | collective-permute-start | bytes 786440 | tf_op jit(solution)/shard_map/ppermute | solution.py:546
  44.3 0.0 copy-start.11
  44.3 1.0 %shard_map.92.refs_1_ = f32[4,256,128]{2,1,0:T(8,128)S(1)} custom-call(f32[4,256,128]{2,1,0:T(8,128)S(1)} %copy-done.2, f32[4,256,128]{2,1,0:T(8,128)S(1)} %copy-done.3, f32[4,256,256]{2,1,0:T(8,128)S(1)} %copy-done.5, f32[4,128,128]{2,1,0:T(8,128)S(1)} %copy-done.10), custom_call_target="tpu_custom_call" | custom-call | flops 1100000000 | tf_op jit(solution)/shard_map/pallas_call | solution.py:465
  45.3 0.0 copy-start.7
  45.3 0.8 %copy-done.7 = f32[4,256,128]{2,1,0:T(8,128)} copy-done((f32[4,256,128]{2,1,0:T(8,128)}, f32[4,256,128]{2,1,0:T(8,128)S(1)}, u32[]{:S(2)}) %copy-start.7) | copy-done | bytes 524312
  46.1 4.8 %collective-permute-done.6 = f32[128,512]{1,0:T(8,128)S(1)} collective-permute-done((f32[128,512]{1,0:T(8,128)S(1)}, f32[128,512]{1,0:T(8,128)S(1)}, u32[]{:S(2)}, u32[]{:S(2)}) %collective-permute-start.6) | collective-permute-done | bytes 262176 | tf_op jit(solution)/shard_map/ppermute | solution.py:546
  50.9 0.7 %add.3 = f32[128,512]{1,0:T(8,128)} add(f32[128,512]{1,0:T(8,128)S(1)} %get-tuple-element.43, f32[128,512]{1,0:T(8,128)S(1)} %collective-permute-done.6) | non-fusion elementwise | flops 65536 | bytes 786432 | tf_op jit(solution)/shard_map/add | solution.py:595
  51.7 4.3 %collective-permute-start.7 = (f32[128,512]{1,0:T(8,128)}, f32[128,512]{1,0:T(8,128)S(1)}, u32[]{:S(2)}, u32[]{:S(2)}) collective-permute-start(f32[128,512]{1,0:T(8,128)} %add.3), channel_id=1, source_target_pairs={{0,6},{2,0},{4,2},{6,4},{1,7},{3,1},{5,3},{7,5},{8,14},{10,8},{12,... | collective-permute-start | bytes 786440 | tf_op jit(solution)/shard_map/ppermute | solution.py:546
  56.0 5.7 %all-to-all-done.refs_0_ = f32[8,416,128]{2,1,0:T(8,128)S(1)} async-done(((f32[8,416,128]{2,1,0:T(8,128)}), f32[8,416,128]{2,1,0:T(8,128)S(1)}, u32[]{:S(2)}, u32[]{:S(2)}) %all-to-all-start) | async-done | bytes 1703968 | tf_op jit(solution)/shard_map/all_to_all | solution.py:627
  61.7 1.0 %copy-done.8 = f32[4,256,128]{2,1,0:T(8,128)S(1)} copy-done((f32[4,256,128]{2,1,0:T(8,128)S(1)}, f32[4,256,128]{2,1,0:T(8,128)}, u32[]{:S(2)}) %copy-start.8) | copy-done | bytes 524312
  62.7 2.2 %shard_map.93 = (f32[4,256,128]{2,1,0:T(8,128)}, f32[4,256,128]{2,1,0:T(8,128)}, f32[2,256,128]{2,1,0:T(8,128)S(1)}) custom-call(f32[8,416,128]{2,1,0:T(8,128)S(1)} %all-to-all-done.refs_0_, f32[4,256,128]{2,1,0:T(8,128)S(1)} %copy-done.8, f32[4,256,256]{2,1,0:T(8,128)S(1)} %copy-done.6, f32[4,128,128]{2,1,0:T(8,128)S(1)} %copy-done.11, ...), custom_call_target="tpu_custom_call" | custom-call | flops 3849999872 | tf_op jit(solution)/shard_map/pallas_call | solution.py:465
  65.0 1.6 %shard_map.95 = (f32[4,256,128]{2,1,0:T(8,128)}, f32[4,256,128]{2,1,0:T(8,128)}) custom-call(f32[4,256,128]{2,1,0:T(8,128)} %get-tuple-element.39.refs_0_, f32[4,256,128]{2,1,0:T(8,128)} %get-tuple-element.40.refs_1_, f32[2,256,128]{2,1,0:T(8,128)S(1)} %get-tuple-element.41.refs_2_, ...), custom_call_target="tpu_custom_call", output_to_operand_aliasing={{0}: (0, {}), {1}: (1, {})} | custom-call | flops 1760000000 | tf_op jit(solution)/shard_map/pallas_call | solution.py:465
  (34 shorter events, 0.1 us)
Async XLA Ops:
  1.3 1.0 %copy-start = (f32[4,256,128]{2,1,0:T(8,128)S(1)}, f32[4,256,128]{2,1,0:T(8,128)}, u32[]{:S(2)}) copy-start(f32[4,256,128]{2,1,0:T(8,128)} %refs_0_.2) | copy-start | bytes 1572868
  3.1 13.6 %collective-permute-start = (f32[536,128]{1,0:T(8,128)S(1)}, f32[536,128]{1,0:T(8,128)S(1)}, u32[]{:S(2)}, u32[]{:S(2)}) collective-permute-start(f32[536,128]{1,0:T(8,128)S(1)} %get-tuple-element.24.refs_1_.refs_2_.refs_7_), channel_id=1, source_target_pairs={{0,2},{2,4},{4,6},{6,0},{1,3},{3,5},{5,7},{7,1},{8,10},{10,12},{12... | collective-permute-start | bytes 823304 | tf_op jit(solution)/shard_map/ppermute | solution.py:546
  6.2 24.1 %collective-permute-start.1 = (f32[536,128]{1,0:T(8,128)S(1)}, f32[536,128]{1,0:T(8,128)S(1)}, u32[]{:S(2)}, u32[]{:S(2)}) collective-permute-start(f32[536,128]{1,0:T(8,128)S(1)} %get-tuple-element.24.refs_1_.refs_2_.refs_7_), channel_id=1, source_target_pairs={{0,6},{2,0},{4,2},{6,4},{1,7},{3,1},{5,3},{7,5},{8,14},{10,8},{12,... | collective-permute-start | bytes 823304 | tf_op jit(solution)/shard_map/ppermute | solution.py:546
  10.8 4.0 %copy-start.14 = (f32[4]{0:T(128)S(1)}, f32[4]{0:T(128)}, u32[]{:S(2)}) copy-start(f32[4]{0:T(128)} %param.13) | copy-start | bytes 52
  10.8 25.0 %all-to-all-start.1 = ((f32[8,392,128]{2,1,0:T(8,128)}), f32[8,392,128]{2,1,0:T(8,128)S(1)}, u32[]{:S(2)}, u32[]{:S(2)}) async-start(f32[8,392,128]{2,1,0:T(8,128)} %shard_map.89.refs_10_), calls=%async_computation.1 | async-start | bytes 3211264 | tf_op jit(solution)/shard_map/all_to_all | solution.py:565
  14.9 1.9 %copy-start.1 = (f32[4,256,128]{2,1,0:T(8,128)S(1)}, f32[4,256,128]{2,1,0:T(8,128)}, u32[]{:S(2)}) copy-start(f32[4,256,128]{2,1,0:T(8,128)} %refs_0_.3) | copy-start | bytes 1572868
  16.1 0.7 %copy-start.9 = (f32[4,128,128]{2,1,0:T(8,128)}, f32[4,128,128]{2,1,0:T(8,128)S(1)}, u32[]{:S(2)}) copy-start(f32[4,128,128]{2,1,0:T(8,128)S(1)} %get-tuple-element.36.refs_3_.refs_4_) | copy-start | bytes 786436
  16.8 4.4 %copy-start.4 = (f32[4,256,256]{2,1,0:T(8,128)}, f32[4,256,256]{2,1,0:T(8,128)S(1)}, u32[]{:S(2)}) copy-start(f32[4,256,256]{2,1,0:T(8,128)S(1)} %get-tuple-element.30.refs_6_.refs_2_.refs_3_) | copy-start | bytes 3145732
  16.8 17.3 %collective-permute-start.2 = (f32[536,128]{1,0:T(8,128)S(1)}, f32[536,128]{1,0:T(8,128)S(1)}, u32[]{:S(2)}, u32[]{:S(2)}) collective-permute-start(f32[536,128]{1,0:T(8,128)S(1)} %collective-permute-done.refs_2_.refs_9_), channel_id=1, source_target_pairs={{0,2},{2,4},{4,6},{6,0},{1,3},{3,5},{5,7},{7,1},{8,10},{10,12},{12... | collective-permute-start | bytes 823304 | tf_op jit(solution)/shard_map/ppermute | solution.py:546
  21.2 11.7 %collective-permute-start.3 = (f32[8,24,128]{2,1,0:T(8,128)S(1)}, f32[8,24,128]{2,1,0:T(8,128)S(1)}, u32[]{:S(2)}, u32[]{:S(2)}) collective-permute-start(f32[8,24,128]{2,1,0:T(8,128)S(1)} %get-tuple-element.33), channel_id=1, source_target_pairs={{0,2},{2,4},{4,6},{6,0},{1,3},{3,5},{5,7},{7,1},{8,10},{10,12},{12... | collective-permute-start | bytes 294920 | tf_op jit(solution)/shard_map/ppermute | solution.py:546
  26.2 7.8 %collective-permute-start.4 = (f32[8,24,128]{2,1,0:T(8,128)S(1)}, f32[8,24,128]{2,1,0:T(8,128)S(1)}, u32[]{:S(2)}, u32[]{:S(2)}) collective-permute-start(f32[8,24,128]{2,1,0:T(8,128)S(1)} %get-tuple-element.34), channel_id=1, source_target_pairs={{0,4},{2,6},{4,0},{6,2},{1,5},{3,7},{5,1},{7,3},{8,12},{10,14},{12... | collective-permute-start | bytes 294920 | tf_op jit(solution)/shard_map/ppermute | solution.py:546
  27.5 6.5 %collective-permute-start.5 = (f32[8,24,128]{2,1,0:T(8,128)S(1)}, f32[8,24,128]{2,1,0:T(8,128)S(1)}, u32[]{:S(2)}, u32[]{:S(2)}) collective-permute-start(f32[8,24,128]{2,1,0:T(8,128)S(1)} %get-tuple-element.35), channel_id=1, source_target_pairs={{0,6},{2,0},{4,2},{6,4},{1,7},{3,1},{5,3},{7,5},{8,14},{10,8},{12,... | collective-permute-start | bytes 294920 | tf_op jit(solution)/shard_map/ppermute | solution.py:546
  35.9 25.8 %all-to-all-start = ((f32[8,416,128]{2,1,0:T(8,128)}), f32[8,416,128]{2,1,0:T(8,128)S(1)}, u32[]{:S(2)}, u32[]{:S(2)}) async-start(f32[8,416,128]{2,1,0:T(8,128)} %shard_map.91), calls=%async_computation | async-start | bytes 3407872 | tf_op jit(solution)/shard_map/all_to_all | solution.py:627
  39.7 4.6 %copy-start.2 = (f32[4,256,128]{2,1,0:T(8,128)S(1)}, f32[4,256,128]{2,1,0:T(8,128)}, u32[]{:S(2)}) copy-start(f32[4,256,128]{2,1,0:T(8,128)} %refs_0_.3) | copy-start | bytes 1572868
  39.7 4.6 %copy-start.3 = (f32[4,256,128]{2,1,0:T(8,128)S(1)}, f32[4,256,128]{2,1,0:T(8,128)}, u32[]{:S(2)}) copy-start(f32[4,256,128]{2,1,0:T(8,128)} %refs_1_.1) | copy-start | bytes 1572868
  39.7 4.6 %copy-start.5 = (f32[4,256,256]{2,1,0:T(8,128)S(1)}, f32[4,256,256]{2,1,0:T(8,128)}, u32[]{:S(2)}) copy-start(f32[4,256,256]{2,1,0:T(8,128)} %copy-done.4) | copy-start | bytes 3145732
  39.7 4.6 %copy-start.10 = (f32[4,128,128]{2,1,0:T(8,128)S(1)}, f32[4,128,128]{2,1,0:T(8,128)}, u32[]{:S(2)}) copy-start(f32[4,128,128]{2,1,0:T(8,128)} %copy-done.9) | copy-start | bytes 786436
  41.2 4.1 %copy-start.12 = (f32[128,512]{1,0:T(8,128)}, f32[128,512]{1,0:T(8,128)S(1)}, u32[]{:S(2)}) copy-start(f32[128,512]{1,0:T(8,128)S(1)} %get-tuple-element.42.refs_5_) | copy-start | bytes 786436
  41.2 9.7 %collective-permute-start.6 = (f32[128,512]{1,0:T(8,128)S(1)}, f32[128,512]{1,0:T(8,128)S(1)}, u32[]{:S(2)}, u32[]{:S(2)}) collective-permute-start(f32[128,512]{1,0:T(8,128)S(1)} %get-tuple-element.44), channel_id=1, source_target_pairs={{0,6},{2,0},{4,2},{6,4},{1,7},{3,1},{5,3},{7,5},{8,14},{10,8},{12,... | collective-permute-start | bytes 786440 | tf_op jit(solution)/shard_map/ppermute | solution.py:546
  44.3 17.4 %copy-start.6 = (f32[4,256,256]{2,1,0:T(8,128)S(1)}, f32[4,256,256]{2,1,0:T(8,128)}, u32[]{:S(2)}) copy-start(f32[4,256,256]{2,1,0:T(8,128)} %copy-done.4) | copy-start | bytes 3145732
  44.3 17.4 %copy-start.11 = (f32[4,128,128]{2,1,0:T(8,128)S(1)}, f32[4,128,128]{2,1,0:T(8,128)}, u32[]{:S(2)}) copy-start(f32[4,128,128]{2,1,0:T(8,128)} %copy-done.9) | copy-start | bytes 786436
  45.3 0.8 %copy-start.7 = (f32[4,256,128]{2,1,0:T(8,128)}, f32[4,256,128]{2,1,0:T(8,128)S(1)}, u32[]{:S(2)}) copy-start(f32[4,256,128]{2,1,0:T(8,128)S(1)} %shard_map.92.refs_1_) | copy-start | bytes 1572868
  46.1 18.8 %collective-permute-start.8 = (f32[128,512]{1,0:T(8,128)}, f32[128,512]{1,0:T(8,128)S(1)}, u32[]{:S(2)}, u32[]{:S(2)}) collective-permute-start(f32[128,512]{1,0:T(8,128)} %get-tuple-element.45), channel_id=1, source_target_pairs={{0,2},{2,4},{4,6},{6,0},{1,3},{3,5},{5,7},{7,1},{8,10},{10,12},{12... | collective-permute-start | bytes 786440 | tf_op jit(solution)/shard_map/ppermute | solution.py:546
  51.7 13.3 %collective-permute-start.7 = (f32[128,512]{1,0:T(8,128)}, f32[128,512]{1,0:T(8,128)S(1)}, u32[]{:S(2)}, u32[]{:S(2)}) collective-permute-start(f32[128,512]{1,0:T(8,128)} %add.3), channel_id=1, source_target_pairs={{0,6},{2,0},{4,2},{6,4},{1,7},{3,1},{5,3},{7,5},{8,14},{10,8},{12,... | collective-permute-start | bytes 786440 | tf_op jit(solution)/shard_map/ppermute | solution.py:546
  61.7 1.0 %copy-start.8 = (f32[4,256,128]{2,1,0:T(8,128)S(1)}, f32[4,256,128]{2,1,0:T(8,128)}, u32[]{:S(2)}) copy-start(f32[4,256,128]{2,1,0:T(8,128)} %copy-done.7) | copy-start | bytes 1572868
  62.7 2.3 %copy-start.13 = (f32[128,512]{1,0:T(8,128)S(1)}, f32[128,512]{1,0:T(8,128)}, u32[]{:S(2)}) copy-start(f32[128,512]{1,0:T(8,128)} %copy-done.12) | copy-start | bytes 786436

commit v5 on v4

--- a/solution.py
+++ b/solution.py
@@ -112,9 +112,11 @@
 def slots_of(rank, weight, label, capacity):
     slot = lax.broadcasted_iota(jnp.int32, (capacity, rank.shape[1]), 0).astype(F32)
     chosen = rank == slot
-    picked = jnp.where(chosen, weight, 0.0)
-    labels = jnp.sum(jnp.where(chosen, label, 0.0), axis=1, keepdims=True)
-    return picked, labels
+    return jnp.where(chosen, weight, 0.0), jnp.where(chosen, label, 0.0)
+
+
+def in_all_lanes(rows):
+    return mm(rows.astype(BF16), jnp.ones((rows.shape[1], LANES), BF16))
 
 
 def place_labels(board, labels, first):
@@ -163,14 +165,16 @@
     wanted = columns_wanted((columns * depth, LANES), depth, inner, at[1], None)
     member, weight, label = route_rows(names, tiles, shares, wanted)
     rank = ranked(member)
+    named = []
+    for n in range(columns * depth):
+        rows, labels = slots_of(rank[n:n + 1], weight[n:n + 1], label[n:n + 1], capacity)
+        picked[n * capacity:(n + 1) * capacity, :] = rows
+        named.append(labels)
+    named = in_all_lanes(stacked(*named))
+    slots = depth * capacity
     for j in range(columns):
         board = jnp.zeros((SUB, LANES), F32)
-        for r in range(depth):
-            n = j * depth + r
-            rows, labels = slots_of(rank[n:n + 1], weight[n:n + 1], label[n:n + 1], capacity)
-            picked[n * capacity:(n + 1) * capacity, :] = rows
-            board = place_labels(board, labels, r * (capacity // SUB))
-        pack_out[j, pack_out.shape[1] - SUB:, :] = board
+        pack_out[j, pack_out.shape[1] - SUB:, :] = place_labels(board, named[j * slots:(j + 1) * slots], 0)
     packed = dot3(picked[...], tile_columns(tiled[...], rest, cells_x // TS))
     put(pack_out, packed.reshape(columns, depth * capacity, packed.shape[1]))
 
@@ -193,9 +197,14 @@
         half = ring.shape[0] - 3 * SUB
         member, weight, label = route_rows(*routing(ring, fanout), wanted)
         rank = ranked(member)
+        named = []
         for j in range(columns):
             rows, labels = slots_of(rank[j:j + 1], weight[j:j + 1], label[j:j + 1], capacity)
             picked[j * capacity:(j + 1) * capacity, :] = rows
+            named.append(labels)
+        named = in_all_lanes(stacked(*named))
+        for j in range(columns):
+            labels = named[j * capacity:(j + 1) * capacity]
             boards[j] = place_labels(boards[j], labels, (first + s) * (capacity // SUB))
         planes = pack_out.shape[1] // size // 2
         cells = tile_columns(ring[:half, :], planes, half // planes // TS)
@@ -266,9 +275,28 @@
     return mm_t(head, high) + mm_t(head, low)
 
 
-def partial_kernel(capacity, arrived, *outs):
-    for r, out in enumerate(outs):
-        out[...] = gather_sum(arrived, capacity, [r], len(outs) * capacity, out.shape[1] // LANES)
+def partial_kernel(capacity, depth, groups, far, *refs):
+    outs, (boards, cells, here) = refs[:-3], refs[-3:]
+    slots, parts = depth * capacity, outs[0].shape[1] // LANES
+    pairs = [(far.at[:, parts * slots:parts * slots + SUB], boards)]
+    for i, r in enumerate(groups):
+        for c in range(parts):
+            first = c * slots + r * capacity
+            pairs.append((far.at[:, first:first + capacity], cells.at[i, c]))
+    copies = [pltpu.make_async_copy(a, b, here.at[i]) for i, (a, b) in enumerate(pairs)]
+    for copy in copies:
+        copy.start()
+    copies[0].wait()
+    for i, (r, out) in enumerate(zip(groups, outs)):
+        for copy in copies[1 + i * parts:1 + (i + 1) * parts]:
+            copy.wait()
+        heads, values = [], []
+        for j in range(boards.shape[0]):
+            heads.append(read_labels(boards[j], r * (capacity // SUB), capacity))
+            values.append(beside(*[cells[i, c, j] for c in range(parts)]))
+        head = stacked(*heads).astype(BF16)
+        high, low = split(stacked(*values))
+        out[...] = mm_t(head, high) + mm_t(head, low)
 
 
 def edge_sums(proj, weight, label, tiles_x, tiles_y, logs, part):
@@ -417,7 +445,17 @@
     return before - dot3(dot3(both_x, pushed), both_y)
 
 
-def near_kernel(capacity, depth, arrived, base, both_x, both_y, curve_x, curve_y, pushed_out, next_out, rest_out):
+def out_copies(near, far, gone, planes, first):
+    return [
+        pltpu.make_async_copy(near.at[z], far.at[first + z], gone.at[z]) for z in range(planes)
+    ]
+
+
+def near_kernel(capacity, depth, arrived, base_far, both_x, both_y, curve_x, curve_y, pushed_far, next_far, rest_out,
+                pushed_out, next_out, pushed_gone, next_gone, base, base_here):
+    del base_far
+    fetched = pltpu.make_async_copy(next_far, base, base_here)
+    fetched.start()
     planes, planes_a = base.shape[0], pushed_out.shape[0]
     cells_x = pushed_out.shape[1]
     total, parts = depth * capacity, 2 * planes_a
@@ -428,29 +466,42 @@
     carry_x = carries[:SUB]
     carry_y = beside(*[carries[i:i + SUB] for i in range(SUB, carries.shape[0], SUB)])
     total = gather_sum(arrived, capacity, list(range(depth)), total, parts)
-    pushed = swap_blocks(tile_rows(total, planes_a, cells_x // TS)).reshape(planes_a, cells_x, LANES)
-    pushed_out[...] = pushed
+    pushed_out[...] = swap_blocks(tile_rows(total, planes_a, cells_x // TS)).reshape(planes_a, cells_x, LANES)
+    copies = out_copies(pushed_out, pushed_far, pushed_gone, planes_a, 0)
+    copies += out_copies(next_out, next_far, next_gone, planes_a, 0)
+    for copy in copies[:planes_a]:
+        copy.start()
+    fetched.wait()
     for z in range(planes):
-        left = jnp.concatenate([masked(curve_x[...], planes, z), masked(carry_y, planes, z)], axis=0)
-        right = jnp.concatenate([dot3(carry_x, both_y[z]), curve_y[...]], axis=0)
+        left = stacked(masked(curve_x[...], planes, z), masked(carry_y, planes, z))
+        right = stacked(dot3(carry_x, both_y[z]), curve_y[...])
         before = base[z] + outer(left, right)
         if z < planes_a:
-            next_out[z] = solve(pushed[z], before, both_x[z], both_y[z])
+            next_out[z] = solve(pushed_out[z], before, both_x[z], both_y[z])
+            copies[planes_a + z].start()
         else:
             rest_out[z - planes_a] = before
+    for copy in copies:
+        copy.wait()
 
 
 def far_kernel(first, pushed_in, next_in, base, both_x, both_y, *refs):
     del pushed_in, next_in
-    sums, (pushed_out, next_out) = refs[:-2], refs[-2:]
+    sums, (pushed_far, next_far, pushed_out, next_out, pushed_gone, next_gone) = refs[:-6], refs[-6:]
     count, cells_x, _ = pushed_out.shape
     total = sums[0][...]
     for part in sums[1:]:
         total = total + part[...]
-    pushed = swap_blocks(tile_rows(total, count, cells_x // TS)).reshape(count, cells_x, LANES)
+    pushed_out[...] = swap_blocks(tile_rows(total, count, cells_x // TS)).reshape(count, cells_x, LANES)
+    copies = out_copies(pushed_out, pushed_far, pushed_gone, count, first)
+    copies += out_copies(next_out, next_far, next_gone, count, first)
+    for copy in copies[:count]:
+        copy.start()
     for z in range(count):
-        pushed_out[z] = pushed[z]
-        next_out[z] = solve(pushed[z], base[z], both_x[first + z], both_y[first + z])
+        next_out[z] = solve(pushed_out[z], base[z], both_x[first + z], both_y[first + z])
+        copies[count + z].start()
+    for copy in copies:
+        copy.wait()
 
 
 def call(name, body, out_shape, in_specs=None, scratch=(), wait=(), **extra):
@@ -586,10 +637,20 @@
         [rings[1], packed_b],
     )(at, logs, target_density, table, lines, coef, both_x, ring, tiled)
     edges = [edges[0]] + [turn(edges[o], "z", o) for o in range(1, depth)]
-    sums = call(
-        "partial", functools.partial(partial_kernel, capacity), [array(tile_count, rest * tile_cells)] * depth,
-        None, (),
-    )(arrived_b)
+    sums = {}
+    for groups in [[depth // 2], [r for r in range(depth) if r != depth // 2]]:
+        parts = 2 * rest
+        some = call(
+            "partial", functools.partial(partial_kernel, capacity, depth, groups),
+            [array(tile_count, rest * tile_cells)] * len(groups),
+            [far],
+            [
+                pltpu.VMEM((columns, SUB, LANES), F32),
+                pltpu.VMEM((len(groups), parts, columns, capacity, LANES), F32),
+                pltpu.SemaphoreType.DMA((1 + len(groups) * parts,)),
+            ],
+        )(arrived_b)
+        sums.update(zip(groups, some))
     moving = {r: sums[r] for r in range(depth)}
     for r in range(depth // 2, 0, -1):
         moving[r - 1] = turn(moving[r], "z", -1) if r == 1 else moving[r - 1] + turn(moving[r], "z", -1)
@@ -625,21 +686,22 @@
         out_specs=far, input_output_aliases={1: 0},
     )(at, packed_a, boards, rings[last], *edges)
     arrived_a = lax.all_to_all(packed_a, ("gx", "x"), 0, 0, tiled=True)
-    base = call("base", base_kernel, array(*potential.shape))(
+    base = call("base", base_kernel, array(*potential.shape), wait=[sums[0]])(
         target_density, potential, both_x, both_y
     )
-    field = (planes_a, cells_x, cells_y)
     shapes = [array(*source_mass.shape), array(*potential.shape)]
-    part = pl.BlockSpec(field, lambda i: (0, 0, 0))
+
+    def staged(count):
+        return [pltpu.VMEM((count, cells_x, cells_y), F32)] * 2 + [pltpu.SemaphoreType.DMA((count,))] * 2
+
     *outs, base = call(
-        "near", functools.partial(near_kernel, capacity, depth),
-        shapes + [array(rest, cells_x, cells_y)], None,
-        out_specs=[part, part, near], grid=(1,),
+        "near", functools.partial(near_kernel, capacity, depth), shapes + [array(rest, cells_x, cells_y)],
+        [near, far] + [near] * 4, staged(planes_a) + [pltpu.VMEM(potential.shape, F32), pltpu.SemaphoreType.DMA],
+        out_specs=[far, far, near], input_output_aliases={1: 1},
     )(arrived_a, base, both_x, both_y, curve_x, curve_y)
-    part = pl.BlockSpec(field, lambda i: (1, 0, 0))
     outs = call(
         "far", functools.partial(far_kernel, planes_a), shapes, [far, far] + [near] * (3 + len(moving)),
-        out_specs=[part, part], grid=(1,), input_output_aliases={0: 0, 1: 1},
+        staged(rest), out_specs=[far, far], input_output_aliases={0: 0, 1: 1},
     )(*outs, base, both_x, both_y, *moving)
     return tuple(outs)
 

time: 66.9 us -> 66.2 us (0.990)
  Pallas kernels: 19.4 us -> 21.5 us
  local copies, waits for them, and re-layouts: 3.62 us -> 1.79 us
  waiting for transfers between devices: 11.7 us -> 10.6 us
    pallas_call x10 -> x11, Pallas kernels: 19.4 us -> 21.5 us  [run(): pl.pallas_call(kernel, out_shape=out_shape, in_specs=specs + [pl.BlockSpe...]
    ppermute x9, waiting for transfers between devices: 5.95 us -> 3.91 us  [turn(): return lax.ppermute(x, axis, [(i, (i + steps) % size) for i in range(size)])]
    unnamed x30 -> x26, local copies, waits for them, and re-layouts: 3.62 us -> 1.79 us
    all_to_all x1, waiting for transfers between devices: 5.7 us -> 6.69 us  [per_device(): arrived_a = lax.all_to_all(packed_a, ('gx', 'x'), 0, 0, tiled=True)]
  transfers between devices with their start and end apart: 11 -> 11, of which waited for: 3 -> 3; matrix products, arithmetic and copies ran while one was open for 1% -> 1% of each run, Pallas kernels for 26% -> 29%
where the time goes in v5:
time: 66.2 us; the launch traced here: 65.9 us
  starting transfers between devices  29.5 us (45%)
  Pallas kernels  21.5 us (32%)
  waiting for transfers between devices  10.6 us (16%)
  local copies, waits for them, and re-layouts  1.79 us (3%)
  other arithmetic  1.54 us (2%)
  between operations  0.89 us (1%)
    ppermute x9, starting transfers between devices, turn(): return lax.ppermute(x, axis, [(i, (i + steps) % size) for i in range(size)])  21.7 us
    pallas_call x11, Pallas kernels, run(): pl.pallas_call(kernel, out_shape=out_shape, in_specs=specs + [pl.BlockSpe...  21.5 us
    all_to_all x1, waiting for transfers between devices, per_device(): arrived_a = lax.all_to_all(packed_a, ('gx', 'x'), 0, 0, tiled=True)  6.69 us
    all_to_all x1, starting transfers between devices, per_device(): arrived_b = lax.all_to_all(packed_b, ('gx', 'x'), 0, 0, tiled=True)  4.01 us
    ppermute x9, waiting for transfers between devices, turn(): return lax.ppermute(x, axis, [(i, (i + steps) % size) for i in range(size)])  3.91 us
    all_to_all x1, starting transfers between devices, per_device(): arrived_a = lax.all_to_all(packed_a, ('gx', 'x'), 0, 0, tiled=True)  3.85 us
    unnamed x26, local copies, waits for them, and re-layouts  1.79 us
  transfers between devices with their start and end apart: 11, of which 3 were waited for; matrix products, arithmetic and copies ran while one was open for 1% of the time, Pallas kernels for 29%

profile of v5, /device:TPU:0, one launch (start us, length us, event | category | flops | bytes accessed | tf_op | source)
XLA Modules:
  0.0 65.9 jit_solution(818254014190531137)
XLA Ops:
  0.6 0.7 %add_convert_fusion.refs_1_ = f32[3,4,128]{2,1,0:T(4,128)S(1)} fusion(s32[1,4,128]{2,1,0:T(4,128)} %bitcast.18, s32[1,4,128]{2,1,0:T(4,128)} %bitcast.19, s32[1,4,128]{2,1,0:T(4,128)} %bitcast.20), kind=kLoop, calls=%fused_computation | loop fusion | flops 4608 | bytes 12288 | tf_op jit(solution)/shard_map/convert_element_type | solution.py:603
  1.4 1.0 %copy-done = f32[4,256,128]{2,1,0:T(8,128)S(1)} copy-done((f32[4,256,128]{2,1,0:T(8,128)S(1)}, f32[4,256,128]{2,1,0:T(8,128)}, u32[]{:S(2)}) %copy-start) | copy-done | bytes 524312
  2.4 0.8 %shard_map.86 = (f32[536,128]{1,0:T(8,128)S(1)}, f32[512,128]{1,0:T(8,128)S(1)}) custom-call(f32[4,256,128]{2,1,0:T(8,128)S(1)} %copy-done, f32[3,4,128]{2,1,0:T(4,128)S(1)} %add_convert_fusion.refs_1_), custom_call_target="tpu_custom_call" | custom-call | flops 880000000 | tf_op jit(solution)/shard_map/pallas_call | solution.py:516
  3.1 3.1 %collective-permute-start = (f32[536,128]{1,0:T(8,128)S(1)}, f32[536,128]{1,0:T(8,128)S(1)}, u32[]{:S(2)}, u32[]{:S(2)}) collective-permute-start(f32[536,128]{1,0:T(8,128)S(1)} %get-tuple-element.23.refs_1_.refs_2_.refs_7_), channel_id=1, source_target_pairs={{0,2},{2,4},{4,6},{6,0},{1,3},{3,5},{5,7},{7,1},{8,10},{10,12},{12... | collective-permute-start | bytes 823304 | tf_op jit(solution)/shard_map/ppermute | solution.py:597
  6.2 2.1 %collective-permute-start.1 = (f32[536,128]{1,0:T(8,128)S(1)}, f32[536,128]{1,0:T(8,128)S(1)}, u32[]{:S(2)}, u32[]{:S(2)}) collective-permute-start(f32[536,128]{1,0:T(8,128)S(1)} %get-tuple-element.23.refs_1_.refs_2_.refs_7_), channel_id=1, source_target_pairs={{0,6},{2,0},{4,2},{6,4},{1,7},{3,1},{5,3},{7,5},{8,14},{10,8},{12,... | collective-permute-start | bytes 823304 | tf_op jit(solution)/shard_map/ppermute | solution.py:597
  8.3 0.1 pad_add_fusion.refs_0_
  8.4 2.5 %shard_map.89.refs_10_ = f32[8,392,128]{2,1,0:T(8,128)} custom-call(s32[3]{0:T(128)S(1)} %pad_add_fusion.refs_0_, f32[536,128]{1,0:T(8,128)S(1)} %get-tuple-element.23.refs_1_.refs_2_.refs_7_, f32[512,128]{1,0:T(8,128)S(1)} %get-tuple-element.30.refs_2_.refs_8_), custom_call_target="tpu_custom_call" | custom-call | flops 2750000128 | tf_op jit(solution)/shard_map/pallas_call | solution.py:516
  10.9 4.0 %all-to-all-start.1 = ((f32[8,392,128]{2,1,0:T(8,128)}), f32[8,392,128]{2,1,0:T(8,128)S(1)}, u32[]{:S(2)}, u32[]{:S(2)}) async-start(f32[8,392,128]{2,1,0:T(8,128)} %shard_map.89.refs_10_), calls=%async_computation.1 | async-start | bytes 3211264 | tf_op jit(solution)/shard_map/all_to_all | solution.py:616
  14.9 1.2 %shard_map.88 = (f32[1024,256]{1,0:T(8,128)S(1)}, f32[4,8,256]{2,1,0:T(8,128)S(1)}, f32[7,8,128]{2,1,0:T(8,128)S(1)}, f32[8,256]{1,0:T(8,128)S(1)}, f32[8,128]{1...) custom-call(f32[4]{0:T(128)S(1)} %get-tuple-element.45.refs_0_, f32[4]{0:T(128)S(1)} %get-tuple-element.44.refs_1_, ...), custom_call_target="tpu_custom_call" | custom-call | flops 22000001024 | tf_op jit(solution)/shard_map/pallas_call | solution.py:516
  16.1 0.0 copy-start.7
  16.1 0.7 %copy-done.7 = f32[4,128,128]{2,1,0:T(8,128)} copy-done((f32[4,128,128]{2,1,0:T(8,128)}, f32[4,128,128]{2,1,0:T(8,128)S(1)}, u32[]{:S(2)}) %copy-start.7) | copy-done | bytes 262168
  16.8 4.4 %shard_map.90 = (f32[8,24,128]{2,1,0:T(8,128)S(1)}, f32[8,24,128]{2,1,0:T(8,128)S(1)}, f32[8,24,128]{2,1,0:T(8,128)S(1)}, f32[8,24,128]{2,1,0:T(8,128)S(1)}) custom-call(s32[3]{0:T(128)S(1)} %pad_add_fusion.refs_0_, f32[4]{0:T(128)S(1)} %get-tuple-element.44.refs_1_, f32[4,256,128]{2,1,0:T(8,128)S(1)} %copy-done.1, ...), custom_call_target="tpu_custom_call" | custom-call | flops 65999998976 | tf_op jit(solution)/shard_map/pallas_call | solution.py:516
  21.3 5.1 %collective-permute-start.3 = (f32[8,24,128]{2,1,0:T(8,128)S(1)}, f32[8,24,128]{2,1,0:T(8,128)S(1)}, u32[]{:S(2)}, u32[]{:S(2)}) collective-permute-start(f32[8,24,128]{2,1,0:T(8,128)S(1)} %get-tuple-element.32), channel_id=1, source_target_pairs={{0,2},{2,4},{4,6},{6,0},{1,3},{3,5},{5,7},{7,1},{8,10},{10,12},{12... | collective-permute-start | bytes 294920 | tf_op jit(solution)/shard_map/ppermute | solution.py:597
  26.3 1.2 %collective-permute-start.4 = (f32[8,24,128]{2,1,0:T(8,128)S(1)}, f32[8,24,128]{2,1,0:T(8,128)S(1)}, u32[]{:S(2)}, u32[]{:S(2)}) collective-permute-start(f32[8,24,128]{2,1,0:T(8,128)S(1)} %get-tuple-element.33), channel_id=1, source_target_pairs={{0,4},{2,6},{4,0},{6,2},{1,5},{3,7},{5,1},{7,3},{8,12},{10,14},{12... | collective-permute-start | bytes 294920 | tf_op jit(solution)/shard_map/ppermute | solution.py:597
  27.5 2.8 %collective-permute-start.5 = (f32[8,24,128]{2,1,0:T(8,128)S(1)}, f32[8,24,128]{2,1,0:T(8,128)S(1)}, u32[]{:S(2)}, u32[]{:S(2)}) collective-permute-start(f32[8,24,128]{2,1,0:T(8,128)S(1)} %get-tuple-element.34), channel_id=1, source_target_pairs={{0,6},{2,0},{4,2},{6,4},{1,7},{3,1},{5,3},{7,5},{8,14},{10,8},{12,... | collective-permute-start | bytes 294920 | tf_op jit(solution)/shard_map/ppermute | solution.py:597
  30.4 2.5 %shard_map.87 = (f32[8,416,128]{2,1,0:T(8,128)}, f32[8,8,128]{2,1,0:T(8,128)S(1)}) custom-call(s32[3]{0:T(128)S(1)} %pad_add_fusion.refs_0_, f32[536,128]{1,0:T(8,128)S(1)} %get-tuple-element.23.refs_1_.refs_2_.refs_7_, f32[536,128]{1,0:T(8,128)S(1)} %collective-permute-done.refs_2_.refs_9_, f32[536,128]{1,0:T(8,128)S(1)} %collective-permute-done.1.refs_3_), custom_call_target="tpu_custom_call" | custom-call | flops 1980000000 | tf_op jit(solution)/shard_map/pallas_call | solution.py:516
  32.9 1.2 %collective-permute-done.4.refs_6_ = f32[8,24,128]{2,1,0:T(8,128)S(1)} collective-permute-done((f32[8,24,128]{2,1,0:T(8,128)S(1)}, f32[8,24,128]{2,1,0:T(8,128)S(1)}, u32[]{:S(2)}, u32[]{:S(2)}) %collective-permute-start.4) | collective-permute-done | bytes 98336 | tf_op jit(solution)/shard_map/ppermute | solution.py:597
  34.1 1.9 %shard_map.91 = f32[8,416,128]{2,1,0:T(8,128)} custom-call(s32[3]{0:T(128)S(1)} %pad_add_fusion.refs_0_, f32[8,416,128]{2,1,0:T(8,128)} %get-tuple-element.24.refs_1_, f32[8,8,128]{2,1,0:T(8,128)S(1)} %get-tuple-element.25.refs_2_, f32[536,128]{1,0:T(8,128)S(1)} %collective-permute-done.2.refs_3_, ...), custom_call_target="tpu_custom_call", output_to_operand_aliasing={{}: (1, {})} | custom-call | flops 1980000000 | tf_op jit(solution)/shard_map/pallas_call | solution.py:516
  36.0 3.8 %all-to-all-start = ((f32[8,416,128]{2,1,0:T(8,128)}), f32[8,416,128]{2,1,0:T(8,128)S(1)}, u32[]{:S(2)}, u32[]{:S(2)}) async-start(f32[8,416,128]{2,1,0:T(8,128)} %shard_map.91), calls=%async_computation | async-start | bytes 3407872 | tf_op jit(solution)/shard_map/all_to_all | solution.py:688
  39.8 0.5 shard_map.95
  40.3 0.0 copy-start.3
  40.3 0.0 copy-start.8
  40.3 3.1 %collective-permute-start.6 = (f32[128,512]{1,0:T(8,128)S(1)}, f32[128,512]{1,0:T(8,128)S(1)}, u32[]{:S(2)}, u32[]{:S(2)}) collective-permute-start(f32[128,512]{1,0:T(8,128)S(1)} %shard_map.95), channel_id=1, source_target_pairs={{0,6},{2,0},{4,2},{6,4},{1,7},{3,1},{5,3},{7,5},{8,14},{10,8},{12,... | collective-permute-start | bytes 786440 | tf_op jit(solution)/shard_map/ppermute | solution.py:597
  43.4 2.1 %shard_map.92 = (f32[128,512]{1,0:T(8,128)S(1)}, f32[128,512]{1,0:T(8,128)S(1)}, f32[128,512]{1,0:T(8,128)}) custom-call(f32[8,392,128]{2,1,0:T(8,128)S(1)} %all-to-all-done.1.refs_0_), custom_call_target="tpu_custom_call" | custom-call | flops 1540000000 | tf_op jit(solution)/shard_map/pallas_call | solution.py:516
  45.5 0.1 collective-permute-start.8
  45.6 1.8 %shard_map.93.refs_1_ = f32[4,256,128]{2,1,0:T(8,128)} custom-call(f32[4,256,128]{2,1,0:T(8,128)S(1)} %copy-done.2, f32[4,256,128]{2,1,0:T(8,128)S(1)} %copy-done.3, f32[4,256,256]{2,1,0:T(8,128)S(1)} %copy-done.5, f32[4,128,128]{2,1,0:T(8,128)S(1)} %copy-done.8, f32[128,512]{1,0:T(8,128)S(1)} %get-tuple-element.36.refs_4_.refs_5_), custom_call_target="tpu_custom_call" | custom-call | flops 1100000000 | tf_op jit(solution)/shard_map/pallas_call | solution.py:516
  47.4 2.7 %collective-permute-done.6 = f32[128,512]{1,0:T(8,128)S(1)} collective-permute-done((f32[128,512]{1,0:T(8,128)S(1)}, f32[128,512]{1,0:T(8,128)S(1)}, u32[]{:S(2)}, u32[]{:S(2)}) %collective-permute-start.6) | collective-permute-done | bytes 262176 | tf_op jit(solution)/shard_map/ppermute | solution.py:597
  50.1 0.7 %add.3 = f32[128,512]{1,0:T(8,128)} add(f32[128,512]{1,0:T(8,128)S(1)} %get-tuple-element.42, f32[128,512]{1,0:T(8,128)S(1)} %collective-permute-done.6) | non-fusion elementwise | flops 65536 | bytes 786432 | tf_op jit(solution)/shard_map/add | solution.py:656
  50.8 4.3 %collective-permute-start.7 = (f32[128,512]{1,0:T(8,128)}, f32[128,512]{1,0:T(8,128)S(1)}, u32[]{:S(2)}, u32[]{:S(2)}) collective-permute-start(f32[128,512]{1,0:T(8,128)} %add.3), channel_id=1, source_target_pairs={{0,6},{2,0},{4,2},{6,4},{1,7},{3,1},{5,3},{7,5},{8,14},{10,8},{12,... | collective-permute-start | bytes 786440 | tf_op jit(solution)/shard_map/ppermute | solution.py:597
  55.1 6.7 %all-to-all-done.refs_0_ = f32[8,416,128]{2,1,0:T(8,128)S(1)} async-done(((f32[8,416,128]{2,1,0:T(8,128)}), f32[8,416,128]{2,1,0:T(8,128)S(1)}, u32[]{:S(2)}, u32[]{:S(2)}) %all-to-all-start) | async-done | bytes 1703968 | tf_op jit(solution)/shard_map/all_to_all | solution.py:688
  61.8 2.5 %shard_map.94 = (f32[4,256,128]{2,1,0:T(8,128)}, f32[4,256,128]{2,1,0:T(8,128)}, f32[2,256,128]{2,1,0:T(8,128)S(1)}) custom-call(f32[8,416,128]{2,1,0:T(8,128)S(1)} %all-to-all-done.refs_0_, f32[4,256,128]{2,1,0:T(8,128)} %shard_map.93.refs_1_, f32[4,256,256]{2,1,0:T(8,128)S(1)} %copy-done.6, ...), custom_call_target="tpu_custom_call", output_to_operand_aliasing={{1}: (1, {})} | custom-call | flops 3849999872 | tf_op jit(solution)/shard_map/pallas_call | solution.py:516
  64.3 1.6 %shard_map.96 = (f32[4,256,128]{2,1,0:T(8,128)}, f32[4,256,128]{2,1,0:T(8,128)}) custom-call(f32[4,256,128]{2,1,0:T(8,128)} %get-tuple-element.39.refs_0_, f32[4,256,128]{2,1,0:T(8,128)} %get-tuple-element.40.refs_1_, f32[2,256,128]{2,1,0:T(8,128)S(1)} %get-tuple-element.41.refs_2_, ...), custom_call_target="tpu_custom_call", output_to_operand_aliasing={{0}: (0, {}), {1}: (1, {})} | custom-call | flops 1760000000 | tf_op jit(solution)/shard_map/pallas_call | solution.py:516
  (31 shorter events, 0.1 us)
Async XLA Ops:
  1.3 1.0 %copy-start = (f32[4,256,128]{2,1,0:T(8,128)S(1)}, f32[4,256,128]{2,1,0:T(8,128)}, u32[]{:S(2)}) copy-start(f32[4,256,128]{2,1,0:T(8,128)} %refs_0_.2) | copy-start | bytes 1572868
  3.1 13.7 %collective-permute-start = (f32[536,128]{1,0:T(8,128)S(1)}, f32[536,128]{1,0:T(8,128)S(1)}, u32[]{:S(2)}, u32[]{:S(2)}) collective-permute-start(f32[536,128]{1,0:T(8,128)S(1)} %get-tuple-element.23.refs_1_.refs_2_.refs_7_), channel_id=1, source_target_pairs={{0,2},{2,4},{4,6},{6,0},{1,3},{3,5},{5,7},{7,1},{8,10},{10,12},{12... | collective-permute-start | bytes 823304 | tf_op jit(solution)/shard_map/ppermute | solution.py:597
  6.2 24.2 %collective-permute-start.1 = (f32[536,128]{1,0:T(8,128)S(1)}, f32[536,128]{1,0:T(8,128)S(1)}, u32[]{:S(2)}, u32[]{:S(2)}) collective-permute-start(f32[536,128]{1,0:T(8,128)S(1)} %get-tuple-element.23.refs_1_.refs_2_.refs_7_), channel_id=1, source_target_pairs={{0,6},{2,0},{4,2},{6,4},{1,7},{3,1},{5,3},{7,5},{8,14},{10,8},{12,... | collective-permute-start | bytes 823304 | tf_op jit(solution)/shard_map/ppermute | solution.py:597
  10.9 4.0 %copy-start.12 = (f32[4]{0:T(128)S(1)}, f32[4]{0:T(128)}, u32[]{:S(2)}) copy-start(f32[4]{0:T(128)} %param.13) | copy-start | bytes 52
  10.9 25.1 %all-to-all-start.1 = ((f32[8,392,128]{2,1,0:T(8,128)}), f32[8,392,128]{2,1,0:T(8,128)S(1)}, u32[]{:S(2)}, u32[]{:S(2)}) async-start(f32[8,392,128]{2,1,0:T(8,128)} %shard_map.89.refs_10_), calls=%async_computation.1 | async-start | bytes 3211264 | tf_op jit(solution)/shard_map/all_to_all | solution.py:616
  14.9 1.9 %copy-start.1 = (f32[4,256,128]{2,1,0:T(8,128)S(1)}, f32[4,256,128]{2,1,0:T(8,128)}, u32[]{:S(2)}) copy-start(f32[4,256,128]{2,1,0:T(8,128)} %refs_0_.3) | copy-start | bytes 1572868
  16.1 0.7 %copy-start.7 = (f32[4,128,128]{2,1,0:T(8,128)}, f32[4,128,128]{2,1,0:T(8,128)S(1)}, u32[]{:S(2)}) copy-start(f32[4,128,128]{2,1,0:T(8,128)S(1)} %get-tuple-element.35.refs_3_.refs_4_) | copy-start | bytes 786436
  16.8 4.4 %copy-start.4 = (f32[4,256,256]{2,1,0:T(8,128)}, f32[4,256,256]{2,1,0:T(8,128)S(1)}, u32[]{:S(2)}) copy-start(f32[4,256,256]{2,1,0:T(8,128)S(1)} %get-tuple-element.29.refs_6_.refs_2_.refs_3_) | copy-start | bytes 3145732
  16.8 17.3 %collective-permute-start.2 = (f32[536,128]{1,0:T(8,128)S(1)}, f32[536,128]{1,0:T(8,128)S(1)}, u32[]{:S(2)}, u32[]{:S(2)}) collective-permute-start(f32[536,128]{1,0:T(8,128)S(1)} %collective-permute-done.refs_2_.refs_9_), channel_id=1, source_target_pairs={{0,2},{2,4},{4,6},{6,0},{1,3},{3,5},{5,7},{7,1},{8,10},{10,12},{12... | collective-permute-start | bytes 823304 | tf_op jit(solution)/shard_map/ppermute | solution.py:597
  21.3 11.6 %collective-permute-start.3 = (f32[8,24,128]{2,1,0:T(8,128)S(1)}, f32[8,24,128]{2,1,0:T(8,128)S(1)}, u32[]{:S(2)}, u32[]{:S(2)}) collective-permute-start(f32[8,24,128]{2,1,0:T(8,128)S(1)} %get-tuple-element.32), channel_id=1, source_target_pairs={{0,2},{2,4},{4,6},{6,0},{1,3},{3,5},{5,7},{7,1},{8,10},{10,12},{12... | collective-permute-start | bytes 294920 | tf_op jit(solution)/shard_map/ppermute | solution.py:597
  26.3 7.8 %collective-permute-start.4 = (f32[8,24,128]{2,1,0:T(8,128)S(1)}, f32[8,24,128]{2,1,0:T(8,128)S(1)}, u32[]{:S(2)}, u32[]{:S(2)}) collective-permute-start(f32[8,24,128]{2,1,0:T(8,128)S(1)} %get-tuple-element.33), channel_id=1, source_target_pairs={{0,4},{2,6},{4,0},{6,2},{1,5},{3,7},{5,1},{7,3},{8,12},{10,14},{12... | collective-permute-start | bytes 294920 | tf_op jit(solution)/shard_map/ppermute | solution.py:597
  27.5 6.6 %collective-permute-start.5 = (f32[8,24,128]{2,1,0:T(8,128)S(1)}, f32[8,24,128]{2,1,0:T(8,128)S(1)}, u32[]{:S(2)}, u32[]{:S(2)}) collective-permute-start(f32[8,24,128]{2,1,0:T(8,128)S(1)} %get-tuple-element.34), channel_id=1, source_target_pairs={{0,6},{2,0},{4,2},{6,4},{1,7},{3,1},{5,3},{7,5},{8,14},{10,8},{12,... | collective-permute-start | bytes 294920 | tf_op jit(solution)/shard_map/ppermute | solution.py:597
  36.0 25.8 %all-to-all-start = ((f32[8,416,128]{2,1,0:T(8,128)}), f32[8,416,128]{2,1,0:T(8,128)S(1)}, u32[]{:S(2)}, u32[]{:S(2)}) async-start(f32[8,416,128]{2,1,0:T(8,128)} %shard_map.91), calls=%async_computation | async-start | bytes 3407872 | tf_op jit(solution)/shard_map/all_to_all | solution.py:688
  40.3 5.3 %copy-start.2 = (f32[4,256,128]{2,1,0:T(8,128)S(1)}, f32[4,256,128]{2,1,0:T(8,128)}, u32[]{:S(2)}) copy-start(f32[4,256,128]{2,1,0:T(8,128)} %refs_0_.3) | copy-start | bytes 1572868
  40.3 5.3 %copy-start.3 = (f32[4,256,128]{2,1,0:T(8,128)S(1)}, f32[4,256,128]{2,1,0:T(8,128)}, u32[]{:S(2)}) copy-start(f32[4,256,128]{2,1,0:T(8,128)} %refs_1_.1) | copy-start | bytes 1572868
  40.3 5.2 %copy-start.5 = (f32[4,256,256]{2,1,0:T(8,128)S(1)}, f32[4,256,256]{2,1,0:T(8,128)}, u32[]{:S(2)}) copy-start(f32[4,256,256]{2,1,0:T(8,128)} %copy-done.4) | copy-start | bytes 3145732
  40.3 5.2 %copy-start.8 = (f32[4,128,128]{2,1,0:T(8,128)S(1)}, f32[4,128,128]{2,1,0:T(8,128)}, u32[]{:S(2)}) copy-start(f32[4,128,128]{2,1,0:T(8,128)} %copy-done.7) | copy-start | bytes 786436
  40.3 9.7 %collective-permute-start.6 = (f32[128,512]{1,0:T(8,128)S(1)}, f32[128,512]{1,0:T(8,128)S(1)}, u32[]{:S(2)}, u32[]{:S(2)}) collective-permute-start(f32[128,512]{1,0:T(8,128)S(1)} %shard_map.95), channel_id=1, source_target_pairs={{0,6},{2,0},{4,2},{6,4},{1,7},{3,1},{5,3},{7,5},{8,14},{10,8},{12,... | collective-permute-start | bytes 786440 | tf_op jit(solution)/shard_map/ppermute | solution.py:597
  45.5 1.9 %copy-start.10 = (f32[128,512]{1,0:T(8,128)}, f32[128,512]{1,0:T(8,128)S(1)}, u32[]{:S(2)}) copy-start(f32[128,512]{1,0:T(8,128)S(1)} %get-tuple-element.36.refs_4_.refs_5_) | copy-start | bytes 786436
  45.5 18.8 %collective-permute-start.8 = (f32[128,512]{1,0:T(8,128)}, f32[128,512]{1,0:T(8,128)S(1)}, u32[]{:S(2)}, u32[]{:S(2)}) collective-permute-start(f32[128,512]{1,0:T(8,128)} %get-tuple-element.43), channel_id=1, source_target_pairs={{0,2},{2,4},{4,6},{6,0},{1,3},{3,5},{5,7},{7,1},{8,10},{10,12},{12... | collective-permute-start | bytes 786440 | tf_op jit(solution)/shard_map/ppermute | solution.py:597
  45.6 16.2 %copy-start.6 = (f32[4,256,256]{2,1,0:T(8,128)S(1)}, f32[4,256,256]{2,1,0:T(8,128)}, u32[]{:S(2)}) copy-start(f32[4,256,256]{2,1,0:T(8,128)} %copy-done.4) | copy-start | bytes 3145732
  45.6 16.2 %copy-start.9 = (f32[4,128,128]{2,1,0:T(8,128)S(1)}, f32[4,128,128]{2,1,0:T(8,128)}, u32[]{:S(2)}) copy-start(f32[4,128,128]{2,1,0:T(8,128)} %copy-done.7) | copy-start | bytes 786436
  50.8 13.5 %collective-permute-start.7 = (f32[128,512]{1,0:T(8,128)}, f32[128,512]{1,0:T(8,128)S(1)}, u32[]{:S(2)}, u32[]{:S(2)}) collective-permute-start(f32[128,512]{1,0:T(8,128)} %add.3), channel_id=1, source_target_pairs={{0,6},{2,0},{4,2},{6,4},{1,7},{3,1},{5,3},{7,5},{8,14},{10,8},{12,... | collective-permute-start | bytes 786440 | tf_op jit(solution)/shard_map/ppermute | solution.py:597
  61.8 2.5 %copy-start.11 = (f32[128,512]{1,0:T(8,128)S(1)}, f32[128,512]{1,0:T(8,128)}, u32[]{:S(2)}) copy-start(f32[128,512]{1,0:T(8,128)} %copy-done.10) | copy-start | bytes 786436

commit v6 on v5

--- a/solution.py
+++ b/solution.py
@@ -10,6 +10,7 @@
 
 TS = 16
 MXU = 256
+CHUNKS = 8
 SUB = 8
 LANES = 128
 F32 = jnp.float32
@@ -158,25 +159,34 @@
     tiled[...] = swap_blocks(source[planes_a:].reshape(tiled.shape[0], LANES))
 
 
-def start_kernel(capacity, columns, depth, inner, planes_a, fanout, at, ring, tiled, pack_out, picked):
+def start_kernel(capacity, columns, depth, inner, planes_a, fanout, at, ring, tiled, far, out, gone):
     cells_x = (ring.shape[0] - 3 * SUB) // planes_a
     rest = tiled.shape[0] // cells_x
     names, tiles, shares = routing(ring, fanout)
     wanted = columns_wanted((columns * depth, LANES), depth, inner, at[1], None)
     member, weight, label = route_rows(names, tiles, shares, wanted)
     rank = ranked(member)
-    named = []
-    for n in range(columns * depth):
-        rows, labels = slots_of(rank[n:n + 1], weight[n:n + 1], label[n:n + 1], capacity)
-        picked[n * capacity:(n + 1) * capacity, :] = rows
-        named.append(labels)
-    named = in_all_lanes(stacked(*named))
+    cells = tile_columns(tiled[...], rest, cells_x // TS)
     slots = depth * capacity
-    for j in range(columns):
-        board = jnp.zeros((SUB, LANES), F32)
-        pack_out[j, pack_out.shape[1] - SUB:, :] = place_labels(board, named[j * slots:(j + 1) * slots], 0)
-    packed = dot3(picked[...], tile_columns(tiled[...], rest, cells_x // TS))
-    put(pack_out, packed.reshape(columns, depth * capacity, packed.shape[1]))
+    step = columns // gone.shape[0]
+    copies = []
+    for first in range(0, columns, step):
+        picked, named = [], []
+        for n in range(first * depth, (first + step) * depth):
+            rows, labels = slots_of(rank[n:n + 1], weight[n:n + 1], label[n:n + 1], capacity)
+            picked.append(rows)
+            named.append(labels)
+        packed = dot3(stacked(*picked), cells)
+        named = in_all_lanes(stacked(*named))
+        put(out.at[first:first + step], packed.reshape(step, slots, packed.shape[1]))
+        for j in range(step):
+            board = jnp.zeros((SUB, LANES), F32)
+            out[first + j, out.shape[1] - SUB:, :] = place_labels(board, named[j * slots:(j + 1) * slots], 0)
+        there = slice(first, first + step)
+        copies.append(pltpu.make_async_copy(out.at[there], far.at[there], gone.at[first // step]))
+        copies[-1].start()
+    for copy in copies:
+        copy.wait()
 
 
 def put(out, slots, first=0, size=None):
@@ -611,7 +621,11 @@
         "start", functools.partial(start_kernel, capacity, columns, depth, inner, planes_a, fanout),
         array(columns, 2 * rest * slots + SUB, LANES),
         [scalars] + [near] * 2,
-        [pltpu.VMEM((columns * depth * capacity, tile_count), F32)],
+        [
+            pltpu.VMEM((columns, 2 * rest * slots + SUB, LANES), F32),
+            pltpu.SemaphoreType.DMA((CHUNKS if columns % CHUNKS == 0 else 1,)),
+        ],
+        out_specs=far,
     )(at, ring, tiled)
     arrived_b = lax.all_to_all(packed_b, ("gx", "x"), 0, 0, tiled=True)
     decay = 1.0 - 1.0 / reach

time: 66.2 us -> 65.8 us (level)
  no operation moved by 1% of the time
where the time goes in v6:
time: 65.8 us; the launch traced here: 65.4 us
  starting transfers between devices  29.5 us (45%)
  Pallas kernels  21.2 us (32%)
  waiting for transfers between devices  10.6 us (16%)
  local copies, waits for them, and re-layouts  1.8 us (3%)
  other arithmetic  1.54 us (2%)
  between operations  0.9 us (1%)
    ppermute x9, starting transfers between devices, turn(): return lax.ppermute(x, axis, [(i, (i + steps) % size) for i in range(size)])  21.7 us
    pallas_call x11, Pallas kernels, run(): pl.pallas_call(kernel, out_shape=out_shape, in_specs=specs + [pl.BlockSpe...  21.2 us
    all_to_all x1, waiting for transfers between devices, per_device(): arrived_a = lax.all_to_all(packed_a, ('gx', 'x'), 0, 0, tiled=True)  6.65 us
    ppermute x9, waiting for transfers between devices, turn(): return lax.ppermute(x, axis, [(i, (i + steps) % size) for i in range(size)])  3.9 us
    all_to_all x1, starting transfers between devices, per_device(): arrived_b = lax.all_to_all(packed_b, ('gx', 'x'), 0, 0, tiled=True)  3.89 us
    all_to_all x1, starting transfers between devices, per_device(): arrived_a = lax.all_to_all(packed_a, ('gx', 'x'), 0, 0, tiled=True)  3.86 us
    unnamed x26, local copies, waits for them, and re-layouts  1.8 us
  transfers between devices with their start and end apart: 11, of which 3 were waited for; matrix products, arithmetic and copies ran while one was open for 1% of the time, Pallas kernels for 29%

profile of v6, /device:TPU:0, one launch (start us, length us, event | category | flops | bytes accessed | tf_op | source)
XLA Modules:
  0.0 65.4 jit_solution(17642936875822937391)
XLA Ops:
  0.6 0.7 %add_convert_fusion.refs_1_ = f32[3,4,128]{2,1,0:T(4,128)S(1)} fusion(s32[1,4,128]{2,1,0:T(4,128)} %bitcast.18, s32[1,4,128]{2,1,0:T(4,128)} %bitcast.19, s32[1,4,128]{2,1,0:T(4,128)} %bitcast.20), kind=kLoop, calls=%fused_computation | loop fusion | flops 4608 | bytes 12288 | tf_op jit(solution)/shard_map/convert_element_type | solution.py:613
  1.4 1.0 %copy-done = f32[4,256,128]{2,1,0:T(8,128)S(1)} copy-done((f32[4,256,128]{2,1,0:T(8,128)S(1)}, f32[4,256,128]{2,1,0:T(8,128)}, u32[]{:S(2)}) %copy-start) | copy-done | bytes 524312
  2.4 0.8 %shard_map.86 = (f32[536,128]{1,0:T(8,128)S(1)}, f32[512,128]{1,0:T(8,128)S(1)}) custom-call(f32[4,256,128]{2,1,0:T(8,128)S(1)} %copy-done, f32[3,4,128]{2,1,0:T(4,128)S(1)} %add_convert_fusion.refs_1_), custom_call_target="tpu_custom_call" | custom-call | flops 880000000 | tf_op jit(solution)/shard_map/pallas_call | solution.py:526
  3.1 3.1 %collective-permute-start = (f32[536,128]{1,0:T(8,128)S(1)}, f32[536,128]{1,0:T(8,128)S(1)}, u32[]{:S(2)}, u32[]{:S(2)}) collective-permute-start(f32[536,128]{1,0:T(8,128)S(1)} %get-tuple-element.23.refs_1_.refs_2_.refs_7_), channel_id=1, source_target_pairs={{0,2},{2,4},{4,6},{6,0},{1,3},{3,5},{5,7},{7,1},{8,10},{10,12},{12... | collective-permute-start | bytes 823304 | tf_op jit(solution)/shard_map/ppermute | solution.py:607
  6.2 2.1 %collective-permute-start.1 = (f32[536,128]{1,0:T(8,128)S(1)}, f32[536,128]{1,0:T(8,128)S(1)}, u32[]{:S(2)}, u32[]{:S(2)}) collective-permute-start(f32[536,128]{1,0:T(8,128)S(1)} %get-tuple-element.23.refs_1_.refs_2_.refs_7_), channel_id=1, source_target_pairs={{0,6},{2,0},{4,2},{6,4},{1,7},{3,1},{5,3},{7,5},{8,14},{10,8},{12,... | collective-permute-start | bytes 823304 | tf_op jit(solution)/shard_map/ppermute | solution.py:607
  8.3 0.1 pad_add_fusion.refs_0_
  8.4 2.2 %shard_map.89.refs_10_ = f32[8,392,128]{2,1,0:T(8,128)} custom-call(s32[3]{0:T(128)S(1)} %pad_add_fusion.refs_0_, f32[536,128]{1,0:T(8,128)S(1)} %get-tuple-element.23.refs_1_.refs_2_.refs_7_, f32[512,128]{1,0:T(8,128)S(1)} %get-tuple-element.30.refs_2_.refs_8_), custom_call_target="tpu_custom_call" | custom-call | flops 2750000128 | tf_op jit(solution)/shard_map/pallas_call | solution.py:526
  10.6 0.0 copy-start.12
  10.6 3.9 %all-to-all-start.1 = ((f32[8,392,128]{2,1,0:T(8,128)}), f32[8,392,128]{2,1,0:T(8,128)S(1)}, u32[]{:S(2)}, u32[]{:S(2)}) async-start(f32[8,392,128]{2,1,0:T(8,128)} %shard_map.89.refs_10_), calls=%async_computation.1 | async-start | bytes 3211264 | tf_op jit(solution)/shard_map/all_to_all | solution.py:630
  14.5 0.0 copy-start.1
  14.5 1.2 %shard_map.88 = (f32[1024,256]{1,0:T(8,128)S(1)}, f32[4,8,256]{2,1,0:T(8,128)S(1)}, f32[7,8,128]{2,1,0:T(8,128)S(1)}, f32[8,256]{1,0:T(8,128)S(1)}, f32[8,128]{1...) custom-call(f32[4]{0:T(128)S(1)} %get-tuple-element.45.refs_0_, f32[4]{0:T(128)S(1)} %get-tuple-element.44.refs_1_, ...), custom_call_target="tpu_custom_call" | custom-call | flops 22000001024 | tf_op jit(solution)/shard_map/pallas_call | solution.py:526
  15.7 0.7 %copy-done.7 = f32[4,128,128]{2,1,0:T(8,128)} copy-done((f32[4,128,128]{2,1,0:T(8,128)}, f32[4,128,128]{2,1,0:T(8,128)S(1)}, u32[]{:S(2)}) %copy-start.7) | copy-done | bytes 262168
  16.4 4.4 %shard_map.90 = (f32[8,24,128]{2,1,0:T(8,128)S(1)}, f32[8,24,128]{2,1,0:T(8,128)S(1)}, f32[8,24,128]{2,1,0:T(8,128)S(1)}, f32[8,24,128]{2,1,0:T(8,128)S(1)}) custom-call(s32[3]{0:T(128)S(1)} %pad_add_fusion.refs_0_, f32[4]{0:T(128)S(1)} %get-tuple-element.44.refs_1_, f32[4,256,128]{2,1,0:T(8,128)S(1)} %copy-done.1, ...), custom_call_target="tpu_custom_call" | custom-call | flops 65999998976 | tf_op jit(solution)/shard_map/pallas_call | solution.py:526
  20.8 5.0 %collective-permute-start.3 = (f32[8,24,128]{2,1,0:T(8,128)S(1)}, f32[8,24,128]{2,1,0:T(8,128)S(1)}, u32[]{:S(2)}, u32[]{:S(2)}) collective-permute-start(f32[8,24,128]{2,1,0:T(8,128)S(1)} %get-tuple-element.32), channel_id=1, source_target_pairs={{0,2},{2,4},{4,6},{6,0},{1,3},{3,5},{5,7},{7,1},{8,10},{10,12},{12... | collective-permute-start | bytes 294920 | tf_op jit(solution)/shard_map/ppermute | solution.py:607
  25.9 1.2 %collective-permute-start.4 = (f32[8,24,128]{2,1,0:T(8,128)S(1)}, f32[8,24,128]{2,1,0:T(8,128)S(1)}, u32[]{:S(2)}, u32[]{:S(2)}) collective-permute-start(f32[8,24,128]{2,1,0:T(8,128)S(1)} %get-tuple-element.33), channel_id=1, source_target_pairs={{0,4},{2,6},{4,0},{6,2},{1,5},{3,7},{5,1},{7,3},{8,12},{10,14},{12... | collective-permute-start | bytes 294920 | tf_op jit(solution)/shard_map/ppermute | solution.py:607
  27.1 2.8 %collective-permute-start.5 = (f32[8,24,128]{2,1,0:T(8,128)S(1)}, f32[8,24,128]{2,1,0:T(8,128)S(1)}, u32[]{:S(2)}, u32[]{:S(2)}) collective-permute-start(f32[8,24,128]{2,1,0:T(8,128)S(1)} %get-tuple-element.34), channel_id=1, source_target_pairs={{0,6},{2,0},{4,2},{6,4},{1,7},{3,1},{5,3},{7,5},{8,14},{10,8},{12,... | collective-permute-start | bytes 294920 | tf_op jit(solution)/shard_map/ppermute | solution.py:607
  30.0 2.5 %shard_map.87 = (f32[8,416,128]{2,1,0:T(8,128)}, f32[8,8,128]{2,1,0:T(8,128)S(1)}) custom-call(s32[3]{0:T(128)S(1)} %pad_add_fusion.refs_0_, f32[536,128]{1,0:T(8,128)S(1)} %get-tuple-element.23.refs_1_.refs_2_.refs_7_, f32[536,128]{1,0:T(8,128)S(1)} %collective-permute-done.refs_2_.refs_9_, f32[536,128]{1,0:T(8,128)S(1)} %collective-permute-done.1.refs_3_), custom_call_target="tpu_custom_call" | custom-call | flops 1980000000 | tf_op jit(solution)/shard_map/pallas_call | solution.py:526
  32.5 1.2 %collective-permute-done.4.refs_6_ = f32[8,24,128]{2,1,0:T(8,128)S(1)} collective-permute-done((f32[8,24,128]{2,1,0:T(8,128)S(1)}, f32[8,24,128]{2,1,0:T(8,128)S(1)}, u32[]{:S(2)}, u32[]{:S(2)}) %collective-permute-start.4) | collective-permute-done | bytes 98336 | tf_op jit(solution)/shard_map/ppermute | solution.py:607
  33.7 1.8 %shard_map.91 = f32[8,416,128]{2,1,0:T(8,128)} custom-call(s32[3]{0:T(128)S(1)} %pad_add_fusion.refs_0_, f32[8,416,128]{2,1,0:T(8,128)} %get-tuple-element.24.refs_1_, f32[8,8,128]{2,1,0:T(8,128)S(1)} %get-tuple-element.25.refs_2_, f32[536,128]{1,0:T(8,128)S(1)} %collective-permute-done.2.refs_3_, ...), custom_call_target="tpu_custom_call", output_to_operand_aliasing={{}: (1, {})} | custom-call | flops 1980000000 | tf_op jit(solution)/shard_map/pallas_call | solution.py:526
  35.5 3.9 %all-to-all-start = ((f32[8,416,128]{2,1,0:T(8,128)}), f32[8,416,128]{2,1,0:T(8,128)S(1)}, u32[]{:S(2)}, u32[]{:S(2)}) async-start(f32[8,416,128]{2,1,0:T(8,128)} %shard_map.91), calls=%async_computation | async-start | bytes 3407872 | tf_op jit(solution)/shard_map/all_to_all | solution.py:702
  39.4 0.5 shard_map.95
  39.9 0.0 copy-start.2
  39.9 3.1 %collective-permute-start.6 = (f32[128,512]{1,0:T(8,128)S(1)}, f32[128,512]{1,0:T(8,128)S(1)}, u32[]{:S(2)}, u32[]{:S(2)}) collective-permute-start(f32[128,512]{1,0:T(8,128)S(1)} %shard_map.95), channel_id=1, source_target_pairs={{0,6},{2,0},{4,2},{6,4},{1,7},{3,1},{5,3},{7,5},{8,14},{10,8},{12,... | collective-permute-start | bytes 786440 | tf_op jit(solution)/shard_map/ppermute | solution.py:607
  43.0 2.1 %shard_map.92 = (f32[128,512]{1,0:T(8,128)S(1)}, f32[128,512]{1,0:T(8,128)S(1)}, f32[128,512]{1,0:T(8,128)}) custom-call(f32[8,392,128]{2,1,0:T(8,128)S(1)} %all-to-all-done.1.refs_0_), custom_call_target="tpu_custom_call" | custom-call | flops 1540000000 | tf_op jit(solution)/shard_map/pallas_call | solution.py:526
  45.1 0.1 collective-permute-start.8
  45.2 1.8 %shard_map.93.refs_1_ = f32[4,256,128]{2,1,0:T(8,128)} custom-call(f32[4,256,128]{2,1,0:T(8,128)S(1)} %copy-done.2, f32[4,256,128]{2,1,0:T(8,128)S(1)} %copy-done.3, f32[4,256,256]{2,1,0:T(8,128)S(1)} %copy-done.5, f32[4,128,128]{2,1,0:T(8,128)S(1)} %copy-done.8, f32[128,512]{1,0:T(8,128)S(1)} %get-tuple-element.36.refs_4_.refs_5_), custom_call_target="tpu_custom_call" | custom-call | flops 1100000000 | tf_op jit(solution)/shard_map/pallas_call | solution.py:526
  47.0 2.7 %collective-permute-done.6 = f32[128,512]{1,0:T(8,128)S(1)} collective-permute-done((f32[128,512]{1,0:T(8,128)S(1)}, f32[128,512]{1,0:T(8,128)S(1)}, u32[]{:S(2)}, u32[]{:S(2)}) %collective-permute-start.6) | collective-permute-done | bytes 262176 | tf_op jit(solution)/shard_map/ppermute | solution.py:607
  49.7 0.7 %add.3 = f32[128,512]{1,0:T(8,128)} add(f32[128,512]{1,0:T(8,128)S(1)} %get-tuple-element.42, f32[128,512]{1,0:T(8,128)S(1)} %collective-permute-done.6) | non-fusion elementwise | flops 65536 | bytes 786432 | tf_op jit(solution)/shard_map/add | solution.py:670
  50.4 4.3 %collective-permute-start.7 = (f32[128,512]{1,0:T(8,128)}, f32[128,512]{1,0:T(8,128)S(1)}, u32[]{:S(2)}, u32[]{:S(2)}) collective-permute-start(f32[128,512]{1,0:T(8,128)} %add.3), channel_id=1, source_target_pairs={{0,6},{2,0},{4,2},{6,4},{1,7},{3,1},{5,3},{7,5},{8,14},{10,8},{12,... | collective-permute-start | bytes 786440 | tf_op jit(solution)/shard_map/ppermute | solution.py:607
  54.7 6.6 %all-to-all-done.refs_0_ = f32[8,416,128]{2,1,0:T(8,128)S(1)} async-done(((f32[8,416,128]{2,1,0:T(8,128)}), f32[8,416,128]{2,1,0:T(8,128)S(1)}, u32[]{:S(2)}, u32[]{:S(2)}) %all-to-all-start) | async-done | bytes 1703968 | tf_op jit(solution)/shard_map/all_to_all | solution.py:702
  61.4 2.5 %shard_map.94 = (f32[4,256,128]{2,1,0:T(8,128)}, f32[4,256,128]{2,1,0:T(8,128)}, f32[2,256,128]{2,1,0:T(8,128)S(1)}) custom-call(f32[8,416,128]{2,1,0:T(8,128)S(1)} %all-to-all-done.refs_0_, f32[4,256,128]{2,1,0:T(8,128)} %shard_map.93.refs_1_, f32[4,256,256]{2,1,0:T(8,128)S(1)} %copy-done.6, ...), custom_call_target="tpu_custom_call", output_to_operand_aliasing={{1}: (1, {})} | custom-call | flops 3849999872 | tf_op jit(solution)/shard_map/pallas_call | solution.py:526
  63.9 1.6 %shard_map.96 = (f32[4,256,128]{2,1,0:T(8,128)}, f32[4,256,128]{2,1,0:T(8,128)}) custom-call(f32[4,256,128]{2,1,0:T(8,128)} %get-tuple-element.39.refs_0_, f32[4,256,128]{2,1,0:T(8,128)} %get-tuple-element.40.refs_1_, f32[2,256,128]{2,1,0:T(8,128)S(1)} %get-tuple-element.41.refs_2_, ...), custom_call_target="tpu_custom_call", output_to_operand_aliasing={{0}: (0, {}), {1}: (1, {})} | custom-call | flops 1760000000 | tf_op jit(solution)/shard_map/pallas_call | solution.py:526
  (31 shorter events, 0.1 us)
Async XLA Ops:
  1.3 1.0 %copy-start = (f32[4,256,128]{2,1,0:T(8,128)S(1)}, f32[4,256,128]{2,1,0:T(8,128)}, u32[]{:S(2)}) copy-start(f32[4,256,128]{2,1,0:T(8,128)} %refs_0_.2) | copy-start | bytes 1572868
  3.1 13.3 %collective-permute-start = (f32[536,128]{1,0:T(8,128)S(1)}, f32[536,128]{1,0:T(8,128)S(1)}, u32[]{:S(2)}, u32[]{:S(2)}) collective-permute-start(f32[536,128]{1,0:T(8,128)S(1)} %get-tuple-element.23.refs_1_.refs_2_.refs_7_), channel_id=1, source_target_pairs={{0,2},{2,4},{4,6},{6,0},{1,3},{3,5},{5,7},{7,1},{8,10},{10,12},{12... | collective-permute-start | bytes 823304 | tf_op jit(solution)/shard_map/ppermute | solution.py:607
  6.2 23.7 %collective-permute-start.1 = (f32[536,128]{1,0:T(8,128)S(1)}, f32[536,128]{1,0:T(8,128)S(1)}, u32[]{:S(2)}, u32[]{:S(2)}) collective-permute-start(f32[536,128]{1,0:T(8,128)S(1)} %get-tuple-element.23.refs_1_.refs_2_.refs_7_), channel_id=1, source_target_pairs={{0,6},{2,0},{4,2},{6,4},{1,7},{3,1},{5,3},{7,5},{8,14},{10,8},{12,... | collective-permute-start | bytes 823304 | tf_op jit(solution)/shard_map/ppermute | solution.py:607
  10.6 3.9 %copy-start.12 = (f32[4]{0:T(128)S(1)}, f32[4]{0:T(128)}, u32[]{:S(2)}) copy-start(f32[4]{0:T(128)} %param.13) | copy-start | bytes 52
  10.6 25.0 %all-to-all-start.1 = ((f32[8,392,128]{2,1,0:T(8,128)}), f32[8,392,128]{2,1,0:T(8,128)S(1)}, u32[]{:S(2)}, u32[]{:S(2)}) async-start(f32[8,392,128]{2,1,0:T(8,128)} %shard_map.89.refs_10_), calls=%async_computation.1 | async-start | bytes 3211264 | tf_op jit(solution)/shard_map/all_to_all | solution.py:630
  14.5 1.9 %copy-start.1 = (f32[4,256,128]{2,1,0:T(8,128)S(1)}, f32[4,256,128]{2,1,0:T(8,128)}, u32[]{:S(2)}) copy-start(f32[4,256,128]{2,1,0:T(8,128)} %refs_0_.3) | copy-start | bytes 1572868
  15.7 0.7 %copy-start.7 = (f32[4,128,128]{2,1,0:T(8,128)}, f32[4,128,128]{2,1,0:T(8,128)S(1)}, u32[]{:S(2)}) copy-start(f32[4,128,128]{2,1,0:T(8,128)S(1)} %get-tuple-element.35.refs_3_.refs_4_) | copy-start | bytes 786436
  16.4 4.4 %copy-start.4 = (f32[4,256,256]{2,1,0:T(8,128)}, f32[4,256,256]{2,1,0:T(8,128)S(1)}, u32[]{:S(2)}) copy-start(f32[4,256,256]{2,1,0:T(8,128)S(1)} %get-tuple-element.29.refs_6_.refs_2_.refs_3_) | copy-start | bytes 3145732
  16.4 17.3 %collective-permute-start.2 = (f32[536,128]{1,0:T(8,128)S(1)}, f32[536,128]{1,0:T(8,128)S(1)}, u32[]{:S(2)}, u32[]{:S(2)}) collective-permute-start(f32[536,128]{1,0:T(8,128)S(1)} %collective-permute-done.refs_2_.refs_9_), channel_id=1, source_target_pairs={{0,2},{2,4},{4,6},{6,0},{1,3},{3,5},{5,7},{7,1},{8,10},{10,12},{12... | collective-permute-start | bytes 823304 | tf_op jit(solution)/shard_map/ppermute | solution.py:607
  20.8 11.6 %collective-permute-start.3 = (f32[8,24,128]{2,1,0:T(8,128)S(1)}, f32[8,24,128]{2,1,0:T(8,128)S(1)}, u32[]{:S(2)}, u32[]{:S(2)}) collective-permute-start(f32[8,24,128]{2,1,0:T(8,128)S(1)} %get-tuple-element.32), channel_id=1, source_target_pairs={{0,2},{2,4},{4,6},{6,0},{1,3},{3,5},{5,7},{7,1},{8,10},{10,12},{12... | collective-permute-start | bytes 294920 | tf_op jit(solution)/shard_map/ppermute | solution.py:607
  25.9 7.8 %collective-permute-start.4 = (f32[8,24,128]{2,1,0:T(8,128)S(1)}, f32[8,24,128]{2,1,0:T(8,128)S(1)}, u32[]{:S(2)}, u32[]{:S(2)}) collective-permute-start(f32[8,24,128]{2,1,0:T(8,128)S(1)} %get-tuple-element.33), channel_id=1, source_target_pairs={{0,4},{2,6},{4,0},{6,2},{1,5},{3,7},{5,1},{7,3},{8,12},{10,14},{12... | collective-permute-start | bytes 294920 | tf_op jit(solution)/shard_map/ppermute | solution.py:607
  27.1 6.6 %collective-permute-start.5 = (f32[8,24,128]{2,1,0:T(8,128)S(1)}, f32[8,24,128]{2,1,0:T(8,128)S(1)}, u32[]{:S(2)}, u32[]{:S(2)}) collective-permute-start(f32[8,24,128]{2,1,0:T(8,128)S(1)} %get-tuple-element.34), channel_id=1, source_target_pairs={{0,6},{2,0},{4,2},{6,4},{1,7},{3,1},{5,3},{7,5},{8,14},{10,8},{12,... | collective-permute-start | bytes 294920 | tf_op jit(solution)/shard_map/ppermute | solution.py:607
  35.5 25.8 %all-to-all-start = ((f32[8,416,128]{2,1,0:T(8,128)}), f32[8,416,128]{2,1,0:T(8,128)S(1)}, u32[]{:S(2)}, u32[]{:S(2)}) async-start(f32[8,416,128]{2,1,0:T(8,128)} %shard_map.91), calls=%async_computation | async-start | bytes 3407872 | tf_op jit(solution)/shard_map/all_to_all | solution.py:702
  39.9 5.3 %copy-start.2 = (f32[4,256,128]{2,1,0:T(8,128)S(1)}, f32[4,256,128]{2,1,0:T(8,128)}, u32[]{:S(2)}) copy-start(f32[4,256,128]{2,1,0:T(8,128)} %refs_0_.3) | copy-start | bytes 1572868
  39.9 5.3 %copy-start.3 = (f32[4,256,128]{2,1,0:T(8,128)S(1)}, f32[4,256,128]{2,1,0:T(8,128)}, u32[]{:S(2)}) copy-start(f32[4,256,128]{2,1,0:T(8,128)} %refs_1_.1) | copy-start | bytes 1572868
  39.9 5.3 %copy-start.5 = (f32[4,256,256]{2,1,0:T(8,128)S(1)}, f32[4,256,256]{2,1,0:T(8,128)}, u32[]{:S(2)}) copy-start(f32[4,256,256]{2,1,0:T(8,128)} %copy-done.4) | copy-start | bytes 3145732
  39.9 5.3 %copy-start.8 = (f32[4,128,128]{2,1,0:T(8,128)S(1)}, f32[4,128,128]{2,1,0:T(8,128)}, u32[]{:S(2)}) copy-start(f32[4,128,128]{2,1,0:T(8,128)} %copy-done.7) | copy-start | bytes 786436
  39.9 9.8 %collective-permute-start.6 = (f32[128,512]{1,0:T(8,128)S(1)}, f32[128,512]{1,0:T(8,128)S(1)}, u32[]{:S(2)}, u32[]{:S(2)}) collective-permute-start(f32[128,512]{1,0:T(8,128)S(1)} %shard_map.95), channel_id=1, source_target_pairs={{0,6},{2,0},{4,2},{6,4},{1,7},{3,1},{5,3},{7,5},{8,14},{10,8},{12,... | collective-permute-start | bytes 786440 | tf_op jit(solution)/shard_map/ppermute | solution.py:607
  45.1 1.9 %copy-start.10 = (f32[128,512]{1,0:T(8,128)}, f32[128,512]{1,0:T(8,128)S(1)}, u32[]{:S(2)}) copy-start(f32[128,512]{1,0:T(8,128)S(1)} %get-tuple-element.36.refs_4_.refs_5_) | copy-start | bytes 786436
  45.1 18.8 %collective-permute-start.8 = (f32[128,512]{1,0:T(8,128)}, f32[128,512]{1,0:T(8,128)S(1)}, u32[]{:S(2)}, u32[]{:S(2)}) collective-permute-start(f32[128,512]{1,0:T(8,128)} %get-tuple-element.43), channel_id=1, source_target_pairs={{0,2},{2,4},{4,6},{6,0},{1,3},{3,5},{5,7},{7,1},{8,10},{10,12},{12... | collective-permute-start | bytes 786440 | tf_op jit(solution)/shard_map/ppermute | solution.py:607
  45.2 16.2 %copy-start.6 = (f32[4,256,256]{2,1,0:T(8,128)S(1)}, f32[4,256,256]{2,1,0:T(8,128)}, u32[]{:S(2)}) copy-start(f32[4,256,256]{2,1,0:T(8,128)} %copy-done.4) | copy-start | bytes 3145732
  45.2 16.2 %copy-start.9 = (f32[4,128,128]{2,1,0:T(8,128)S(1)}, f32[4,128,128]{2,1,0:T(8,128)}, u32[]{:S(2)}) copy-start(f32[4,128,128]{2,1,0:T(8,128)} %copy-done.7) | copy-start | bytes 786436
  50.4 13.4 %collective-permute-start.7 = (f32[128,512]{1,0:T(8,128)}, f32[128,512]{1,0:T(8,128)S(1)}, u32[]{:S(2)}, u32[]{:S(2)}) collective-permute-start(f32[128,512]{1,0:T(8,128)} %add.3), channel_id=1, source_target_pairs={{0,6},{2,0},{4,2},{6,4},{1,7},{3,1},{5,3},{7,5},{8,14},{10,8},{12,... | collective-permute-start | bytes 786440 | tf_op jit(solution)/shard_map/ppermute | solution.py:607
  61.4 2.5 %copy-start.11 = (f32[128,512]{1,0:T(8,128)S(1)}, f32[128,512]{1,0:T(8,128)}, u32[]{:S(2)}) copy-start(f32[128,512]{1,0:T(8,128)} %copy-done.10) | copy-start | bytes 786436

commit v7 on v6

--- a/solution.py
+++ b/solution.py
@@ -135,15 +135,24 @@
     return jnp.concatenate(rows, axis=0)
 
 
-def turned_by(at, steps, size):
-    at = at + steps
-    return jnp.where(at >= size, at - size, at)
-
-
-def columns_wanted(shape, depth, inner, level, steps):
+def ring_order(depth):
+    return list(range(0, depth, 2)) + list(range(1, depth, 2))[::-1]
+
+
+def seat_of(level, depth):
+    return jnp.where(level % 2 == 0, level // 2, depth - (level + 1) // 2)
+
+
+def level_of(seat, steps, depth):
+    there = seat - steps
+    there = jnp.where(there < 0, there + depth, there)
+    return jnp.where(2 * there < depth, 2 * there, 2 * (depth - there) - 1)
+
+
+def columns_wanted(shape, depth, inner, seat, steps):
     row = lax.broadcasted_iota(jnp.int32, shape, 0)
     column, steps = (row // depth, row % depth) if steps is None else (row, steps)
-    level = turned_by(level, depth - steps, depth)
+    level = level_of(seat, steps, depth)
     return (column // inner * (depth * inner) + level * inner + column % inner).astype(F32)
 
 
@@ -163,7 +172,7 @@
     cells_x = (ring.shape[0] - 3 * SUB) // planes_a
     rest = tiled.shape[0] // cells_x
     names, tiles, shares = routing(ring, fanout)
-    wanted = columns_wanted((columns * depth, LANES), depth, inner, at[1], None)
+    wanted = columns_wanted((columns * depth, LANES), depth, inner, at[3], None)
     member, weight, label = route_rows(names, tiles, shares, wanted)
     rank = ranked(member)
     cells = tile_columns(tiled[...], rest, cells_x // TS)
@@ -201,8 +210,8 @@
     return [ring[first + k * SUB:first + k * SUB + fanout, :] for k in range(3)]
 
 
-def pack(capacity, columns, depth, inner, fanout, level, rings, picked, pack_out, boards, first, size):
-    wanted = columns_wanted((columns, LANES), depth, inner, level, 0)
+def pack(capacity, columns, depth, inner, fanout, seat, rings, picked, pack_out, boards, first, size):
+    wanted = columns_wanted((columns, LANES), depth, inner, seat, 0)
     for s, ring in enumerate(rings):
         half = ring.shape[0] - 3 * SUB
         member, weight, label = route_rows(*routing(ring, fanout), wanted)
@@ -235,7 +244,7 @@
     rings, (far, boards_out, picked, out, gone) = refs[:-5], refs[-5:]
     size = len(rings) * capacity
     boards = [jnp.zeros((SUB, LANES), F32) for _ in range(columns)]
-    boards = pack(capacity, columns, depth, inner, fanout, at[1], rings, picked, out, boards, 0, size)
+    boards = pack(capacity, columns, depth, inner, fanout, at[3], rings, picked, out, boards, 0, size)
     for j in range(columns):
         boards_out[j] = boards[j]
     send(
@@ -252,7 +261,7 @@
     del far_in
     boards = [boards_in[j] for j in range(columns)]
     boards = pack(
-        capacity, columns, depth, inner, fanout, at[1], [ring], picked, out, boards, total // capacity - 1, capacity
+        capacity, columns, depth, inner, fanout, at[3], [ring], picked, out, boards, total // capacity - 1, capacity
     )
     for j in range(columns):
         tail[j, :SUB, :] = boards[j]
@@ -432,7 +441,7 @@
                     rows[p, :, i * LANES:(i + 1) * LANES]
                 )
     for o, out in enumerate(outs):
-        out[...] = carries[turned_by(at[1], o, depth)]
+        out[...] = carries[lax.rem(at[1] + o, depth)]
 
 
 def masked(rows, planes, z):
@@ -595,16 +604,21 @@
     planes_a = planes // 2
     rest = planes - planes_a
     tile_cells = 2 * LANES
-    at = jnp.stack([lax.axis_index("gx"), lax.axis_index("z"), lax.axis_index("x")])
+    level = lax.axis_index("z")
+    at = jnp.stack([lax.axis_index("gx"), level, lax.axis_index("x"), seat_of(level, depth)])
     scalars, near = pl.BlockSpec(memory_space=pltpu.SMEM), pl.BlockSpec(memory_space=pltpu.VMEM)
     far = pl.BlockSpec(memory_space=pl.ANY)
 
     def array(*shape):
         return jax.ShapeDtypeStruct(shape, F32)
 
-    def turn(x, axis, steps):
-        size = lax.axis_size(axis)
-        return lax.ppermute(x, axis, [(i, (i + steps) % size) for i in range(size)])
+    seats = ring_order(depth)
+
+    def turn(x, steps):
+        return lax.ppermute(x, "z", [(seats[i], seats[(i + steps) % depth]) for i in range(depth)])
+
+    def step(x, steps):
+        return lax.ppermute(x, "z", [(i, (i + steps) % depth) for i in range(depth)])
 
     routes = jnp.stack([x.reshape(tile_count, fanout).T for x in (dest_device, dest_tile, mass_counts)])
     ring, tiled = call(
@@ -613,9 +627,9 @@
     )(source_mass, routes.astype(F32))
     rings = [ring] + [None] * (depth - 1)
     for s in range(1, depth // 2 + 1):
-        rings[s] = turn(rings[s - 1], "z", 1)
+        rings[s] = step(rings[s - 1], 1)
         if s < depth - s:
-            rings[depth - s] = turn(rings[(depth - s + 1) % depth], "z", -1)
+            rings[depth - s] = step(rings[(depth - s + 1) % depth], -1)
 
     packed_b = call(
         "start", functools.partial(start_kernel, capacity, columns, depth, inner, planes_a, fanout),
@@ -650,7 +664,7 @@
         [pltpu.VMEM((depth, columns, edge_rows, LANES), F32)],
         [rings[1], packed_b],
     )(at, logs, target_density, table, lines, coef, both_x, ring, tiled)
-    edges = [edges[0]] + [turn(edges[o], "z", o) for o in range(1, depth)]
+    edges = [edges[0]] + [step(edges[o], o) for o in range(1, depth)]
     sums = {}
     for groups in [[depth // 2], [r for r in range(depth) if r != depth // 2]]:
         parts = 2 * rest
@@ -667,12 +681,12 @@
         sums.update(zip(groups, some))
     moving = {r: sums[r] for r in range(depth)}
     for r in range(depth // 2, 0, -1):
-        moving[r - 1] = turn(moving[r], "z", -1) if r == 1 else moving[r - 1] + turn(moving[r], "z", -1)
+        moving[r - 1] = turn(moving[r], -1) if r == 1 else moving[r - 1] + turn(moving[r], -1)
     moving = [sums[0], moving[0]]
     if depth > 2:
         more = sums[depth // 2 + 1]
         for r in range(depth // 2 + 1, depth):
-            more = turn(more, "z", 1)
+            more = turn(more, 1)
             if r < depth - 1:
                 more = more + sums[r + 1]
         moving.append(more)

time: 65.8 us -> 65.8 us (level)
  starting transfers between devices: 29.5 us -> 26.9 us
  waiting for transfers between devices: 10.6 us -> 13.1 us
    ppermute x9, starting transfers between devices: 21.7 us -> 19.2 us  [the longest x6 14.3 us: step(): lax.ppermute(x, 'z', [(i, (i + steps) % depth) for i in range(depth)])]
    all_to_all x1, waiting for transfers between devices: 6.65 us -> 9.04 us  [per_device(): arrived_a = lax.all_to_all(packed_a, ('gx', 'x'), 0, 0, tiled=True)]
where the time goes in v7:
time: 65.8 us; the launch traced here: 65.4 us
  starting transfers between devices  26.9 us (41%)
  Pallas kernels  21.2 us (32%)
  waiting for transfers between devices  13.1 us (20%)
  local copies, waits for them, and re-layouts  1.8 us (3%)
  other arithmetic  1.54 us (2%)
  between operations  0.86 us (1%)
    pallas_call x11, Pallas kernels, run(): pl.pallas_call(kernel, out_shape=out_shape, in_specs=specs + [pl.BlockSpe...  21.2 us
    ppermute x6, starting transfers between devices, step(): lax.ppermute(x, 'z', [(i, (i + steps) % depth) for i in range(depth)])  14.3 us
    all_to_all x1, waiting for transfers between devices, per_device(): arrived_a = lax.all_to_all(packed_a, ('gx', 'x'), 0, 0, tiled=True)  9.04 us
    ppermute x3, starting transfers between devices, turn(): lax.ppermute(x, 'z', [(seats[i], seats[(i + steps) % depth]) for i in ran...  4.91 us
    all_to_all x1, starting transfers between devices, per_device(): arrived_b = lax.all_to_all(packed_b, ('gx', 'x'), 0, 0, tiled=True)  3.89 us
    all_to_all x1, starting transfers between devices, per_device(): arrived_a = lax.all_to_all(packed_a, ('gx', 'x'), 0, 0, tiled=True)  3.85 us
    ppermute x3, waiting for transfers between devices, turn(): lax.ppermute(x, 'z', [(seats[i], seats[(i + steps) % depth]) for i in ran...  2.85 us
    unnamed x26, local copies, waits for them, and re-layouts  1.8 us
  transfers between devices with their start and end apart: 11, of which 3 were waited for; matrix products, arithmetic and copies ran while one was open for 1% of the time, Pallas kernels for 29%

profile of v7, /device:TPU:0, one launch (start us, length us, event | category | flops | bytes accessed | tf_op | source)
XLA Modules:
  0.0 65.4 jit_solution(6531192456779334792)
XLA Ops:
  0.6 0.7 %add_convert_fusion.refs_1_ = f32[3,4,128]{2,1,0:T(4,128)S(1)} fusion(s32[1,4,128]{2,1,0:T(4,128)} %bitcast.19, s32[1,4,128]{2,1,0:T(4,128)} %bitcast.20, s32[1,4,128]{2,1,0:T(4,128)} %bitcast.21), kind=kLoop, calls=%fused_computation | loop fusion | flops 4608 | bytes 12288 | tf_op jit(solution)/shard_map/convert_element_type | solution.py:627
  1.4 1.0 %copy-done = f32[4,256,128]{2,1,0:T(8,128)S(1)} copy-done((f32[4,256,128]{2,1,0:T(8,128)S(1)}, f32[4,256,128]{2,1,0:T(8,128)}, u32[]{:S(2)}) %copy-start) | copy-done | bytes 524312
  2.4 0.8 %shard_map.86 = (f32[536,128]{1,0:T(8,128)S(1)}, f32[512,128]{1,0:T(8,128)S(1)}) custom-call(f32[4,256,128]{2,1,0:T(8,128)S(1)} %copy-done, f32[3,4,128]{2,1,0:T(4,128)S(1)} %add_convert_fusion.refs_1_), custom_call_target="tpu_custom_call" | custom-call | flops 880000000 | tf_op jit(solution)/shard_map/pallas_call | solution.py:535
  3.1 3.1 %collective-permute-start = (f32[536,128]{1,0:T(8,128)S(1)}, f32[536,128]{1,0:T(8,128)S(1)}, u32[]{:S(2)}, u32[]{:S(2)}) collective-permute-start(f32[536,128]{1,0:T(8,128)S(1)} %get-tuple-element.23.refs_1_.refs_2_.refs_7_), channel_id=1, source_target_pairs={{0,2},{2,4},{4,6},{6,0},{1,3},{3,5},{5,7},{7,1},{8,10},{10,12},{12... | collective-permute-start | bytes 823304 | tf_op jit(solution)/shard_map/ppermute | solution.py:621
  6.2 2.1 %collective-permute-start.1 = (f32[536,128]{1,0:T(8,128)S(1)}, f32[536,128]{1,0:T(8,128)S(1)}, u32[]{:S(2)}, u32[]{:S(2)}) collective-permute-start(f32[536,128]{1,0:T(8,128)S(1)} %get-tuple-element.23.refs_1_.refs_2_.refs_7_), channel_id=1, source_target_pairs={{0,6},{2,0},{4,2},{6,4},{1,7},{3,1},{5,3},{7,5},{8,14},{10,8},{12,... | collective-permute-start | bytes 823304 | tf_op jit(solution)/shard_map/ppermute | solution.py:621
  8.3 0.1 pad_add_fusion.refs_0_
  8.4 2.2 %shard_map.89.refs_10_ = f32[8,392,128]{2,1,0:T(8,128)} custom-call(s32[4]{0:T(128)S(1)} %pad_add_fusion.refs_0_, f32[536,128]{1,0:T(8,128)S(1)} %get-tuple-element.23.refs_1_.refs_2_.refs_7_, f32[512,128]{1,0:T(8,128)S(1)} %get-tuple-element.30.refs_2_.refs_8_), custom_call_target="tpu_custom_call" | custom-call | flops 2750000128 | tf_op jit(solution)/shard_map/pallas_call | solution.py:535
  10.6 3.9 %all-to-all-start.1 = ((f32[8,392,128]{2,1,0:T(8,128)}), f32[8,392,128]{2,1,0:T(8,128)S(1)}, u32[]{:S(2)}, u32[]{:S(2)}) async-start(f32[8,392,128]{2,1,0:T(8,128)} %shard_map.89.refs_10_), calls=%async_computation.1 | async-start | bytes 3211264 | tf_op jit(solution)/shard_map/all_to_all | solution.py:644
  14.5 1.2 %shard_map.88 = (f32[1024,256]{1,0:T(8,128)S(1)}, f32[4,8,256]{2,1,0:T(8,128)S(1)}, f32[7,8,128]{2,1,0:T(8,128)S(1)}, f32[8,256]{1,0:T(8,128)S(1)}, f32[8,128]{1...) custom-call(f32[4]{0:T(128)S(1)} %get-tuple-element.45.refs_0_, f32[4]{0:T(128)S(1)} %get-tuple-element.44.refs_1_, ...), custom_call_target="tpu_custom_call" | custom-call | flops 22000001024 | tf_op jit(solution)/shard_map/pallas_call | solution.py:535
  15.7 0.7 %copy-done.7 = f32[4,128,128]{2,1,0:T(8,128)} copy-done((f32[4,128,128]{2,1,0:T(8,128)}, f32[4,128,128]{2,1,0:T(8,128)S(1)}, u32[]{:S(2)}) %copy-start.7) | copy-done | bytes 262168
  16.4 4.4 %shard_map.90 = (f32[8,24,128]{2,1,0:T(8,128)S(1)}, f32[8,24,128]{2,1,0:T(8,128)S(1)}, f32[8,24,128]{2,1,0:T(8,128)S(1)}, f32[8,24,128]{2,1,0:T(8,128)S(1)}) custom-call(s32[4]{0:T(128)S(1)} %pad_add_fusion.refs_0_, f32[4]{0:T(128)S(1)} %get-tuple-element.44.refs_1_, f32[4,256,128]{2,1,0:T(8,128)S(1)} %copy-done.1, ...), custom_call_target="tpu_custom_call" | custom-call | flops 65999998976 | tf_op jit(solution)/shard_map/pallas_call | solution.py:535
  20.8 5.1 %collective-permute-start.3 = (f32[8,24,128]{2,1,0:T(8,128)S(1)}, f32[8,24,128]{2,1,0:T(8,128)S(1)}, u32[]{:S(2)}, u32[]{:S(2)}) collective-permute-start(f32[8,24,128]{2,1,0:T(8,128)S(1)} %get-tuple-element.32), channel_id=1, source_target_pairs={{0,2},{2,4},{4,6},{6,0},{1,3},{3,5},{5,7},{7,1},{8,10},{10,12},{12... | collective-permute-start | bytes 294920 | tf_op jit(solution)/shard_map/ppermute | solution.py:621
  25.9 1.2 %collective-permute-start.4 = (f32[8,24,128]{2,1,0:T(8,128)S(1)}, f32[8,24,128]{2,1,0:T(8,128)S(1)}, u32[]{:S(2)}, u32[]{:S(2)}) collective-permute-start(f32[8,24,128]{2,1,0:T(8,128)S(1)} %get-tuple-element.33), channel_id=1, source_target_pairs={{0,4},{2,6},{4,0},{6,2},{1,5},{3,7},{5,1},{7,3},{8,12},{10,14},{12... | collective-permute-start | bytes 294920 | tf_op jit(solution)/shard_map/ppermute | solution.py:621
  27.1 2.8 %collective-permute-start.5 = (f32[8,24,128]{2,1,0:T(8,128)S(1)}, f32[8,24,128]{2,1,0:T(8,128)S(1)}, u32[]{:S(2)}, u32[]{:S(2)}) collective-permute-start(f32[8,24,128]{2,1,0:T(8,128)S(1)} %get-tuple-element.34), channel_id=1, source_target_pairs={{0,6},{2,0},{4,2},{6,4},{1,7},{3,1},{5,3},{7,5},{8,14},{10,8},{12,... | collective-permute-start | bytes 294920 | tf_op jit(solution)/shard_map/ppermute | solution.py:621
  30.0 2.5 %shard_map.87 = (f32[8,416,128]{2,1,0:T(8,128)}, f32[8,8,128]{2,1,0:T(8,128)S(1)}) custom-call(s32[4]{0:T(128)S(1)} %pad_add_fusion.refs_0_, f32[536,128]{1,0:T(8,128)S(1)} %get-tuple-element.23.refs_1_.refs_2_.refs_7_, f32[536,128]{1,0:T(8,128)S(1)} %collective-permute-done.refs_2_.refs_9_, f32[536,128]{1,0:T(8,128)S(1)} %collective-permute-done.1.refs_3_), custom_call_target="tpu_custom_call" | custom-call | flops 1980000000 | tf_op jit(solution)/shard_map/pallas_call | solution.py:535
  32.5 1.2 %collective-permute-done.4.refs_6_ = f32[8,24,128]{2,1,0:T(8,128)S(1)} collective-permute-done((f32[8,24,128]{2,1,0:T(8,128)S(1)}, f32[8,24,128]{2,1,0:T(8,128)S(1)}, u32[]{:S(2)}, u32[]{:S(2)}) %collective-permute-start.4) | collective-permute-done | bytes 98336 | tf_op jit(solution)/shard_map/ppermute | solution.py:621
  33.7 1.9 %shard_map.91 = f32[8,416,128]{2,1,0:T(8,128)} custom-call(s32[4]{0:T(128)S(1)} %pad_add_fusion.refs_0_, f32[8,416,128]{2,1,0:T(8,128)} %get-tuple-element.24.refs_1_, f32[8,8,128]{2,1,0:T(8,128)S(1)} %get-tuple-element.25.refs_2_, f32[536,128]{1,0:T(8,128)S(1)} %collective-permute-done.2.refs_3_, ...), custom_call_target="tpu_custom_call", output_to_operand_aliasing={{}: (1, {})} | custom-call | flops 1980000000 | tf_op jit(solution)/shard_map/pallas_call | solution.py:535
  35.5 3.8 %all-to-all-start = ((f32[8,416,128]{2,1,0:T(8,128)}), f32[8,416,128]{2,1,0:T(8,128)S(1)}, u32[]{:S(2)}, u32[]{:S(2)}) async-start(f32[8,416,128]{2,1,0:T(8,128)} %shard_map.91), calls=%async_computation | async-start | bytes 3407872 | tf_op jit(solution)/shard_map/all_to_all | solution.py:716
  39.4 0.5 shard_map.95
  39.9 0.0 copy-start.3
  39.9 0.0 copy-start.8
  39.9 2.5 %collective-permute-start.6 = (f32[128,512]{1,0:T(8,128)S(1)}, f32[128,512]{1,0:T(8,128)S(1)}, u32[]{:S(2)}, u32[]{:S(2)}) collective-permute-start(f32[128,512]{1,0:T(8,128)S(1)} %shard_map.95), channel_id=1, source_target_pairs={{0,2},{4,0},{6,4},{2,6},{1,3},{5,1},{7,5},{3,7},{8,10},{12,8},{14,... | collective-permute-start | bytes 786440 | tf_op jit(solution)/shard_map/ppermute | solution.py:618
  42.5 2.1 %shard_map.92 = (f32[128,512]{1,0:T(8,128)S(1)}, f32[128,512]{1,0:T(8,128)S(1)}, f32[128,512]{1,0:T(8,128)}) custom-call(f32[8,392,128]{2,1,0:T(8,128)S(1)} %all-to-all-done.1.refs_0_), custom_call_target="tpu_custom_call" | custom-call | flops 1540000000 | tf_op jit(solution)/shard_map/pallas_call | solution.py:535
  44.5 0.5 collective-permute-start.8
  45.0 0.0 copy-start.9
  45.1 1.8 %shard_map.93.refs_1_ = f32[4,256,128]{2,1,0:T(8,128)} custom-call(f32[4,256,128]{2,1,0:T(8,128)S(1)} %copy-done.2, f32[4,256,128]{2,1,0:T(8,128)S(1)} %copy-done.3, f32[4,256,256]{2,1,0:T(8,128)S(1)} %copy-done.5, f32[4,128,128]{2,1,0:T(8,128)S(1)} %copy-done.8, f32[128,512]{1,0:T(8,128)S(1)} %get-tuple-element.36.refs_4_.refs_5_), custom_call_target="tpu_custom_call" | custom-call | flops 1100000000 | tf_op jit(solution)/shard_map/pallas_call | solution.py:535
  46.8 2.8 %collective-permute-done.6 = f32[128,512]{1,0:T(8,128)S(1)} collective-permute-done((f32[128,512]{1,0:T(8,128)S(1)}, f32[128,512]{1,0:T(8,128)S(1)}, u32[]{:S(2)}, u32[]{:S(2)}) %collective-permute-start.6) | collective-permute-done | bytes 262176 | tf_op jit(solution)/shard_map/ppermute | solution.py:618
  49.7 0.7 %add.14 = f32[128,512]{1,0:T(8,128)} add(f32[128,512]{1,0:T(8,128)S(1)} %get-tuple-element.42, f32[128,512]{1,0:T(8,128)S(1)} %collective-permute-done.6) | non-fusion elementwise | flops 65536 | bytes 786432 | tf_op jit(solution)/shard_map/add | solution.py:684
  50.4 1.9 %collective-permute-start.7 = (f32[128,512]{1,0:T(8,128)}, f32[128,512]{1,0:T(8,128)S(1)}, u32[]{:S(2)}, u32[]{:S(2)}) collective-permute-start(f32[128,512]{1,0:T(8,128)} %add.14), channel_id=1, source_target_pairs={{0,2},{4,0},{6,4},{2,6},{1,3},{5,1},{7,5},{3,7},{8,10},{12,8},{14,... | collective-permute-start | bytes 786440 | tf_op jit(solution)/shard_map/ppermute | solution.py:618
  52.3 9.0 %all-to-all-done.refs_0_ = f32[8,416,128]{2,1,0:T(8,128)S(1)} async-done(((f32[8,416,128]{2,1,0:T(8,128)}), f32[8,416,128]{2,1,0:T(8,128)S(1)}, u32[]{:S(2)}, u32[]{:S(2)}) %all-to-all-start) | async-done | bytes 1703968 | tf_op jit(solution)/shard_map/all_to_all | solution.py:716
  61.4 2.5 %shard_map.94 = (f32[4,256,128]{2,1,0:T(8,128)}, f32[4,256,128]{2,1,0:T(8,128)}, f32[2,256,128]{2,1,0:T(8,128)S(1)}) custom-call(f32[8,416,128]{2,1,0:T(8,128)S(1)} %all-to-all-done.refs_0_, f32[4,256,128]{2,1,0:T(8,128)} %shard_map.93.refs_1_, f32[4,256,256]{2,1,0:T(8,128)S(1)} %copy-done.6, ...), custom_call_target="tpu_custom_call", output_to_operand_aliasing={{1}: (1, {})} | custom-call | flops 3849999872 | tf_op jit(solution)/shard_map/pallas_call | solution.py:535
  63.9 1.6 %shard_map.96 = (f32[4,256,128]{2,1,0:T(8,128)}, f32[4,256,128]{2,1,0:T(8,128)}) custom-call(f32[4,256,128]{2,1,0:T(8,128)} %get-tuple-element.39.refs_0_, f32[4,256,128]{2,1,0:T(8,128)} %get-tuple-element.40.refs_1_, f32[2,256,128]{2,1,0:T(8,128)S(1)} %get-tuple-element.41.refs_2_, ...), custom_call_target="tpu_custom_call", output_to_operand_aliasing={{0}: (0, {}), {1}: (1, {})} | custom-call | flops 1760000000 | tf_op jit(solution)/shard_map/pallas_call | solution.py:535
  (31 shorter events, 0.1 us)
Async XLA Ops:
  1.3 1.0 %copy-start = (f32[4,256,128]{2,1,0:T(8,128)S(1)}, f32[4,256,128]{2,1,0:T(8,128)}, u32[]{:S(2)}) copy-start(f32[4,256,128]{2,1,0:T(8,128)} %refs_0_.2) | copy-start | bytes 1572868
  3.1 13.3 %collective-permute-start = (f32[536,128]{1,0:T(8,128)S(1)}, f32[536,128]{1,0:T(8,128)S(1)}, u32[]{:S(2)}, u32[]{:S(2)}) collective-permute-start(f32[536,128]{1,0:T(8,128)S(1)} %get-tuple-element.23.refs_1_.refs_2_.refs_7_), channel_id=1, source_target_pairs={{0,2},{2,4},{4,6},{6,0},{1,3},{3,5},{5,7},{7,1},{8,10},{10,12},{12... | collective-permute-start | bytes 823304 | tf_op jit(solution)/shard_map/ppermute | solution.py:621
  6.2 23.7 %collective-permute-start.1 = (f32[536,128]{1,0:T(8,128)S(1)}, f32[536,128]{1,0:T(8,128)S(1)}, u32[]{:S(2)}, u32[]{:S(2)}) collective-permute-start(f32[536,128]{1,0:T(8,128)S(1)} %get-tuple-element.23.refs_1_.refs_2_.refs_7_), channel_id=1, source_target_pairs={{0,6},{2,0},{4,2},{6,4},{1,7},{3,1},{5,3},{7,5},{8,14},{10,8},{12,... | collective-permute-start | bytes 823304 | tf_op jit(solution)/shard_map/ppermute | solution.py:621
  10.6 3.9 %copy-start.12 = (f32[4]{0:T(128)S(1)}, f32[4]{0:T(128)}, u32[]{:S(2)}) copy-start(f32[4]{0:T(128)} %param.13) | copy-start | bytes 52
  10.6 25.0 %all-to-all-start.1 = ((f32[8,392,128]{2,1,0:T(8,128)}), f32[8,392,128]{2,1,0:T(8,128)S(1)}, u32[]{:S(2)}, u32[]{:S(2)}) async-start(f32[8,392,128]{2,1,0:T(8,128)} %shard_map.89.refs_10_), calls=%async_computation.1 | async-start | bytes 3211264 | tf_op jit(solution)/shard_map/all_to_all | solution.py:644
  14.5 1.9 %copy-start.1 = (f32[4,256,128]{2,1,0:T(8,128)S(1)}, f32[4,256,128]{2,1,0:T(8,128)}, u32[]{:S(2)}) copy-start(f32[4,256,128]{2,1,0:T(8,128)} %refs_0_.3) | copy-start | bytes 1572868
  15.7 0.7 %copy-start.7 = (f32[4,128,128]{2,1,0:T(8,128)}, f32[4,128,128]{2,1,0:T(8,128)S(1)}, u32[]{:S(2)}) copy-start(f32[4,128,128]{2,1,0:T(8,128)S(1)} %get-tuple-element.35.refs_3_.refs_4_) | copy-start | bytes 786436
  16.4 4.4 %copy-start.4 = (f32[4,256,256]{2,1,0:T(8,128)}, f32[4,256,256]{2,1,0:T(8,128)S(1)}, u32[]{:S(2)}) copy-start(f32[4,256,256]{2,1,0:T(8,128)S(1)} %get-tuple-element.29.refs_6_.refs_2_.refs_3_) | copy-start | bytes 3145732
  16.4 17.3 %collective-permute-start.2 = (f32[536,128]{1,0:T(8,128)S(1)}, f32[536,128]{1,0:T(8,128)S(1)}, u32[]{:S(2)}, u32[]{:S(2)}) collective-permute-start(f32[536,128]{1,0:T(8,128)S(1)} %collective-permute-done.refs_2_.refs_9_), channel_id=1, source_target_pairs={{0,2},{2,4},{4,6},{6,0},{1,3},{3,5},{5,7},{7,1},{8,10},{10,12},{12... | collective-permute-start | bytes 823304 | tf_op jit(solution)/shard_map/ppermute | solution.py:621
  20.8 11.6 %collective-permute-start.3 = (f32[8,24,128]{2,1,0:T(8,128)S(1)}, f32[8,24,128]{2,1,0:T(8,128)S(1)}, u32[]{:S(2)}, u32[]{:S(2)}) collective-permute-start(f32[8,24,128]{2,1,0:T(8,128)S(1)} %get-tuple-element.32), channel_id=1, source_target_pairs={{0,2},{2,4},{4,6},{6,0},{1,3},{3,5},{5,7},{7,1},{8,10},{10,12},{12... | collective-permute-start | bytes 294920 | tf_op jit(solution)/shard_map/ppermute | solution.py:621
  25.9 7.8 %collective-permute-start.4 = (f32[8,24,128]{2,1,0:T(8,128)S(1)}, f32[8,24,128]{2,1,0:T(8,128)S(1)}, u32[]{:S(2)}, u32[]{:S(2)}) collective-permute-start(f32[8,24,128]{2,1,0:T(8,128)S(1)} %get-tuple-element.33), channel_id=1, source_target_pairs={{0,4},{2,6},{4,0},{6,2},{1,5},{3,7},{5,1},{7,3},{8,12},{10,14},{12... | collective-permute-start | bytes 294920 | tf_op jit(solution)/shard_map/ppermute | solution.py:621
  27.1 6.6 %collective-permute-start.5 = (f32[8,24,128]{2,1,0:T(8,128)S(1)}, f32[8,24,128]{2,1,0:T(8,128)S(1)}, u32[]{:S(2)}, u32[]{:S(2)}) collective-permute-start(f32[8,24,128]{2,1,0:T(8,128)S(1)} %get-tuple-element.34), channel_id=1, source_target_pairs={{0,6},{2,0},{4,2},{6,4},{1,7},{3,1},{5,3},{7,5},{8,14},{10,8},{12,... | collective-permute-start | bytes 294920 | tf_op jit(solution)/shard_map/ppermute | solution.py:621
  35.5 25.8 %all-to-all-start = ((f32[8,416,128]{2,1,0:T(8,128)}), f32[8,416,128]{2,1,0:T(8,128)S(1)}, u32[]{:S(2)}, u32[]{:S(2)}) async-start(f32[8,416,128]{2,1,0:T(8,128)} %shard_map.91), calls=%async_computation | async-start | bytes 3407872 | tf_op jit(solution)/shard_map/all_to_all | solution.py:716
  39.9 5.2 %copy-start.2 = (f32[4,256,128]{2,1,0:T(8,128)S(1)}, f32[4,256,128]{2,1,0:T(8,128)}, u32[]{:S(2)}) copy-start(f32[4,256,128]{2,1,0:T(8,128)} %refs_0_.3) | copy-start | bytes 1572868
  39.9 5.1 %copy-start.3 = (f32[4,256,128]{2,1,0:T(8,128)S(1)}, f32[4,256,128]{2,1,0:T(8,128)}, u32[]{:S(2)}) copy-start(f32[4,256,128]{2,1,0:T(8,128)} %refs_1_.1) | copy-start | bytes 1572868
  39.9 5.1 %copy-start.5 = (f32[4,256,256]{2,1,0:T(8,128)S(1)}, f32[4,256,256]{2,1,0:T(8,128)}, u32[]{:S(2)}) copy-start(f32[4,256,256]{2,1,0:T(8,128)} %copy-done.4) | copy-start | bytes 3145732
  39.9 5.1 %copy-start.8 = (f32[4,128,128]{2,1,0:T(8,128)S(1)}, f32[4,128,128]{2,1,0:T(8,128)}, u32[]{:S(2)}) copy-start(f32[4,128,128]{2,1,0:T(8,128)} %copy-done.7) | copy-start | bytes 786436
  39.9 9.8 %collective-permute-start.6 = (f32[128,512]{1,0:T(8,128)S(1)}, f32[128,512]{1,0:T(8,128)S(1)}, u32[]{:S(2)}, u32[]{:S(2)}) collective-permute-start(f32[128,512]{1,0:T(8,128)S(1)} %shard_map.95), channel_id=1, source_target_pairs={{0,2},{4,0},{6,4},{2,6},{1,3},{5,1},{7,5},{3,7},{8,10},{12,8},{14,... | collective-permute-start | bytes 786440 | tf_op jit(solution)/shard_map/ppermute | solution.py:618
  44.5 2.3 %copy-start.10 = (f32[128,512]{1,0:T(8,128)}, f32[128,512]{1,0:T(8,128)S(1)}, u32[]{:S(2)}) copy-start(f32[128,512]{1,0:T(8,128)S(1)} %get-tuple-element.36.refs_4_.refs_5_) | copy-start | bytes 786436
  44.5 19.3 %collective-permute-start.8 = (f32[128,512]{1,0:T(8,128)}, f32[128,512]{1,0:T(8,128)S(1)}, u32[]{:S(2)}, u32[]{:S(2)}) collective-permute-start(f32[128,512]{1,0:T(8,128)} %get-tuple-element.43), channel_id=1, source_target_pairs={{0,4},{4,6},{6,2},{2,0},{1,5},{5,7},{7,3},{3,1},{8,12},{12,14},{14... | collective-permute-start | bytes 786440 | tf_op jit(solution)/shard_map/ppermute | solution.py:618
  45.0 16.3 %copy-start.6 = (f32[4,256,256]{2,1,0:T(8,128)S(1)}, f32[4,256,256]{2,1,0:T(8,128)}, u32[]{:S(2)}) copy-start(f32[4,256,256]{2,1,0:T(8,128)} %copy-done.4) | copy-start | bytes 3145732
  45.0 16.3 %copy-start.9 = (f32[4,128,128]{2,1,0:T(8,128)S(1)}, f32[4,128,128]{2,1,0:T(8,128)}, u32[]{:S(2)}) copy-start(f32[4,128,128]{2,1,0:T(8,128)} %copy-done.7) | copy-start | bytes 786436
  50.4 13.4 %collective-permute-start.7 = (f32[128,512]{1,0:T(8,128)}, f32[128,512]{1,0:T(8,128)S(1)}, u32[]{:S(2)}, u32[]{:S(2)}) collective-permute-start(f32[128,512]{1,0:T(8,128)} %add.14), channel_id=1, source_target_pairs={{0,2},{4,0},{6,4},{2,6},{1,3},{5,1},{7,5},{3,7},{8,10},{12,8},{14,... | collective-permute-start | bytes 786440 | tf_op jit(solution)/shard_map/ppermute | solution.py:618
  61.4 2.5 %copy-start.11 = (f32[128,512]{1,0:T(8,128)S(1)}, f32[128,512]{1,0:T(8,128)}, u32[]{:S(2)}) copy-start(f32[128,512]{1,0:T(8,128)} %copy-done.10) | copy-start | bytes 786436
